TPU v7x, 256 devices: a whole 4x4x8 slice. The times are simulated.
256 devices in a mesh: gx: 16 (over y, x_lo, core), gy: 16 (over z, x_hi).
Axes of the slice: x: 4 (x_hi: 2, x_lo: 2; x = x_hi * 2 + x_lo), y: 4, z: 8, core: 2. Of those that a mesh axis runs over, the one named last changes fastest.
Arguments:
- start_state: float32 [2, 8, 2, 128, 2048], P(None, None, None, 'gx', 'gy'), may hold values from -6 to 6
- probe_state: float32 [2, 8, 2, 128, 2048], P(None, None, None, 'gx', 'gy'), may hold values from -6 to 6
- hop_offsets: int32 [10, 2, 128, 2048], P(None, None, 'gx', 'gy'), may hold values from 0 to 24, as said below
- hop_orbitals: int32 [10, 2, 128, 2048], P(None, None, 'gx', 'gy'), may hold values from 0 to 1, as said below
- hop_index: int32 [10, 2, 128, 2048], P(None, None, 'gx', 'gy'), may hold values from 0 to 63, as said below
- orbital_type: int32 [2, 128, 2048], P(None, 'gx', 'gy'), may hold values from 0 to 3
- hop_table: float32 [64], replicated, may hold values from -0.09 to -0.045
- onsite_table: float32 [4], replicated, may hold values from -0.1 to 0.1
Outputs:
- final_state: float32 [2, 8, 2, 128, 2048], P(None, None, None, 'gx', 'gy')
- intersections: float32 [4, 2, 8], replicated
Inputs may be any that keep to these rules, and one draw needn't show every extreme that they name: `hop_offsets`: a code o stands for the offset (o // 5 - 2, o % 5 - 2) in cells along x and y; hoppings come in mirrored pairs: if hopping k into orbital a of cell (x, y) comes from orbital b of the cell at offset (p, q), then hopping k into orbital b of that cell comes from orbital a of cell (x, y), with offset (-p, -q) and the same hop_index entry. `hop_orbitals`: the source orbital is the receiving orbital where the two components of the offset add up to an odd number, and the other orbital where they add up to an even number. `hop_index`: a hopping and its mirrored partner name the same entry.
All inputs are finite; a program needn't handle non-finite values.
Results may differ from a plain program's by a relative error of at most 0.0001.
Values sent between devices are 32-bit elements; how exact they have to be, the bound alone decides.
No kernel may reach another device: no remote copies, remote signals or barrier semaphores. Data moves between devices by JAX's collectives and lax.ppermute only.
A program may use at most 128 MiB of HBM per device.

v0:
```python
import math

import jax
import jax.numpy as jnp
from jax import lax
from jax.sharding import PartitionSpec as P

APPLY = 4
STEPS = 4


time_step = 2.6


def padded(cells, sides, width):
    for axis, dim in sides:
        count = lax.axis_size(axis)
        head = lax.slice_in_dim(cells, 0, width, axis=dim)
        tail = lax.slice_in_dim(cells, cells.shape[dim] - width, cells.shape[dim], axis=dim)
        cells = jnp.concatenate(
            [
                lax.ppermute(tail, axis, [(i, (i + 1) % count) for i in range(count)]),
                cells,
                lax.ppermute(head, axis, [((i + 1) % count, i) for i in range(count)]),
            ],
            axis=dim,
        )
    return cells


def bessel(order, arg):
    total = 0.0
    for term in range(40):
        total += (
            (-1.0) ** term
            * (arg / 2.0) ** (2 * term + order)
            / (math.factorial(term) * math.factorial(term + order))
        )
    return total


def weights(count):
    real_part = []
    imag_part = []
    phases = [(1.0, 0.0), (0.0, -1.0), (-1.0, 0.0), (0.0, 1.0)]
    for order in range(count + 1):
        scale = bessel(order, time_step) * (1.0 if order == 0 else 2.0)
        real_part.append(scale * phases[order % 4][0])
        imag_part.append(scale * phases[order % 4][1])
    return (real_part, imag_part)


def add_term(accum, term, order, real_part, imag_part):
    half = term.shape[0] // 2
    rotated = jnp.concatenate([-term[half:], term[:half]], axis=0)
    return accum + real_part[order] * term + imag_part[order] * rotated


def lookup(indices, table):
    entries = jnp.arange(table.shape[0], dtype=jnp.int32)
    return jnp.sum(jnp.where(indices[..., None] == entries, table, 0.0), axis=-1)


def apply_hops(field, coefficients):
    orbits = field.shape[1]
    out_x = field.shape[2] - 4
    out_y = field.shape[3] - 4
    window_coef = coefficients
    window_coef = window_coef.reshape(25, orbits, orbits, out_x, out_y)
    total = jnp.zeros((field.shape[0], orbits, out_x, out_y), jnp.float32)
    for group in range(5):
        windows = jnp.stack(
            [field[:, :, group : group + out_x, column : column + out_y] for column in range(5)]
        )
        group_coef = window_coef[5 * group : 5 * group + 5]
        total = total + jnp.sum(windows[:, :, :, None] * group_coef[:, None], axis=(0, 2))
    return total


def partial_intersection(probe, state):
    half = state.shape[0] // 2
    real_sum = jnp.sum(probe[:half] * state[:half] + probe[half:] * state[half:], axis=(1, 2, 3))
    imag_sum = jnp.sum(probe[:half] * state[half:] - probe[half:] * state[:half], axis=(1, 2, 3))
    return jnp.stack([real_sum, imag_sum])


def per_device(
    start_state,
    probe_state,
    hop_offsets,
    hop_orbitals,
    hop_index,
    orbital_type,
    hop_table,
    onsite_table,
):
    vectors = start_state.shape[1]
    orbits = start_state.shape[2]
    cells_x = start_state.shape[3]
    cells_y = start_state.shape[4]
    slots = hop_offsets.shape[0]
    offset_ids = jnp.arange(25, dtype=jnp.int32)[:, None, None, None]
    orbit_ids = jnp.arange(orbits, dtype=jnp.int32)[:, None, None, None]
    coefficients = jnp.zeros((25, orbits, orbits, cells_x, cells_y), jnp.float32)
    for slot in range(slots):
        amount = lookup(hop_index[slot], hop_table)
        pick_offset = (hop_offsets[slot][None] == offset_ids).astype(jnp.float32)
        pick_source = (hop_orbitals[slot][None] == orbit_ids).astype(jnp.float32)
        coefficients = coefficients + pick_offset[:, None] * pick_source[None] * amount[None, None]
    onsite = lookup(orbital_type, onsite_table)
    identity = (jnp.arange(orbits)[:, None] == jnp.arange(orbits)[None, :]).astype(jnp.float32)
    coefficients = coefficients.at[12].add(identity[:, :, None, None] * onsite[None])
    coefficients = coefficients.reshape(25 * orbits * orbits, cells_x, cells_y)
    real_part, imag_part = weights(APPLY)
    state = start_state.reshape(2 * vectors, orbits, cells_x, cells_y)
    probe = probe_state.reshape(2 * vectors, orbits, cells_x, cells_y)
    total_cells = cells_x * cells_y * lax.axis_size("gx") * lax.axis_size("gy")
    norm = 1.0 / math.sqrt(2.0 * orbits * total_cells)
    results = []
    for step in range(STEPS):
        accum = add_term(jnp.zeros_like(state), state, 0, real_part, imag_part)
        previous = state
        current = state
        for order in range(1, APPLY + 1):
            extended = padded(current, (("gx", 2), ("gy", 3)), 2)
            image = apply_hops(extended, coefficients)
            following = image if order == 1 else 2.0 * image - previous
            previous, current = (current, following)
            accum = add_term(accum, current, order, real_part, imag_part)
        state = accum
        local_terms = partial_intersection(probe, state)
        results.append(lax.psum(local_terms, ("gx", "gy")) * norm)
    intersections = jnp.stack(results)
    final_state = state.reshape(2, vectors, orbits, cells_x, cells_y)
    return (final_state, intersections)


def solution(mesh):
    return jax.shard_map(
        per_device,
        mesh=mesh,
        in_specs=(
            P(None, None, None, "gx", "gy"),
            P(None, None, None, "gx", "gy"),
            P(None, None, "gx", "gy"),
            P(None, None, "gx", "gy"),
            P(None, None, "gx", "gy"),
            P(None, "gx", "gy"),
            P(),
            P(),
        ),
        out_specs=(P(None, None, None, "gx", "gy"), P()),
        check_vma=False,
    )
```

profile of v0, /device:TPU:1, one launch (start us, length us, event | category | flops | bytes accessed | tf_op | source)
XLA Modules:
  0.0 453.8 jit_solution(12899724957612039956)
XLA Ops:
  10.8 7.4 %collective-permute-start.3 = (f32[16,2,12,2]{3,2,1,0:T(8,128)S(1)}, f32[16,2,12,2]{3,2,1,0:T(8,128)S(1)}, u32[]{:S(2)}, u32[]{:S(2)}) collective-permute-start(f32[16,2,12,2]{3,2,1,0:T(8,128)S(1)} %get-tuple-element.437), channel_id=1, source_target_pairs={{1,0},{2,1},{3,2},{4,3},{5,4},{6,5},{7,6},{8,7},{9,8},{10,9},{11,1... | collective-permute-start | bytes 9224 | tf_op jit(solution)/shard_map/ppermute | solution.py:24
  44.7 5.6 %collective-permute-done.6 = f32[16,2,12,2]{3,2,1,0:T(8,128)S(1)} collective-permute-done((f32[16,2,12,2]{3,2,1,0:T(8,128)S(1)}, f32[16,2,12,2]{3,2,1,0:T(8,128)S(1)}, u32[]{:S(2)}, u32[]{:S(2)}) %collective-permute-start.6) | collective-permute-done | bytes 3104 | tf_op jit(solution)/shard_map/ppermute | solution.py:22
  52.1 6.5 %collective-permute-start.9 = (f32[16,2,2,128]{3,2,1,0:T(2,128)S(1)}, f32[16,2,2,128]{3,2,1,0:T(2,128)S(1)}, u32[]{:S(2)}, u32[]{:S(2)}) collective-permute-start(f32[16,2,2,128]{3,2,1,0:T(2,128)S(1)} %get-tuple-element.675), channel_id=1, source_target_pairs={{16,0},{32,16},{48,32},{64,48},{80,64},{96,80},{112,96},{128,112},... | collective-permute-start | bytes 98312 | tf_op jit(solution)/shard_map/ppermute | solution.py:24
  67.4 5.6 %collective-permute-done.10 = f32[16,2,12,2]{3,2,1,0:T(8,128)S(1)} collective-permute-done((f32[16,2,12,2]{3,2,1,0:T(8,128)S(1)}, f32[16,2,12,2]{3,2,1,0:T(8,128)S(1)}, u32[]{:S(2)}, u32[]{:S(2)}) %collective-permute-start.10) | collective-permute-done | bytes 3104 | tf_op jit(solution)/shard_map/ppermute | solution.py:22
  74.8 6.2 %collective-permute-start.13 = (f32[16,2,2,128]{3,2,1,0:T(2,128)S(1)}, f32[16,2,2,128]{3,2,1,0:T(2,128)S(1)}, u32[]{:S(2)}, u32[]{:S(2)}) collective-permute-start(f32[16,2,2,128]{3,2,1,0:T(2,128)S(1)} %get-tuple-element.671), channel_id=1, source_target_pairs={{16,0},{32,16},{48,32},{64,48},{80,64},{96,80},{112,96},{128,112},... | collective-permute-start | bytes 98312 | tf_op jit(solution)/shard_map/ppermute | solution.py:24
  89.6 5.6 %collective-permute-done.14 = f32[16,2,12,2]{3,2,1,0:T(8,128)S(1)} collective-permute-done((f32[16,2,12,2]{3,2,1,0:T(8,128)S(1)}, f32[16,2,12,2]{3,2,1,0:T(8,128)S(1)}, u32[]{:S(2)}, u32[]{:S(2)}) %collective-permute-start.14) | collective-permute-done | bytes 3104 | tf_op jit(solution)/shard_map/ppermute | solution.py:22
  97.8 6.5 %collective-permute-start.17 = (f32[16,2,2,128]{3,2,1,0:T(2,128)S(1)}, f32[16,2,2,128]{3,2,1,0:T(2,128)S(1)}, u32[]{:S(2)}, u32[]{:S(2)}) collective-permute-start(f32[16,2,2,128]{3,2,1,0:T(2,128)S(1)} %get-tuple-element.667), channel_id=1, source_target_pairs={{16,0},{32,16},{48,32},{64,48},{80,64},{96,80},{112,96},{128,112},... | collective-permute-start | bytes 98312 | tf_op jit(solution)/shard_map/ppermute | solution.py:24
  112.6 5.4 %collective-permute-done.18 = f32[16,2,12,2]{3,2,1,0:T(8,128)S(1)} collective-permute-done((f32[16,2,12,2]{3,2,1,0:T(8,128)S(1)}, f32[16,2,12,2]{3,2,1,0:T(8,128)S(1)}, u32[]{:S(2)}, u32[]{:S(2)}) %collective-permute-start.18) | collective-permute-done | bytes 3104 | tf_op jit(solution)/shard_map/ppermute | solution.py:22
  119.9 6.5 %collective-permute-start.21 = (f32[16,2,2,128]{3,2,1,0:T(2,128)S(1)}, f32[16,2,2,128]{3,2,1,0:T(2,128)S(1)}, u32[]{:S(2)}, u32[]{:S(2)}) collective-permute-start(f32[16,2,2,128]{3,2,1,0:T(2,128)S(1)} %get-tuple-element.643), channel_id=1, source_target_pairs={{16,0},{32,16},{48,32},{64,48},{80,64},{96,80},{112,96},{128,112},... | collective-permute-start | bytes 98312 | tf_op jit(solution)/shard_map/ppermute | solution.py:24
  134.6 5.5 %collective-permute-done.22 = f32[16,2,12,2]{3,2,1,0:T(8,128)S(1)} collective-permute-done((f32[16,2,12,2]{3,2,1,0:T(8,128)S(1)}, f32[16,2,12,2]{3,2,1,0:T(8,128)S(1)}, u32[]{:S(2)}, u32[]{:S(2)}) %collective-permute-start.22) | collective-permute-done | bytes 3104 | tf_op jit(solution)/shard_map/ppermute | solution.py:22
  141.9 6.4 %collective-permute-start.25 = (f32[16,2,2,128]{3,2,1,0:T(2,128)S(1)}, f32[16,2,2,128]{3,2,1,0:T(2,128)S(1)}, u32[]{:S(2)}, u32[]{:S(2)}) collective-permute-start(f32[16,2,2,128]{3,2,1,0:T(2,128)S(1)} %get-tuple-element.638), channel_id=1, source_target_pairs={{16,0},{32,16},{48,32},{64,48},{80,64},{96,80},{112,96},{128,112},... | collective-permute-start | bytes 98312 | tf_op jit(solution)/shard_map/ppermute | solution.py:24
  163.8 6.3 %collective-permute-start.29 = (f32[16,2,2,128]{3,2,1,0:T(2,128)S(1)}, f32[16,2,2,128]{3,2,1,0:T(2,128)S(1)}, u32[]{:S(2)}, u32[]{:S(2)}) collective-permute-start(f32[16,2,2,128]{3,2,1,0:T(2,128)S(1)} %get-tuple-element.634), channel_id=1, source_target_pairs={{16,0},{32,16},{48,32},{64,48},{80,64},{96,80},{112,96},{128,112},... | collective-permute-start | bytes 98312 | tf_op jit(solution)/shard_map/ppermute | solution.py:24
  185.3 6.3 %collective-permute-start.33 = (f32[16,2,2,128]{3,2,1,0:T(2,128)S(1)}, f32[16,2,2,128]{3,2,1,0:T(2,128)S(1)}, u32[]{:S(2)}, u32[]{:S(2)}) collective-permute-start(f32[16,2,2,128]{3,2,1,0:T(2,128)S(1)} %get-tuple-element.630), channel_id=1, source_target_pairs={{16,0},{32,16},{48,32},{64,48},{80,64},{96,80},{112,96},{128,112},... | collective-permute-start | bytes 98312 | tf_op jit(solution)/shard_map/ppermute | solution.py:24
  207.4 6.2 %collective-permute-start.37 = (f32[16,2,2,128]{3,2,1,0:T(2,128)S(1)}, f32[16,2,2,128]{3,2,1,0:T(2,128)S(1)}, u32[]{:S(2)}, u32[]{:S(2)}) collective-permute-start(f32[16,2,2,128]{3,2,1,0:T(2,128)S(1)} %get-tuple-element.606), channel_id=1, source_target_pairs={{16,0},{32,16},{48,32},{64,48},{80,64},{96,80},{112,96},{128,112},... | collective-permute-start | bytes 98312 | tf_op jit(solution)/shard_map/ppermute | solution.py:24
  229.3 6.2 %collective-permute-start.41 = (f32[16,2,2,128]{3,2,1,0:T(2,128)S(1)}, f32[16,2,2,128]{3,2,1,0:T(2,128)S(1)}, u32[]{:S(2)}, u32[]{:S(2)}) collective-permute-start(f32[16,2,2,128]{3,2,1,0:T(2,128)S(1)} %get-tuple-element.601), channel_id=1, source_target_pairs={{16,0},{32,16},{48,32},{64,48},{80,64},{96,80},{112,96},{128,112},... | collective-permute-start | bytes 98312 | tf_op jit(solution)/shard_map/ppermute | solution.py:24
  251.1 6.2 %collective-permute-start.45 = (f32[16,2,2,128]{3,2,1,0:T(2,128)S(1)}, f32[16,2,2,128]{3,2,1,0:T(2,128)S(1)}, u32[]{:S(2)}, u32[]{:S(2)}) collective-permute-start(f32[16,2,2,128]{3,2,1,0:T(2,128)S(1)} %get-tuple-element.597), channel_id=1, source_target_pairs={{16,0},{32,16},{48,32},{64,48},{80,64},{96,80},{112,96},{128,112},... | collective-permute-start | bytes 98312 | tf_op jit(solution)/shard_map/ppermute | solution.py:24
  273.6 6.5 %collective-permute-start.49 = (f32[16,2,2,128]{3,2,1,0:T(2,128)S(1)}, f32[16,2,2,128]{3,2,1,0:T(2,128)S(1)}, u32[]{:S(2)}, u32[]{:S(2)}) collective-permute-start(f32[16,2,2,128]{3,2,1,0:T(2,128)S(1)} %get-tuple-element.591), channel_id=1, source_target_pairs={{16,0},{32,16},{48,32},{64,48},{80,64},{96,80},{112,96},{128,112},... | collective-permute-start | bytes 98312 | tf_op jit(solution)/shard_map/ppermute | solution.py:24
  289.1 5.8 %collective-permute-done.50 = f32[16,2,12,2]{3,2,1,0:T(8,128)S(1)} collective-permute-done((f32[16,2,12,2]{3,2,1,0:T(8,128)S(1)}, f32[16,2,12,2]{3,2,1,0:T(8,128)S(1)}, u32[]{:S(2)}, u32[]{:S(2)}) %collective-permute-start.50) | collective-permute-done | bytes 3104 | tf_op jit(solution)/shard_map/ppermute | solution.py:22
  296.8 6.0 %collective-permute-start.53 = (f32[16,2,2,128]{3,2,1,0:T(2,128)S(1)}, f32[16,2,2,128]{3,2,1,0:T(2,128)S(1)}, u32[]{:S(2)}, u32[]{:S(2)}) collective-permute-start(f32[16,2,2,128]{3,2,1,0:T(2,128)S(1)} %get-tuple-element.571), channel_id=1, source_target_pairs={{16,0},{32,16},{48,32},{64,48},{80,64},{96,80},{112,96},{128,112},... | collective-permute-start | bytes 98312 | tf_op jit(solution)/shard_map/ppermute | solution.py:24
  312.0 5.6 %collective-permute-done.54 = f32[16,2,12,2]{3,2,1,0:T(8,128)S(1)} collective-permute-done((f32[16,2,12,2]{3,2,1,0:T(8,128)S(1)}, f32[16,2,12,2]{3,2,1,0:T(8,128)S(1)}, u32[]{:S(2)}, u32[]{:S(2)}) %collective-permute-start.54) | collective-permute-done | bytes 3104 | tf_op jit(solution)/shard_map/ppermute | solution.py:22
  319.4 6.2 %collective-permute-start.57 = (f32[16,2,2,128]{3,2,1,0:T(2,128)S(1)}, f32[16,2,2,128]{3,2,1,0:T(2,128)S(1)}, u32[]{:S(2)}, u32[]{:S(2)}) collective-permute-start(f32[16,2,2,128]{3,2,1,0:T(2,128)S(1)} %get-tuple-element.566), channel_id=1, source_target_pairs={{16,0},{32,16},{48,32},{64,48},{80,64},{96,80},{112,96},{128,112},... | collective-permute-start | bytes 98312 | tf_op jit(solution)/shard_map/ppermute | solution.py:24
  334.0 6.5 %collective-permute-done.58 = f32[16,2,12,2]{3,2,1,0:T(8,128)S(1)} collective-permute-done((f32[16,2,12,2]{3,2,1,0:T(8,128)S(1)}, f32[16,2,12,2]{3,2,1,0:T(8,128)S(1)}, u32[]{:S(2)}, u32[]{:S(2)}) %collective-permute-start.58) | collective-permute-done | bytes 3104 | tf_op jit(solution)/shard_map/ppermute | solution.py:22
  357.1 6.3 %collective-permute-done.62 = f32[16,2,12,2]{3,2,1,0:T(8,128)S(1)} collective-permute-done((f32[16,2,12,2]{3,2,1,0:T(8,128)S(1)}, f32[16,2,12,2]{3,2,1,0:T(8,128)S(1)}, u32[]{:S(2)}, u32[]{:S(2)}) %collective-permute-start.62) | collective-permute-done | bytes 3104 | tf_op jit(solution)/shard_map/ppermute | solution.py:22
  367.5 80.3 %all-reduce = (f32[2,8]{1,0:T(2,128)}, f32[2,8]{1,0:T(2,128)}, f32[2,8]{1,0:T(2,128)}, f32[2,8]{1,0:T(2,128)}) all-reduce(f32[2,8]{1,0:T(2,128)S(1)} %pad_maximum_fusion.68, f32[2,8]{1,0:T(2,128)S(1)} %pad_maximum_fusion.67, f32[2,8]{1,0:T(2,128)S(1)} %pad_maximum_fusion.66, ...), channel_id=1, replica_groups=mesh['gx'=16,'gy'=16] {'gx','gy'}, use_global_device_ids=true, to_apply=%region_102.103 | all-reduce | flops 64 | bytes 512 | tf_op jit(solution)/shard_map/psum | solution.py:132
  (432 shorter events, 229.6 us)
Async XLA Ops:
  1.6 8.7 %collective-permute-start.1 = (f32[16,2,2,128]{3,2,1,0:T(2,128)S(1)}, f32[16,2,2,128]{3,2,1,0:T(2,128)S(1)}, u32[]{:S(2)}, u32[]{:S(2)}) collective-permute-start(f32[16,2,2,128]{3,2,1,0:T(2,128)S(1)} %get-tuple-element.684), channel_id=1, source_target_pairs={{16,0},{32,16},{48,32},{64,48},{80,64},{96,80},{112,96},{128,112},... | collective-permute-start | bytes 98312 | tf_op jit(solution)/shard_map/ppermute | solution.py:24
  10.8 11.1 %collective-permute-start.3 = (f32[16,2,12,2]{3,2,1,0:T(8,128)S(1)}, f32[16,2,12,2]{3,2,1,0:T(8,128)S(1)}, u32[]{:S(2)}, u32[]{:S(2)}) collective-permute-start(f32[16,2,12,2]{3,2,1,0:T(8,128)S(1)} %get-tuple-element.437), channel_id=1, source_target_pairs={{1,0},{2,1},{3,2},{4,3},{5,4},{6,5},{7,6},{8,7},{9,8},{10,9},{11,1... | collective-permute-start | bytes 9224 | tf_op jit(solution)/shard_map/ppermute | solution.py:24
  18.3 8.8 %collective-permute-start.2 = (f32[16,2,12,2]{3,2,1,0:T(8,128)S(1)}, f32[16,2,12,2]{3,2,1,0:T(8,128)S(1)}, u32[]{:S(2)}, u32[]{:S(2)}) collective-permute-start(f32[16,2,12,2]{3,2,1,0:T(8,128)S(1)} %get-tuple-element.438), channel_id=1, source_target_pairs={{0,1},{1,2},{2,3},{3,4},{4,5},{5,6},{6,7},{7,8},{8,9},{9,10},{10,1... | collective-permute-start | bytes 9224 | tf_op jit(solution)/shard_map/ppermute | solution.py:22
  36.0 8.7 %collective-permute-start.7 = (f32[16,2,12,2]{3,2,1,0:T(8,128)S(1)}, f32[16,2,12,2]{3,2,1,0:T(8,128)S(1)}, u32[]{:S(2)}, u32[]{:S(2)}) collective-permute-start(f32[16,2,12,2]{3,2,1,0:T(8,128)S(1)} %get-tuple-element.435), channel_id=1, source_target_pairs={{1,0},{2,1},{3,2},{4,3},{5,4},{6,5},{7,6},{8,7},{9,8},{10,9},{11,1... | collective-permute-start | bytes 9224 | tf_op jit(solution)/shard_map/ppermute | solution.py:24
  41.4 8.9 %collective-permute-start.6 = (f32[16,2,12,2]{3,2,1,0:T(8,128)S(1)}, f32[16,2,12,2]{3,2,1,0:T(8,128)S(1)}, u32[]{:S(2)}, u32[]{:S(2)}) collective-permute-start(f32[16,2,12,2]{3,2,1,0:T(8,128)S(1)} %get-tuple-element.436), channel_id=1, source_target_pairs={{0,1},{1,2},{2,3},{3,4},{4,5},{5,6},{6,7},{7,8},{8,9},{9,10},{10,1... | collective-permute-start | bytes 9224 | tf_op jit(solution)/shard_map/ppermute | solution.py:22
  60.0 7.4 %collective-permute-start.11 = (f32[16,2,12,2]{3,2,1,0:T(8,128)S(1)}, f32[16,2,12,2]{3,2,1,0:T(8,128)S(1)}, u32[]{:S(2)}, u32[]{:S(2)}) collective-permute-start(f32[16,2,12,2]{3,2,1,0:T(8,128)S(1)} %get-tuple-element.433), channel_id=1, source_target_pairs={{1,0},{2,1},{3,2},{4,3},{5,4},{6,5},{7,6},{8,7},{9,8},{10,9},{11,1... | collective-permute-start | bytes 9224 | tf_op jit(solution)/shard_map/ppermute | solution.py:24
  64.0 8.9 %collective-permute-start.10 = (f32[16,2,12,2]{3,2,1,0:T(8,128)S(1)}, f32[16,2,12,2]{3,2,1,0:T(8,128)S(1)}, u32[]{:S(2)}, u32[]{:S(2)}) collective-permute-start(f32[16,2,12,2]{3,2,1,0:T(8,128)S(1)} %get-tuple-element.434), channel_id=1, source_target_pairs={{0,1},{1,2},{2,3},{3,4},{4,5},{5,6},{6,7},{7,8},{8,9},{9,10},{10,1... | collective-permute-start | bytes 9224 | tf_op jit(solution)/shard_map/ppermute | solution.py:22
  86.3 8.9 %collective-permute-start.14 = (f32[16,2,12,2]{3,2,1,0:T(8,128)S(1)}, f32[16,2,12,2]{3,2,1,0:T(8,128)S(1)}, u32[]{:S(2)}, u32[]{:S(2)}) collective-permute-start(f32[16,2,12,2]{3,2,1,0:T(8,128)S(1)} %get-tuple-element.432), channel_id=1, source_target_pairs={{0,1},{1,2},{2,3},{3,4},{4,5},{5,6},{6,7},{7,8},{8,9},{9,10},{10,1... | collective-permute-start | bytes 9224 | tf_op jit(solution)/shard_map/ppermute | solution.py:22
  97.8 7.4 %collective-permute-start.17 = (f32[16,2,2,128]{3,2,1,0:T(2,128)S(1)}, f32[16,2,2,128]{3,2,1,0:T(2,128)S(1)}, u32[]{:S(2)}, u32[]{:S(2)}) collective-permute-start(f32[16,2,2,128]{3,2,1,0:T(2,128)S(1)} %get-tuple-element.667), channel_id=1, source_target_pairs={{16,0},{32,16},{48,32},{64,48},{80,64},{96,80},{112,96},{128,112},... | collective-permute-start | bytes 98312 | tf_op jit(solution)/shard_map/ppermute | solution.py:24
  108.9 9.1 %collective-permute-start.18 = (f32[16,2,12,2]{3,2,1,0:T(8,128)S(1)}, f32[16,2,12,2]{3,2,1,0:T(8,128)S(1)}, u32[]{:S(2)}, u32[]{:S(2)}) collective-permute-start(f32[16,2,12,2]{3,2,1,0:T(8,128)S(1)} %get-tuple-element.430), channel_id=1, source_target_pairs={{0,1},{1,2},{2,3},{3,4},{4,5},{5,6},{6,7},{7,8},{8,9},{9,10},{10,1... | collective-permute-start | bytes 9224 | tf_op jit(solution)/shard_map/ppermute | solution.py:22
  131.1 8.9 %collective-permute-start.22 = (f32[16,2,12,2]{3,2,1,0:T(8,128)S(1)}, f32[16,2,12,2]{3,2,1,0:T(8,128)S(1)}, u32[]{:S(2)}, u32[]{:S(2)}) collective-permute-start(f32[16,2,12,2]{3,2,1,0:T(8,128)S(1)} %get-tuple-element.428), channel_id=1, source_target_pairs={{0,1},{1,2},{2,3},{3,4},{4,5},{5,6},{6,7},{7,8},{8,9},{9,10},{10,1... | collective-permute-start | bytes 9224 | tf_op jit(solution)/shard_map/ppermute | solution.py:22
  152.4 9.5 %collective-permute-start.26 = (f32[16,2,12,2]{3,2,1,0:T(8,128)S(1)}, f32[16,2,12,2]{3,2,1,0:T(8,128)S(1)}, u32[]{:S(2)}, u32[]{:S(2)}) collective-permute-start(f32[16,2,12,2]{3,2,1,0:T(8,128)S(1)} %get-tuple-element.426), channel_id=1, source_target_pairs={{0,1},{1,2},{2,3},{3,4},{4,5},{5,6},{6,7},{7,8},{8,9},{9,10},{10,1... | collective-permute-start | bytes 9224 | tf_op jit(solution)/shard_map/ppermute | solution.py:22
  173.7 8.9 %collective-permute-start.30 = (f32[16,2,12,2]{3,2,1,0:T(8,128)S(1)}, f32[16,2,12,2]{3,2,1,0:T(8,128)S(1)}, u32[]{:S(2)}, u32[]{:S(2)}) collective-permute-start(f32[16,2,12,2]{3,2,1,0:T(8,128)S(1)} %get-tuple-element.424), channel_id=1, source_target_pairs={{0,1},{1,2},{2,3},{3,4},{4,5},{5,6},{6,7},{7,8},{8,9},{9,10},{10,1... | collective-permute-start | bytes 9224 | tf_op jit(solution)/shard_map/ppermute | solution.py:22
  196.5 8.9 %collective-permute-start.34 = (f32[16,2,12,2]{3,2,1,0:T(8,128)S(1)}, f32[16,2,12,2]{3,2,1,0:T(8,128)S(1)}, u32[]{:S(2)}, u32[]{:S(2)}) collective-permute-start(f32[16,2,12,2]{3,2,1,0:T(8,128)S(1)} %get-tuple-element.422), channel_id=1, source_target_pairs={{0,1},{1,2},{2,3},{3,4},{4,5},{5,6},{6,7},{7,8},{8,9},{9,10},{10,1... | collective-permute-start | bytes 9224 | tf_op jit(solution)/shard_map/ppermute | solution.py:22
  218.4 9.1 %collective-permute-start.38 = (f32[16,2,12,2]{3,2,1,0:T(8,128)S(1)}, f32[16,2,12,2]{3,2,1,0:T(8,128)S(1)}, u32[]{:S(2)}, u32[]{:S(2)}) collective-permute-start(f32[16,2,12,2]{3,2,1,0:T(8,128)S(1)} %get-tuple-element.420), channel_id=1, source_target_pairs={{0,1},{1,2},{2,3},{3,4},{4,5},{5,6},{6,7},{7,8},{8,9},{9,10},{10,1... | collective-permute-start | bytes 9224 | tf_op jit(solution)/shard_map/ppermute | solution.py:22
  240.3 8.9 %collective-permute-start.42 = (f32[16,2,12,2]{3,2,1,0:T(8,128)S(1)}, f32[16,2,12,2]{3,2,1,0:T(8,128)S(1)}, u32[]{:S(2)}, u32[]{:S(2)}) collective-permute-start(f32[16,2,12,2]{3,2,1,0:T(8,128)S(1)} %get-tuple-element.418), channel_id=1, source_target_pairs={{0,1},{1,2},{2,3},{3,4},{4,5},{5,6},{6,7},{7,8},{8,9},{9,10},{10,1... | collective-permute-start | bytes 9224 | tf_op jit(solution)/shard_map/ppermute | solution.py:22
  262.0 8.9 %collective-permute-start.46 = (f32[16,2,12,2]{3,2,1,0:T(8,128)S(1)}, f32[16,2,12,2]{3,2,1,0:T(8,128)S(1)}, u32[]{:S(2)}, u32[]{:S(2)}) collective-permute-start(f32[16,2,12,2]{3,2,1,0:T(8,128)S(1)} %get-tuple-element.416), channel_id=1, source_target_pairs={{0,1},{1,2},{2,3},{3,4},{4,5},{5,6},{6,7},{7,8},{8,9},{9,10},{10,1... | collective-permute-start | bytes 9224 | tf_op jit(solution)/shard_map/ppermute | solution.py:22
  281.5 7.6 %collective-permute-start.51 = (f32[16,2,12,2]{3,2,1,0:T(8,128)S(1)}, f32[16,2,12,2]{3,2,1,0:T(8,128)S(1)}, u32[]{:S(2)}, u32[]{:S(2)}) collective-permute-start(f32[16,2,12,2]{3,2,1,0:T(8,128)S(1)} %get-tuple-element.413), channel_id=1, source_target_pairs={{1,0},{2,1},{3,2},{4,3},{5,4},{6,5},{7,6},{8,7},{9,8},{10,9},{11,1... | collective-permute-start | bytes 9224 | tf_op jit(solution)/shard_map/ppermute | solution.py:24
  285.8 9.1 %collective-permute-start.50 = (f32[16,2,12,2]{3,2,1,0:T(8,128)S(1)}, f32[16,2,12,2]{3,2,1,0:T(8,128)S(1)}, u32[]{:S(2)}, u32[]{:S(2)}) collective-permute-start(f32[16,2,12,2]{3,2,1,0:T(8,128)S(1)} %get-tuple-element.414), channel_id=1, source_target_pairs={{0,1},{1,2},{2,3},{3,4},{4,5},{5,6},{6,7},{7,8},{8,9},{9,10},{10,1... | collective-permute-start | bytes 9224 | tf_op jit(solution)/shard_map/ppermute | solution.py:22
  304.2 7.7 %collective-permute-start.55 = (f32[16,2,12,2]{3,2,1,0:T(8,128)S(1)}, f32[16,2,12,2]{3,2,1,0:T(8,128)S(1)}, u32[]{:S(2)}, u32[]{:S(2)}) collective-permute-start(f32[16,2,12,2]{3,2,1,0:T(8,128)S(1)} %get-tuple-element.411), channel_id=1, source_target_pairs={{1,0},{2,1},{3,2},{4,3},{5,4},{6,5},{7,6},{8,7},{9,8},{10,9},{11,1... | collective-permute-start | bytes 9224 | tf_op jit(solution)/shard_map/ppermute | solution.py:24
  308.6 8.9 %collective-permute-start.54 = (f32[16,2,12,2]{3,2,1,0:T(8,128)S(1)}, f32[16,2,12,2]{3,2,1,0:T(8,128)S(1)}, u32[]{:S(2)}, u32[]{:S(2)}) collective-permute-start(f32[16,2,12,2]{3,2,1,0:T(8,128)S(1)} %get-tuple-element.412), channel_id=1, source_target_pairs={{0,1},{1,2},{2,3},{3,4},{4,5},{5,6},{6,7},{7,8},{8,9},{9,10},{10,1... | collective-permute-start | bytes 9224 | tf_op jit(solution)/shard_map/ppermute | solution.py:22
  330.7 9.9 %collective-permute-start.58 = (f32[16,2,12,2]{3,2,1,0:T(8,128)S(1)}, f32[16,2,12,2]{3,2,1,0:T(8,128)S(1)}, u32[]{:S(2)}, u32[]{:S(2)}) collective-permute-start(f32[16,2,12,2]{3,2,1,0:T(8,128)S(1)} %get-tuple-element.410), channel_id=1, source_target_pairs={{0,1},{1,2},{2,3},{3,4},{4,5},{5,6},{6,7},{7,8},{8,9},{9,10},{10,1... | collective-permute-start | bytes 9224 | tf_op jit(solution)/shard_map/ppermute | solution.py:22
  349.1 8.0 %collective-permute-start.63 = (f32[16,2,12,2]{3,2,1,0:T(8,128)S(1)}, f32[16,2,12,2]{3,2,1,0:T(8,128)S(1)}, u32[]{:S(2)}, u32[]{:S(2)}) collective-permute-start(f32[16,2,12,2]{3,2,1,0:T(8,128)S(1)} %get-tuple-element.407), channel_id=1, source_target_pairs={{1,0},{2,1},{3,2},{4,3},{5,4},{6,5},{7,6},{8,7},{9,8},{10,9},{11,1... | collective-permute-start | bytes 9224 | tf_op jit(solution)/shard_map/ppermute | solution.py:24
  353.8 9.6 %collective-permute-start.62 = (f32[16,2,12,2]{3,2,1,0:T(8,128)S(1)}, f32[16,2,12,2]{3,2,1,0:T(8,128)S(1)}, u32[]{:S(2)}, u32[]{:S(2)}) collective-permute-start(f32[16,2,12,2]{3,2,1,0:T(8,128)S(1)} %get-tuple-element.408), channel_id=1, source_target_pairs={{0,1},{1,2},{2,3},{3,4},{4,5},{5,6},{6,7},{7,8},{8,9},{9,10},{10,1... | collective-permute-start | bytes 9224 | tf_op jit(solution)/shard_map/ppermute | solution.py:22
  (45 other events, 203.3 us)
where the time goes:
time: 463 us; the launch traced here: 454 us
  waiting for transfers between devices  163 us (35%)
  starting transfers between devices  159 us (34%)
  blocking collectives  80.3 us (17%)
  other arithmetic  29.8 us (6%)
  local copies, waits for them, and re-layouts  19.1 us (4%)
    ppermute x32, starting transfers between devices, padded(): lax.ppermute(head, axis, [((i + 1) % count, i) for i in range(count)])  156 us
    ppermute x32, waiting for transfers between devices, padded(): lax.ppermute(tail, axis, [(i, (i + 1) % count) for i in range(count)])  94.3 us
    psum x1, blocking collectives, per_device(): results.append(lax.psum(local_terms, ('gx', 'gy')) * norm)  80.3 us
    ppermute x32, waiting for transfers between devices, padded(): lax.ppermute(head, axis, [((i + 1) % count, i) for i in range(count)])  68.6 us
    unnamed x58, local copies, waits for them, and re-layouts  9.32 us
  transfers between devices with their start and end apart: 64, of which 62 were waited for; matrix products, arithmetic and copies ran while one was open for 1% of the time, Pallas kernels for 0%

commit v1 on v0

v1 whole, which is shorter than its diff:
```python
import functools
import math

import jax
import jax.numpy as jnp
from jax import lax
from jax.experimental import pallas as pl
from jax.experimental.pallas import tpu as pltpu
from jax.sharding import PartitionSpec as P

APPLY = 4
STEPS = 4
TIME_STEP = 2.6

ROWS = 8
LANES = 128
EDGE = 32
REGION = 3 * ROWS
TILES = 3
VMEM_LIMIT = 48 * 1024 * 1024

HALF = [(p, q) for p in range(3) for q in range(-2, 3) if p > 0 or q > 0]
CROSS = 2 * len(HALF)
ONSITE = CROSS + 1
KINDS = ONSITE + 2
SHIFTED = [(number, half) for number, half in enumerate(HALF) if half[1] != 0]
SHIFT_SLOT = {half: 2 * place for place, (_, half) in enumerate(SHIFTED)}
COEF_ROWS = KINDS + 2 * len(SHIFTED)


def bessel(order, arg):
    total = 0.0
    for term in range(40):
        total += (
            (-1.0) ** term
            * (arg / 2.0) ** (2 * term + order)
            / (math.factorial(term) * math.factorial(term + order))
        )
    return total


def roll(tile, amount):
    amount = amount % LANES
    return tile if amount == 0 else pltpu.roll(tile, amount, 1)


def lane_ids():
    return lax.broadcasted_iota(jnp.int32, (ROWS, LANES), 1)


def shift_tiles(tiles, amount, lanes):
    even, odd, tail = (roll(tile, amount) for tile in tiles)
    if amount > 0:
        tail = jnp.where(lanes < amount, even, tail)
        tail = jnp.where((lanes >= 64) & (lanes < 64 + amount), odd, tail)
    else:
        even = jnp.where(lanes >= LANES + amount, tail, even)
        odd = jnp.where((lanes >= 64 + amount) & (lanes < 64), tail, odd)
    return even, odd, tail


def in_group(lanes, group):
    return (lanes >= EDGE * group) & (lanes < EDGE * (group + 1))


def turned(real, imag):
    return roll(real, EDGE), roll(imag, EDGE + 64)


def pack_kernel(vectors, slots, state, offsets, index, kinds, hop_table, onsite_table, coef, to_right, to_left):
    lanes = lane_ids()
    low = lanes < 64
    first = in_group(lanes, 0) | in_group(lanes, 2)
    for v in range(vectors):
        strips = []
        for a in range(2):
            real, imag = turned(state[0, v, a], state[1, v, a])
            strips.append(jnp.where(low, real, imag))
        to_right[v] = jnp.where(first, strips[0], roll(strips[1], EDGE))
        to_left[v] = jnp.where(first, roll(strips[1], -EDGE), strips[0])
    table = jnp.broadcast_to(hop_table[...], (ROWS, LANES))
    levels = jnp.broadcast_to(onsite_table[...], (ROWS, LANES))
    arrays = [jnp.zeros((ROWS, LANES), jnp.float32) for _ in range(KINDS)]
    for a in range(2):
        for slot in range(slots):
            amount = jnp.take_along_axis(table, index[slot, a], axis=1)
            code = offsets[slot, a]
            for number, (p, q) in enumerate(HALF):
                at = 2 * number + a
                arrays[at] = arrays[at] + jnp.where(code == 5 * (p + 2) + q + 2, amount, 0.0)
            if a == 0:
                arrays[CROSS] = arrays[CROSS] + jnp.where(code == 12, amount, 0.0)
        arrays[ONSITE + a] = jnp.take_along_axis(levels, kinds[a], axis=1)
    for start in range(0, KINDS, 4):
        right = left = None
        for group in range(min(4, KINDS - start)):
            double = 2.0 * arrays[start + group]
            coef[start + group] = double
            base = roll(double, EDGE)
            from_tail = roll(base, EDGE * group)
            from_head = roll(base, EDGE * (group - 1))
            right = from_tail if right is None else jnp.where(in_group(lanes, group), from_tail, right)
            left = from_head if left is None else jnp.where(in_group(lanes, group), from_head, left)
        to_right[vectors + start // 4] = right
        to_left[vectors + start // 4] = left


def widen_kernel(vectors, state, coef, from_left, from_right, wide):
    lanes = lane_ids()
    groups = [in_group(lanes, g) for g in range(4)]
    for v in range(vectors):
        for a in range(2):
            real, imag = turned(state[0, v, a], state[1, v, a])
            left = roll(from_left[v], -EDGE * a)
            right = roll(from_right[v], EDGE * a)
            at = (2 * v + a) * TILES
            wide[at] = jnp.where(groups[0], left, real)
            wide[at + 1] = jnp.where(groups[2], left, imag)
            wide[at + 2] = jnp.where(groups[0], real, jnp.where(groups[2], imag, right))
    base = 2 * vectors * TILES
    for pair in range(0, KINDS, 2):
        tails = None
        for j in range(pair, min(pair + 2, KINDS)):
            group = j % 4
            body = roll(coef[j], EDGE)
            left = roll(from_left[vectors + j // 4], -EDGE * group)
            right = roll(from_right[vectors + j // 4], EDGE * (1 - group))
            wide[base + j] = jnp.where(groups[0], left, body)
            tail = jnp.where(groups[0], body, right)
            tails = tail if tails is None else jnp.where(lanes < 64, tails, roll(tail, 64))
        wide[base + KINDS + pair // 2] = tails


def spread_coefficients(base, blocks, coefs):
    lanes = lane_ids()
    low = lanes < 64
    for part, block in enumerate(blocks):
        rows = pl.ds(ROWS * part, ROWS)
        for j in range(KINDS):
            even = block[base + j]
            odd = roll(even, 64)
            tail = block[base + KINDS + j // 2]
            other = roll(tail, 64)
            tail = jnp.where(low, tail, other) if j % 2 == 0 else jnp.where(low, other, tail)
            tiles = (even, odd, tail)
            for t in range(TILES):
                coefs[TILES * j + t, rows, :] = tiles[t]
            if j < CROSS and HALF[j // 2][1] != 0:
                moved = shift_tiles(tiles, HALF[j // 2][1], lanes)
                at = KINDS + SHIFT_SLOT[HALF[j // 2]] + j % 2
                for t in range(TILES):
                    coefs[TILES * at + t, rows, :] = moved[t]


def coefficient(coefs, dx, dy, a, t, top):
    source = a if (dx + dy) % 2 else 1 - a
    if (dx, dy) == (0, 0):
        at, row = CROSS, top
    elif (dx, dy) in HALF:
        at = KINDS + SHIFT_SLOT[(dx, dy)] + a if dy else 2 * HALF.index((dx, dy)) + a
        row = top
    else:
        at, row = 2 * HALF.index((-dx, -dy)) + source, top + dx
    return source, coefs[TILES * at + t, pl.ds(row, ROWS), :]


def apply_twice(field, coefs, a, group, width, top, lanes):
    sums = [[[None] * 5 for _ in range(TILES)] for _ in range(width)]
    for dx in range(-2, 3):
        rows = pl.ds(top + dx, ROWS)
        for t in range(TILES):
            values = [
                [field[((group * width + w) * 2 + b) * TILES + t, rows, :] for b in range(2)]
                for w in range(width)
            ]
            for dy in range(-2, 3):
                source, factor = coefficient(coefs, dx, dy, a, t, top)
                for w in range(width):
                    term = factor * values[w][source]
                    old = sums[w][t][dy + 2]
                    sums[w][t][dy + 2] = term if old is None else old + term
            if dx == 0:
                factor = coefs[TILES * (ONSITE + a) + t, pl.ds(top, ROWS), :]
                for w in range(width):
                    sums[w][t][2] = sums[w][t][2] + factor * values[w][a]
    results = []
    for w in range(width):
        total = [sums[w][t][2] for t in range(TILES)]
        for dy in (-2, -1, 1, 2):
            moved = shift_tiles([sums[w][t][dy + 2] for t in range(TILES)], -dy, lanes)
            total = [total[t] + moved[t] for t in range(TILES)]
        results.append(total)
    return results


def time_step(vectors, width, coefs, probe, terms, products, finish):
    lanes = lane_ids()
    scale = [bessel(order, TIME_STEP) * (1.0 if order == 0 else 2.0) for order in range(APPLY + 1)]
    for order in range(1, APPLY + 1):
        low, high = 2 * order, REGION - 2 * order
        tops = list(range(low, high - ROWS + 1, ROWS))
        if tops[-1] != high - ROWS:
            tops.append(high - ROWS)
        for a in range(2):

            def body(group, carry):
                for top in tops:
                    images = apply_twice(terms[order - 1], coefs, a, group, width, top, lanes)
                    for w in range(width):
                        v = group * width + w
                        at = (2 * v + a) * TILES
                        rows = pl.ds(top, ROWS)
                        if order == 1:
                            new = [0.5 * images[w][t] for t in range(TILES)]
                        else:
                            new = [images[w][t] - terms[order - 2][at + t, rows, :] for t in range(TILES)]
                        if order < APPLY:
                            for t in range(TILES):
                                terms[order][at + t, rows, :] = new[t]
                            continue
                        even = []
                        odd = []
                        for t in range(TILES):
                            part = [terms[k][at + t, rows, :] for k in range(APPLY)]
                            even.append(scale[0] * part[0] - scale[2] * part[2] + scale[4] * new[t])
                            odd.append(roll(scale[1] * part[1] - scale[3] * part[3], 64))
                        real = even[0] + odd[1]
                        imag = even[1] - odd[0]
                        tail = even[2] + jnp.where(lanes < 64, odd[2], -odd[2])
                        own_real = roll(jnp.where(in_group(lanes, 0), tail, real), -EDGE)
                        own_imag = roll(jnp.where(in_group(lanes, 2), tail, imag), -EDGE - 64)
                        probe_real, probe_imag = probe[0, v, a], probe[1, v, a]
                        same = probe_real * own_real + probe_imag * own_imag
                        cross = probe_real * own_imag - probe_imag * own_real
                        if a == 1:
                            same = same + products[v]
                            cross = cross + products[vectors + v]
                        products[v] = same
                        products[vectors + v] = cross
                        finish(at, v, a, (real, imag, tail), (own_real, own_imag))
                return carry

            lax.fori_loop(0, vectors // width, body, 0)


def probe_row(products):
    count = products.shape[0]
    sums = jnp.sum(jnp.sum(products[...], axis=1), axis=1, keepdims=True)
    rows = lax.broadcasted_iota(jnp.int32, (count, LANES), 0)
    lanes = lax.broadcasted_iota(jnp.int32, (count, LANES), 1)
    return jnp.sum(jnp.where(rows == lanes, sums, 0.0), axis=0, keepdims=True)


def gather_rows(vectors, first, own, up, down):
    for part, block in enumerate((up, own, down)):
        for at in range(2 * vectors * TILES):
            first[at, pl.ds(ROWS * part, ROWS), :] = block[at]


def first_kernel(vectors, width, own, up, down, probe, state, coefs, sums, t0, t1, t2, t3, products):
    gather_rows(vectors, t0, own, up, down)
    spread_coefficients(2 * vectors * TILES, (up, own, down), coefs)

    def finish(at, v, a, tiles, cells):
        for t in range(TILES):
            state[at + t] = tiles[t]

    time_step(vectors, width, coefs, probe, (t0, t1, t2, t3), products, finish)
    sums[...] = probe_row(products)


def middle_kernel(vectors, width, own, up, down, coefs, probe, state, sums, t0, t1, t2, t3, products):
    gather_rows(vectors, t0, own, up, down)

    def finish(at, v, a, tiles, cells):
        for t in range(TILES):
            state[at + t] = tiles[t]

    time_step(vectors, width, coefs, probe, (t0, t1, t2, t3), products, finish)
    sums[...] = probe_row(products)


def last_kernel(vectors, width, own, up, down, coefs, probe, s0, s1, s2, state, sums, t0, t1, t2, t3, products):
    gather_rows(vectors, t0, own, up, down)

    def finish(at, v, a, tiles, cells):
        state[0, v, a] = cells[0]
        state[1, v, a] = cells[1]

    time_step(vectors, width, coefs, probe, (t0, t1, t2, t3), products, finish)
    rows = jnp.concatenate([s0[...], s1[...], s2[...], probe_row(products)], axis=0)
    for copy in range(sums.shape[0]):
        sums[copy] = rows


def call(kernel, out_shapes, scratch=()):
    return pl.pallas_call(
        kernel,
        out_shape=[jax.ShapeDtypeStruct(shape, jnp.float32) for shape in out_shapes],
        scratch_shapes=[pltpu.VMEM(shape, jnp.float32) for shape in scratch],
        compiler_params=pltpu.CompilerParams(vmem_limit_bytes=VMEM_LIMIT),
    )


def neighbours(block, axis):
    count = lax.axis_size(axis)
    return (
        lax.ppermute(block, axis, [(i, (i + 1) % count) for i in range(count)]),
        lax.ppermute(block, axis, [((i + 1) % count, i) for i in range(count)]),
    )


def per_device(start, probe, offsets, orbitals, index, kinds, hop_table, onsite_table):
    vectors = start.shape[1]
    slots = offsets.shape[0]
    width = 2
    cells = 2 * vectors * TILES
    edge_tiles = vectors + (KINDS + 3) // 4
    wide_tiles = cells + KINDS + (KINDS + 1) // 2
    table = jnp.pad(hop_table, (0, LANES - hop_table.shape[0]))[None]
    levels = jnp.pad(onsite_table, (0, LANES - onsite_table.shape[0]))[None]
    block = (ROWS, LANES)
    coef, to_right, to_left = call(
        functools.partial(pack_kernel, vectors, slots),
        [(KINDS, *block), (edge_tiles, *block), (edge_tiles, *block)],
    )(start, offsets, index, kinds, table, levels)
    count = lax.axis_size("gy")
    from_left = lax.ppermute(to_right, "gy", [(i, (i + 1) % count) for i in range(count)])
    from_right = lax.ppermute(to_left, "gy", [((i + 1) % count, i) for i in range(count)])
    (wide,) = call(functools.partial(widen_kernel, vectors), [(wide_tiles, *block)])(
        start, coef, from_left, from_right
    )
    scratch = [(cells, REGION, LANES)] * APPLY + [(2 * vectors, *block)]
    below, above = neighbours(wide, "gx")
    state, coefs, first = call(
        functools.partial(first_kernel, vectors, width),
        [(cells, *block), (COEF_ROWS * TILES, REGION, LANES), (1, LANES)],
        scratch,
    )(wide, below, above, probe)
    sums = [first]
    for _ in range(STEPS - 2):
        below, above = neighbours(state, "gx")
        state, part = call(
            functools.partial(middle_kernel, vectors, width), [(cells, *block), (1, LANES)], scratch
        )(state, below, above, coefs, probe)
        sums.append(part)
    below, above = neighbours(state, "gx")
    final, rows = call(
        functools.partial(last_kernel, vectors, width),
        [start.shape, (lax.axis_size("gx"), STEPS, LANES)],
        scratch,
    )(state, below, above, coefs, probe, *sums)
    part = jnp.sum(lax.all_to_all(rows, "gx", 0, 0), axis=0)
    copies = jnp.broadcast_to(part[None], (count, STEPS, LANES))
    total = jnp.sum(lax.all_to_all(copies, "gy", 0, 0), axis=0)
    total_cells = start.shape[3] * start.shape[4] * lax.axis_size("gx") * count
    norm = 1.0 / math.sqrt(2.0 * 2 * total_cells)
    return final, total[:, : 2 * vectors].reshape(STEPS, 2, vectors) * norm


def solution(mesh):
    return jax.shard_map(
        per_device,
        mesh=mesh,
        in_specs=(
            P(None, None, None, "gx", "gy"),
            P(None, None, None, "gx", "gy"),
            P(None, None, "gx", "gy"),
            P(None, None, "gx", "gy"),
            P(None, None, "gx", "gy"),
            P(None, "gx", "gy"),
            P(),
            P(),
        ),
        out_specs=(P(None, None, None, "gx", "gy"), P()),
        check_vma=False,
    )
```

time: 463 us -> 112 us (0.24); the launches traced: 454 us -> 111 us
  waiting for transfers between devices: 163 us -> 19.8 us
  starting transfers between devices: 159 us -> 25.1 us
  blocking collectives: 80.3 us -> 31.2 us
  other arithmetic: 29.8 us -> 0.06 us
  Pallas kernels: 0 us -> 28.8 us
  local copies, waits for them, and re-layouts: 19.1 us -> 5.64 us
    ppermute x64 -> x10, waiting for transfers between devices: 163 us -> 19.8 us  [the longest x4 11.3 us: neighbours(): lax.ppermute(block, axis, [((i + 1) % count, i) for i in range(count)])]
    ppermute x64 -> x10, starting transfers between devices: 159 us -> 25.1 us  [the longest x4 15.7 us: neighbours(): lax.ppermute(block, axis, [((i + 1) % count, i) for i in range(count)])]
    psum x1 -> x0, blocking collectives: 80.3 us -> none  [per_device(): results.append(lax.psum(local_terms, ('gx', 'gy')) * norm)]
    all_to_all x0 -> x2, blocking collectives: none -> 31.2 us  [the longest x1 19.1 us: per_device(): total = jnp.sum(lax.all_to_all(copies, 'gy', 0, 0), axis=0)]
    pallas_call x0 -> x6, Pallas kernels: none -> 28.8 us  [the longest x2 12.3 us: per_device(): call(functools.partial(middle_kernel, vectors, width), [(cells, *block),...]
    reduce_sum x84 -> x2, other arithmetic: 9.45 us -> 0.05 us  [the longest x1 0.03 us: per_device(): total = jnp.sum(lax.all_to_all(copies, 'gy', 0, 0), axis=0)]
    concatenate x45 -> x0, other arithmetic: 6.56 us -> none  [the longest x32 6.31 us: padded(): jnp.concatenate([lax.ppermute(tail, axis, [(i, (i + 1) % count) for i in...]
    unnamed x58 -> x10, local copies, waits for them, and re-layouts: 9.32 us -> 4.28 us
  transfers between devices with their start and end apart: 64 -> 10, of which waited for: 62 -> 8; matrix products, arithmetic and copies ran while one was open for 1% -> 0% of each run, Pallas kernels for 0% -> 0%
where the time goes in v1:
time: 112 us; the launch traced here: 111 us
  blocking collectives  31.2 us (28%)
  Pallas kernels  28.8 us (26%)
  starting transfers between devices  25.1 us (22%)
  waiting for transfers between devices  19.8 us (18%)
  local copies, waits for them, and re-layouts  5.64 us (5%)
    all_to_all x1, blocking collectives, per_device(): total = jnp.sum(lax.all_to_all(copies, 'gy', 0, 0), axis=0)  19.1 us
    ppermute x4, starting transfers between devices, neighbours(): lax.ppermute(block, axis, [((i + 1) % count, i) for i in range(count)])  15.7 us
    pallas_call x2, Pallas kernels, per_device(): call(functools.partial(middle_kernel, vectors, width), [(cells, *block),...  12.3 us
    all_to_all x1, blocking collectives, per_device(): part = jnp.sum(lax.all_to_all(rows, 'gx', 0, 0), axis=0)  12.1 us
    ppermute x4, waiting for transfers between devices, neighbours(): lax.ppermute(block, axis, [((i + 1) % count, i) for i in range(count)])  11.3 us
    pallas_call x1, Pallas kernels, per_device(): call(functools.partial(first_kernel, vectors, width), [(cells, *block), (...  9.02 us
    ppermute x4, waiting for transfers between devices, neighbours(): lax.ppermute(block, axis, [(i, (i + 1) % count) for i in range(count)])  6.97 us
    pallas_call x1, Pallas kernels, per_device(): call(functools.partial(last_kernel, vectors, width), [start.shape, (lax.a...  6.72 us
  transfers between devices with their start and end apart: 10, of which 8 were waited for; matrix products, arithmetic and copies ran while one was open for 0% of the time, Pallas kernels for 0%

profile of v1, /device:TPU:1, one launch (start us, length us, event | category | flops | bytes accessed | tf_op | source)
XLA Modules:
  0.0 111.3 jit_solution(1427778770539575405)
XLA Ops:
  1.3 0.9 copy-done.1
  2.2 0.9 copy-done.2
  3.1 0.9 copy-done.3
  5.1 3.7 %collective-permute-start = (f32[15,8,128]{2,1,0:T(8,128)S(1)}, f32[15,8,128]{2,1,0:T(8,128)S(1)}, u32[]{:S(2)}, u32[]{:S(2)}) collective-permute-start(f32[15,8,128]{2,1,0:T(8,128)S(1)} %get-tuple-element.15), channel_id=1, source_target_pairs={{0,1},{1,2},{2,3},{3,4},{4,5},{5,6},{6,7},{7,8},{8,9},{9,10},{10,1... | collective-permute-start | bytes 184328 | tf_op jit(solution)/shard_map/ppermute | solution.py:328
  8.7 5.4 %collective-permute-start.1 = (f32[15,8,128]{2,1,0:T(8,128)S(1)}, f32[15,8,128]{2,1,0:T(8,128)S(1)}, u32[]{:S(2)}, u32[]{:S(2)}) collective-permute-start(f32[15,8,128]{2,1,0:T(8,128)S(1)} %get-tuple-element.16), channel_id=1, source_target_pairs={{1,0},{2,1},{3,2},{4,3},{5,4},{6,5},{7,6},{8,7},{9,8},{10,9},{11,1... | collective-permute-start | bytes 184328 | tf_op jit(solution)/shard_map/ppermute | solution.py:329
  14.1 1.5 %collective-permute-done.from_left = f32[15,8,128]{2,1,0:T(8,128)S(1)} collective-permute-done((f32[15,8,128]{2,1,0:T(8,128)S(1)}, f32[15,8,128]{2,1,0:T(8,128)S(1)}, u32[]{:S(2)}, u32[]{:S(2)}) %collective-permute-start) | collective-permute-done | bytes 61472 | tf_op jit(solution)/shard_map/ppermute | solution.py:328
  15.9 1.6 %collective-permute-start.3 = (f32[89,8,128]{2,1,0:T(8,128)S(1)}, f32[89,8,128]{2,1,0:T(8,128)S(1)}, u32[]{:S(2)}, u32[]{:S(2)}) collective-permute-start(f32[89,8,128]{2,1,0:T(8,128)S(1)} %shard_map.87.own), channel_id=1, source_target_pairs={{16,0},{32,16},{48,32},{64,48},{80,64},{96,80},{112,96},{128,112},... | collective-permute-start | bytes 1093640 | tf_op jit(solution)/shard_map/ppermute | solution.py:309
  17.9 7.2 %collective-permute-done.3.down = f32[89,8,128]{2,1,0:T(8,128)S(1)} collective-permute-done((f32[89,8,128]{2,1,0:T(8,128)S(1)}, f32[89,8,128]{2,1,0:T(8,128)S(1)}, u32[]{:S(2)}, u32[]{:S(2)}) %collective-permute-start.3) | collective-permute-done | bytes 364576 | tf_op jit(solution)/shard_map/ppermute | solution.py:309
  25.1 0.9 copy-done
  26.0 9.0 %shard_map.88 = (f32[48,8,128]{2,1,0:T(8,128)S(1)}, f32[141,24,128]{2,1,0:T(8,128)S(1)}, f32[1,128]{1,0:T(1,128)S(1)}) custom-call(f32[89,8,128]{2,1,0:T(8,128)S(1)} %shard_map.87.own, f32[89,8,128]{2,1,0:T(8,128)S(1)} %collective-permute-done.2.up, f32[89,8,128]{2,1,0:T(8,128)S(1)} %collective-permute-done.3.down, f32[2,8,2,8,128]{4,3,2,1,0:T(8,128)S(1)} %copy-done), custom_call_target="tpu_custom_call" | custom-call | tf_op jit(solution)/shard_map/pallas_call | solution.py:335
  35.0 4.9 %collective-permute-start.5 = (f32[48,8,128]{2,1,0:T(8,128)S(1)}, f32[48,8,128]{2,1,0:T(8,128)S(1)}, u32[]{:S(2)}, u32[]{:S(2)}) collective-permute-start(f32[48,8,128]{2,1,0:T(8,128)S(1)} %get-tuple-element.17.own), channel_id=1, source_target_pairs={{16,0},{32,16},{48,32},{64,48},{80,64},{96,80},{112,96},{128,112},... | collective-permute-start | bytes 589832 | tf_op jit(solution)/shard_map/ppermute | solution.py:309
  39.9 1.1 collective-permute-done.5.down
  41.0 2.9 %collective-permute-done.4.up = f32[48,8,128]{2,1,0:T(8,128)S(1)} collective-permute-done((f32[48,8,128]{2,1,0:T(8,128)S(1)}, f32[48,8,128]{2,1,0:T(8,128)S(1)}, u32[]{:S(2)}, u32[]{:S(2)}) %collective-permute-start.4) | collective-permute-done | bytes 196640 | tf_op jit(solution)/shard_map/ppermute | solution.py:308
  43.8 6.2 %shard_map.89 = (f32[48,8,128]{2,1,0:T(8,128)S(1)}, f32[1,128]{1,0:T(1,128)S(1)}) custom-call(f32[48,8,128]{2,1,0:T(8,128)S(1)} %get-tuple-element.17.own, f32[48,8,128]{2,1,0:T(8,128)S(1)} %collective-permute-done.4.up, f32[48,8,128]{2,1,0:T(8,128)S(1)} %collective-permute-done.5.down, f32[141,24,128]{2,1,0:T(8,128)S(1)} %get-tuple-element.18.coefs, ...), custom_call_target="tpu_custom_call" | custom-call | tf_op jit(solution)/shard_map/pallas_call | solution.py:343
  50.0 3.9 %collective-permute-start.7 = (f32[48,8,128]{2,1,0:T(8,128)S(1)}, f32[48,8,128]{2,1,0:T(8,128)S(1)}, u32[]{:S(2)}, u32[]{:S(2)}) collective-permute-start(f32[48,8,128]{2,1,0:T(8,128)S(1)} %get-tuple-element.19.own), channel_id=1, source_target_pairs={{16,0},{32,16},{48,32},{64,48},{80,64},{96,80},{112,96},{128,112},... | collective-permute-start | bytes 589832 | tf_op jit(solution)/shard_map/ppermute | solution.py:309
  53.9 1.9 %collective-permute-done.7.down = f32[48,8,128]{2,1,0:T(8,128)S(1)} collective-permute-done((f32[48,8,128]{2,1,0:T(8,128)S(1)}, f32[48,8,128]{2,1,0:T(8,128)S(1)}, u32[]{:S(2)}, u32[]{:S(2)}) %collective-permute-start.7) | collective-permute-done | bytes 196640 | tf_op jit(solution)/shard_map/ppermute | solution.py:309
  55.9 1.2 %collective-permute-done.6.up = f32[48,8,128]{2,1,0:T(8,128)S(1)} collective-permute-done((f32[48,8,128]{2,1,0:T(8,128)S(1)}, f32[48,8,128]{2,1,0:T(8,128)S(1)}, u32[]{:S(2)}, u32[]{:S(2)}) %collective-permute-start.6) | collective-permute-done | bytes 196640 | tf_op jit(solution)/shard_map/ppermute | solution.py:308
  57.1 6.2 %shard_map.90 = (f32[48,8,128]{2,1,0:T(8,128)S(1)}, f32[1,128]{1,0:T(1,128)S(1)}) custom-call(f32[48,8,128]{2,1,0:T(8,128)S(1)} %get-tuple-element.19.own, f32[48,8,128]{2,1,0:T(8,128)S(1)} %collective-permute-done.6.up, f32[48,8,128]{2,1,0:T(8,128)S(1)} %collective-permute-done.7.down, f32[141,24,128]{2,1,0:T(8,128)S(1)} %get-tuple-element.18.coefs, ...), custom_call_target="tpu_custom_call" | custom-call | tf_op jit(solution)/shard_map/pallas_call | solution.py:343
  63.3 5.4 %collective-permute-start.9 = (f32[48,8,128]{2,1,0:T(8,128)S(1)}, f32[48,8,128]{2,1,0:T(8,128)S(1)}, u32[]{:S(2)}, u32[]{:S(2)}) collective-permute-start(f32[48,8,128]{2,1,0:T(8,128)S(1)} %get-tuple-element.20.own), channel_id=1, source_target_pairs={{16,0},{32,16},{48,32},{64,48},{80,64},{96,80},{112,96},{128,112},... | collective-permute-start | bytes 589832 | tf_op jit(solution)/shard_map/ppermute | solution.py:309
  68.6 1.1 collective-permute-done.9.down
  69.7 2.9 %collective-permute-done.8.up = f32[48,8,128]{2,1,0:T(8,128)S(1)} collective-permute-done((f32[48,8,128]{2,1,0:T(8,128)S(1)}, f32[48,8,128]{2,1,0:T(8,128)S(1)}, u32[]{:S(2)}, u32[]{:S(2)}) %collective-permute-start.8) | collective-permute-done | bytes 196640 | tf_op jit(solution)/shard_map/ppermute | solution.py:308
  72.6 6.7 %shard_map.91 = (f32[2,8,2,8,128]{4,3,2,1,0:T(8,128)}, f32[16,4,128]{2,1,0:T(4,128)S(1)}) custom-call(f32[48,8,128]{2,1,0:T(8,128)S(1)} %get-tuple-element.20.own, f32[48,8,128]{2,1,0:T(8,128)S(1)} %collective-permute-done.8.up, f32[48,8,128]{2,1,0:T(8,128)S(1)} %collective-permute-done.9.down, f32[141,24,128]{2,1,0:T(8,128)S(1)} %get-tuple-element.18.coefs, ...), custom_call_target="tpu_custom_call" | custom-call | tf_op jit(solution)/shard_map/pallas_call | solution.py:348
  79.3 12.1 %all_to_all.10 = f32[16,4,128]{2,1,0:T(4,128)S(1)} all-to-all(f32[16,4,128]{2,1,0:T(4,128)S(1)} %get-tuple-element.25), channel_id=1, replica_groups=mesh['gx'=16,'gy'=16] {'gx'}, dimensions={0} | all-to-all | bytes 65536 | tf_op jit(solution)/shard_map/all_to_all | solution.py:353
  91.4 19.1 %all_to_all.11 = f32[16,4,128]{2,1,0:T(4,128)S(1)} all-to-all(f32[16,4,128]{2,1,0:T(4,128)S(1)} %broadcast_in_dim.14), channel_id=1, replica_groups=mesh['gx'=16,'gy'=16] {'gy'}, dimensions={0} | all-to-all | bytes 65536 | tf_op jit(solution)/shard_map/all_to_all | solution.py:355
  (20 shorter events, 3.1 us)
Async XLA Ops:
  1.3 0.9 copy-start.1
  2.2 0.9 copy-start.2
  3.1 0.9 copy-start.3
  4.0 0.7 copy-start.4
  5.1 10.6 %collective-permute-start = (f32[15,8,128]{2,1,0:T(8,128)S(1)}, f32[15,8,128]{2,1,0:T(8,128)S(1)}, u32[]{:S(2)}, u32[]{:S(2)}) collective-permute-start(f32[15,8,128]{2,1,0:T(8,128)S(1)} %get-tuple-element.15), channel_id=1, source_target_pairs={{0,1},{1,2},{2,3},{3,4},{4,5},{5,6},{6,7},{7,8},{8,9},{9,10},{10,1... | collective-permute-start | bytes 184328 | tf_op jit(solution)/shard_map/ppermute | solution.py:328
  8.7 6.9 %collective-permute-start.1 = (f32[15,8,128]{2,1,0:T(8,128)S(1)}, f32[15,8,128]{2,1,0:T(8,128)S(1)}, u32[]{:S(2)}, u32[]{:S(2)}) collective-permute-start(f32[15,8,128]{2,1,0:T(8,128)S(1)} %get-tuple-element.16), channel_id=1, source_target_pairs={{1,0},{2,1},{3,2},{4,3},{5,4},{6,5},{7,6},{8,7},{9,8},{10,9},{11,1... | collective-permute-start | bytes 184328 | tf_op jit(solution)/shard_map/ppermute | solution.py:329
  15.9 9.2 %collective-permute-start.3 = (f32[89,8,128]{2,1,0:T(8,128)S(1)}, f32[89,8,128]{2,1,0:T(8,128)S(1)}, u32[]{:S(2)}, u32[]{:S(2)}) collective-permute-start(f32[89,8,128]{2,1,0:T(8,128)S(1)} %shard_map.87.own), channel_id=1, source_target_pairs={{16,0},{32,16},{48,32},{64,48},{80,64},{96,80},{112,96},{128,112},... | collective-permute-start | bytes 1093640 | tf_op jit(solution)/shard_map/ppermute | solution.py:309
  17.6 7.5 %collective-permute-start.2 = (f32[89,8,128]{2,1,0:T(8,128)S(1)}, f32[89,8,128]{2,1,0:T(8,128)S(1)}, u32[]{:S(2)}, u32[]{:S(2)}) collective-permute-start(f32[89,8,128]{2,1,0:T(8,128)S(1)} %shard_map.87.own), channel_id=1, source_target_pairs={{0,16},{16,32},{32,48},{48,64},{64,80},{80,96},{96,112},{112,128},... | collective-permute-start | bytes 1093640 | tf_op jit(solution)/shard_map/ppermute | solution.py:308
  25.1 0.9 copy-start
  35.0 5.9 %collective-permute-start.5 = (f32[48,8,128]{2,1,0:T(8,128)S(1)}, f32[48,8,128]{2,1,0:T(8,128)S(1)}, u32[]{:S(2)}, u32[]{:S(2)}) collective-permute-start(f32[48,8,128]{2,1,0:T(8,128)S(1)} %get-tuple-element.17.own), channel_id=1, source_target_pairs={{16,0},{32,16},{48,32},{64,48},{80,64},{96,80},{112,96},{128,112},... | collective-permute-start | bytes 589832 | tf_op jit(solution)/shard_map/ppermute | solution.py:309
  39.9 3.9 %collective-permute-start.4 = (f32[48,8,128]{2,1,0:T(8,128)S(1)}, f32[48,8,128]{2,1,0:T(8,128)S(1)}, u32[]{:S(2)}, u32[]{:S(2)}) collective-permute-start(f32[48,8,128]{2,1,0:T(8,128)S(1)} %get-tuple-element.17.own), channel_id=1, source_target_pairs={{0,16},{16,32},{32,48},{48,64},{64,80},{80,96},{96,112},{112,128},... | collective-permute-start | bytes 589832 | tf_op jit(solution)/shard_map/ppermute | solution.py:308
  50.0 5.8 %collective-permute-start.7 = (f32[48,8,128]{2,1,0:T(8,128)S(1)}, f32[48,8,128]{2,1,0:T(8,128)S(1)}, u32[]{:S(2)}, u32[]{:S(2)}) collective-permute-start(f32[48,8,128]{2,1,0:T(8,128)S(1)} %get-tuple-element.19.own), channel_id=1, source_target_pairs={{16,0},{32,16},{48,32},{64,48},{80,64},{96,80},{112,96},{128,112},... | collective-permute-start | bytes 589832 | tf_op jit(solution)/shard_map/ppermute | solution.py:309
  53.9 3.2 %collective-permute-start.6 = (f32[48,8,128]{2,1,0:T(8,128)S(1)}, f32[48,8,128]{2,1,0:T(8,128)S(1)}, u32[]{:S(2)}, u32[]{:S(2)}) collective-permute-start(f32[48,8,128]{2,1,0:T(8,128)S(1)} %get-tuple-element.19.own), channel_id=1, source_target_pairs={{0,16},{16,32},{32,48},{48,64},{64,80},{80,96},{96,112},{112,128},... | collective-permute-start | bytes 589832 | tf_op jit(solution)/shard_map/ppermute | solution.py:308
  63.3 6.4 %collective-permute-start.9 = (f32[48,8,128]{2,1,0:T(8,128)S(1)}, f32[48,8,128]{2,1,0:T(8,128)S(1)}, u32[]{:S(2)}, u32[]{:S(2)}) collective-permute-start(f32[48,8,128]{2,1,0:T(8,128)S(1)} %get-tuple-element.20.own), channel_id=1, source_target_pairs={{16,0},{32,16},{48,32},{64,48},{80,64},{96,80},{112,96},{128,112},... | collective-permute-start | bytes 589832 | tf_op jit(solution)/shard_map/ppermute | solution.py:309
  68.6 3.9 %collective-permute-start.8 = (f32[48,8,128]{2,1,0:T(8,128)S(1)}, f32[48,8,128]{2,1,0:T(8,128)S(1)}, u32[]{:S(2)}, u32[]{:S(2)}) collective-permute-start(f32[48,8,128]{2,1,0:T(8,128)S(1)} %get-tuple-element.20.own), channel_id=1, source_target_pairs={{0,16},{16,32},{32,48},{48,64},{64,80},{80,96},{96,112},{112,128},... | collective-permute-start | bytes 589832 | tf_op jit(solution)/shard_map/ppermute | solution.py:308

commit v2 on v1

v2 whole, which is shorter than its diff:
```python
import functools
import math

import jax
import jax.numpy as jnp
from jax import lax
from jax.experimental import pallas as pl
from jax.experimental.pallas import tpu as pltpu
from jax.sharding import PartitionSpec as P

APPLY = 4
STEPS = 4
TIME_STEP = 2.6

ROWS = 8
LANES = 128
EDGE = 32
REGION = 3 * ROWS
TILES = 3
PARTS = 2
VMEM_LIMIT = 48 * 1024 * 1024

HALF = [(p, q) for p in range(3) for q in range(-2, 3) if p > 0 or q > 0]
CROSS = 2 * len(HALF)
ONSITE = CROSS + 1
KINDS = ONSITE + 2
SHIFTED = [(number, half) for number, half in enumerate(HALF) if half[1] != 0]
SHIFT_SLOT = {half: 2 * place for place, (_, half) in enumerate(SHIFTED)}
COEF_ROWS = KINDS + 2 * len(SHIFTED)


def bessel(order, arg):
    total = 0.0
    for term in range(40):
        total += (
            (-1.0) ** term
            * (arg / 2.0) ** (2 * term + order)
            / (math.factorial(term) * math.factorial(term + order))
        )
    return total


def roll(tile, amount):
    amount = amount % LANES
    return tile if amount == 0 else pltpu.roll(tile, amount, 1)


def lane_ids():
    return lax.broadcasted_iota(jnp.int32, (ROWS, LANES), 1)


def shift_tiles(tiles, amount, lanes):
    even, odd, tail = (roll(tile, amount) for tile in tiles)
    if amount > 0:
        tail = jnp.where(lanes < amount, even, tail)
        tail = jnp.where((lanes >= 64) & (lanes < 64 + amount), odd, tail)
    else:
        even = jnp.where(lanes >= LANES + amount, tail, even)
        odd = jnp.where((lanes >= 64 + amount) & (lanes < 64), tail, odd)
    return even, odd, tail


def in_group(lanes, group):
    return (lanes >= EDGE * group) & (lanes < EDGE * (group + 1))


def turned(real, imag):
    return roll(real, EDGE), roll(imag, EDGE + 64)


def fetch(pairs, semaphores):
    copies = [pltpu.make_async_copy(source, target, semaphores.at[i]) for i, (source, target) in enumerate(pairs)]
    for copy in copies:
        copy.start()
    for copy in copies:
        copy.wait()


def pack_kernel(
    vectors, slots, start, probe, offsets, index, kinds, hop_table, onsite_table, parities,
    probe_copy, block, pair_one, pair_two, state, offsets_here, index_here, kinds_here, table_here, semaphores,
):
    fetch(
        [
            (start, state), (offsets, offsets_here), (index, index_here), (kinds, kinds_here),
            (hop_table, table_here), (probe, probe_copy),
        ],
        semaphores,
    )
    lanes = lane_ids()
    even = jnp.full((ROWS, LANES), parities[1], jnp.int32) == 0
    coefs_at = 4 * vectors

    def send(at, to_right, to_left):
        pair_one[at] = jnp.where(even, to_right, to_left)
        pair_two[at] = jnp.where(even, to_left, to_right)

    low = lanes < 64
    first = in_group(lanes, 0) | in_group(lanes, 2)
    for v in range(vectors):
        strips = []
        for a in range(2):
            block[4 * v + 2 * a] = state[0, v, a]
            block[4 * v + 2 * a + 1] = state[1, v, a]
            real, imag = turned(state[0, v, a], state[1, v, a])
            strips.append(jnp.where(low, real, imag))
        to_right = jnp.where(first, strips[0], roll(strips[1], EDGE))
        to_left = jnp.where(first, roll(strips[1], -EDGE), strips[0])
        send(v, to_right, to_left)
    entries = table_here[...]
    spare = LANES - entries.shape[1]
    table = jnp.broadcast_to(jnp.concatenate([entries, jnp.zeros((1, spare), jnp.float32)], axis=1), (ROWS, LANES))
    arrays = [jnp.zeros((ROWS, LANES), jnp.float32) for _ in range(KINDS)]
    for a in range(2):
        for slot in range(slots):
            amount = jnp.take_along_axis(table, index_here[slot, a], axis=1)
            code = offsets_here[slot, a]
            for number, (p, q) in enumerate(HALF):
                at = 2 * number + a
                arrays[at] = arrays[at] + jnp.where(code == 5 * (p + 2) + q + 2, amount, 0.0)
            if a == 0:
                arrays[CROSS] = arrays[CROSS] + jnp.where(code == 12, amount, 0.0)
        for entry in range(onsite_table.shape[0]):
            arrays[ONSITE + a] = jnp.where(kinds_here[a] == entry, onsite_table[entry], arrays[ONSITE + a])
    for start_at in range(0, KINDS, 4):
        right = left = None
        for group in range(min(4, KINDS - start_at)):
            double = 2.0 * arrays[start_at + group]
            block[coefs_at + start_at + group] = double
            base = roll(double, EDGE)
            from_tail = roll(base, EDGE * group)
            from_head = roll(base, EDGE * (group - 1))
            right = from_tail if right is None else jnp.where(in_group(lanes, group), from_tail, right)
            left = from_head if left is None else jnp.where(in_group(lanes, group), from_head, left)
        send(vectors + start_at // 4, right, left)


def sides(strips, parity):
    edge = strips.shape[0] // 2
    left_at = jnp.where(parity == 0, edge, 0)
    return lambda at: strips[left_at + at], lambda at: strips[edge - left_at + at]


def widen_state(block, left_of, right_of, v, a, lanes):
    real, imag = turned(block[4 * v + 2 * a], block[4 * v + 2 * a + 1])
    left = roll(left_of(v), -EDGE * a)
    right = roll(right_of(v), EDGE * a)
    first, third = in_group(lanes, 0), in_group(lanes, 2)
    return (
        jnp.where(first, left, real),
        jnp.where(third, left, imag),
        jnp.where(first, real, jnp.where(third, imag, right)),
    )


def widen_coef(vectors, block, left_of, right_of, j, lanes):
    group = j % 4
    body = roll(block[4 * vectors + j], EDGE)
    left = roll(left_of(vectors + j // 4), -EDGE * group)
    right = roll(right_of(vectors + j // 4), EDGE * (1 - group))
    first = in_group(lanes, 0)
    even = jnp.where(first, left, body)
    tail = jnp.where(first, body, right)
    return even, roll(even, 64), jnp.where(lanes < 64, tail, roll(tail, 64))


def spread(vectors, block, left_of, right_of, put):
    lanes = lane_ids()
    for j in range(KINDS):
        tiles = widen_coef(vectors, block, left_of, right_of, j, lanes)
        for t in range(TILES):
            put(TILES * j + t, tiles[t])
        if j < CROSS and HALF[j // 2][1] != 0:
            moved = shift_tiles(tiles, HALF[j // 2][1], lanes)
            at = KINDS + SHIFT_SLOT[HALF[j // 2]] + j % 2
            for t in range(TILES):
                put(TILES * at + t, moved[t])


def own_kernel(vectors, block, strips, parities, wide, coefs):
    lanes = lane_ids()
    left_of, right_of = sides(strips, parities[1])
    for v in range(vectors):
        for a in range(2):
            tiles = widen_state(block, left_of, right_of, v, a, lanes)
            for t in range(TILES):
                wide[(2 * v + a) * TILES + t] = tiles[t]

    def put(at, tile):
        coefs[at] = tile

    spread(vectors, block, left_of, right_of, put)


def pair_tops(parities):
    last = 2 * ROWS
    top = pl.multiple_of(jnp.where(parities[0] == 0, last, 0), ROWS)
    return top, pl.multiple_of(last - top, ROWS)


def coefficient(coefs, dx, dy, a, t, top):
    source = a if (dx + dy) % 2 else 1 - a
    if (dx, dy) == (0, 0):
        at, row = CROSS, top
    elif (dx, dy) in HALF:
        at = KINDS + SHIFT_SLOT[(dx, dy)] + a if dy else 2 * HALF.index((dx, dy)) + a
        row = top
    else:
        at, row = 2 * HALF.index((-dx, -dy)) + source, top + dx
    return source, coefs[TILES * at + t, pl.ds(row, ROWS), :]


def apply_twice(field, coefs, a, group, width, top, lanes):
    sums = [[[None] * 5 for _ in range(TILES)] for _ in range(width)]
    for dx in range(-2, 3):
        rows = pl.ds(top + dx, ROWS)
        for t in range(TILES):
            values = [
                [field[((group * width + w) * 2 + b) * TILES + t, rows, :] for b in range(2)]
                for w in range(width)
            ]
            for dy in range(-2, 3):
                source, factor = coefficient(coefs, dx, dy, a, t, top)
                for w in range(width):
                    term = factor * values[w][source]
                    old = sums[w][t][dy + 2]
                    sums[w][t][dy + 2] = term if old is None else old + term
            if dx == 0:
                factor = coefs[TILES * (ONSITE + a) + t, pl.ds(top, ROWS), :]
                for w in range(width):
                    sums[w][t][2] = sums[w][t][2] + factor * values[w][a]
    results = []
    for w in range(width):
        total = [sums[w][t][2] for t in range(TILES)]
        for dy in (-2, -1, 1, 2):
            moved = shift_tiles([sums[w][t][dy + 2] for t in range(TILES)], -dy, lanes)
            total = [total[t] + moved[t] for t in range(TILES)]
        results.append(total)
    return results


def time_step(half, width, coefs, probe, terms, products, finish):
    vectors, start = half
    lanes = lane_ids()
    scale = [bessel(order, TIME_STEP) * (1.0 if order == 0 else 2.0) for order in range(APPLY + 1)]
    for order in range(1, APPLY + 1):
        low, high = 2 * order, REGION - 2 * order
        tops = list(range(low, high - ROWS + 1, ROWS))
        if tops[-1] != high - ROWS:
            tops.append(high - ROWS)
        for a in range(2):

            def body(group, carry):
                for top in tops:
                    images = apply_twice(terms[order - 1], coefs, a, group, width, top, lanes)
                    for w in range(width):
                        v = group * width + w
                        at = (2 * v + a) * TILES
                        rows = pl.ds(top, ROWS)
                        if order == 1:
                            new = [0.5 * images[w][t] for t in range(TILES)]
                        else:
                            new = [images[w][t] - terms[order - 2][at + t, rows, :] for t in range(TILES)]
                        if order < APPLY:
                            for t in range(TILES):
                                terms[order][at + t, rows, :] = new[t]
                            continue
                        even = []
                        odd = []
                        for t in range(TILES):
                            part = [terms[k][at + t, rows, :] for k in range(APPLY)]
                            even.append(scale[0] * part[0] - scale[2] * part[2] + scale[4] * new[t])
                            odd.append(roll(scale[1] * part[1] - scale[3] * part[3], 64))
                        real = even[0] + odd[1]
                        imag = even[1] - odd[0]
                        tail = even[2] + jnp.where(lanes < 64, odd[2], -odd[2])
                        own_real = roll(jnp.where(in_group(lanes, 0), tail, real), -EDGE)
                        own_imag = roll(jnp.where(in_group(lanes, 2), tail, imag), -EDGE - 64)
                        probe_real, probe_imag = probe[0, start + v, a], probe[1, start + v, a]
                        same = probe_real * own_real + probe_imag * own_imag
                        cross = probe_real * own_imag - probe_imag * own_real
                        if a == 1:
                            same = same + products[v]
                            cross = cross + products[vectors + v]
                        products[v] = same
                        products[vectors + v] = cross
                        finish(at, v, a, (real, imag, tail), (own_real, own_imag))
                return carry

            lax.fori_loop(0, vectors // width, body, 0)


def probe_row(half, whole, products):
    vectors, start = half
    sums = jnp.sum(jnp.sum(products[...], axis=1), axis=1, keepdims=True)
    rows = lax.broadcasted_iota(jnp.int32, (2 * vectors, LANES), 0)
    lanes = lax.broadcasted_iota(jnp.int32, (2 * vectors, LANES), 1)
    place = jnp.where(rows < vectors, start + rows, whole + start + rows - vectors)
    return jnp.sum(jnp.where(lanes == place, sums, 0.0), axis=0, keepdims=True)


def add_row(half, whole, step, rows, products):
    here = lax.broadcasted_iota(jnp.int32, (STEPS, LANES), 0) == step
    row = jnp.where(here, probe_row(half, whole, products), 0.0)
    return row if rows is None else rows[...] + row


def put_state(state):
    def finish(at, v, a, tiles, cells):
        for t in range(TILES):
            state[at + t] = tiles[t]

    return finish


def put_cells(state, start):
    def finish(at, v, a, tiles, cells):
        state[0, start + v, a] = cells[0]
        state[1, start + v, a] = cells[1]

    return finish


def first_kernel(
    half, whole, width, wide, coefs_own, block_one, block_two, strips_one, strips_two, probe, parities, *refs
):
    lanes = lane_ids()
    vectors, _ = half
    split = vectors < whole
    state, coefs = refs[:2]
    other, rows = refs[2:4] if split else (None, refs[2])
    t0, t1, t2, t3, products = refs[-5:]
    for at in range(2 * whole * TILES):
        into, place = (t0, at) if at < t0.shape[0] else (other, at - t0.shape[0])
        into[place, pl.ds(ROWS, ROWS), :] = wide[at]
    for at in range(COEF_ROWS * TILES):
        coefs[at, pl.ds(ROWS, ROWS), :] = coefs_own[at]
    for top, block, strips in zip(pair_tops(parities), (block_one, block_two), (strips_one, strips_two)):
        left_of, right_of = sides(strips, parities[1])
        for v in range(whole):
            for a in range(2):
                tiles = widen_state(block, left_of, right_of, v, a, lanes)
                for t in range(TILES):
                    into = t0 if v < vectors else other
                    into[(2 * (v % vectors) + a) * TILES + t, pl.ds(top, ROWS), :] = tiles[t]

        def put(at, tile, top=top):
            coefs[at, pl.ds(top, ROWS), :] = tile

        spread(whole, block, left_of, right_of, put)
    time_step(half, width, coefs, probe, (t0, t1, t2, t3), products, put_state(state))
    rows[...] = add_row(half, whole, 0, None, products)


def second_kernel(half, whole, width, t0, coefs, probe, rows_in, state, rows, t1, t2, t3, products):
    time_step(half, width, coefs, probe, (t0, t1, t2, t3), products, put_state(state))
    rows[...] = add_row(half, whole, 0, rows_in, products)


def gather_rows(first, own, one, two, parities):
    top_one, top_two = pair_tops(parities)
    for top, block in ((ROWS, own), (top_one, one), (top_two, two)):
        for at in range(first.shape[0]):
            first[at, pl.ds(top, ROWS), :] = block[at]


def middle_kernel(
    half, whole, width, step, own, one, two, coefs, probe, parities, rows_in, state, rows, t0, t1, t2, t3, products
):
    gather_rows(t0, own, one, two, parities)
    time_step(half, width, coefs, probe, (t0, t1, t2, t3), products, put_state(state))
    rows[...] = add_row(half, whole, step, rows_in, products)


def close_kernel(half, whole, width, own, one, two, coefs, probe, parities, rows_in, state, rows, t0, t1, t2, t3, products):
    gather_rows(t0, own, one, two, parities)
    time_step(half, width, coefs, probe, (t0, t1, t2, t3), products, put_cells(state, 0))
    rows[...] = add_row(half, whole, STEPS - 1, rows_in, products)


def last_kernel(half, whole, width, own, one, two, coefs, probe, parities, rows_in, *refs):
    state, copies, t0, t1, t2, t3, products = refs[-7:]
    gather_rows(t0, own, one, two, parities)
    for done in refs[:-7]:
        for part in range(2):
            for v in range(done.shape[1]):
                for a in range(2):
                    state[part, v, a] = done[part, v, a]
    time_step(half, width, coefs, probe, (t0, t1, t2, t3), products, put_cells(state, half[1]))
    rows = add_row(half, whole, STEPS - 1, rows_in, products)
    for copy in range(copies.shape[0]):
        copies[copy] = rows


def call(kernel, out_shapes, scratch=(), scalars=None, operands=0):
    in_memory = pl.BlockSpec(memory_space=pltpu.VMEM)
    specs = [pl.BlockSpec(memory_space=pltpu.SMEM) if i == scalars else in_memory for i in range(operands)]
    return pl.pallas_call(
        kernel,
        out_shape=[jax.ShapeDtypeStruct(shape, jnp.float32) for shape in out_shapes],
        in_specs=specs,
        scratch_shapes=[pltpu.VMEM(shape, jnp.float32) for shape in scratch],
        compiler_params=pltpu.CompilerParams(vmem_limit_bytes=VMEM_LIMIT),
    )


def pairings(axis):
    count = lax.axis_size(axis)
    one = [(i, i + 1 - 2 * (i % 2)) for i in range(count)]
    two = [(i, (i - 1 + 2 * (i % 2)) % count) for i in range(count)]
    return one, two


def swap(block, axis):
    one, two = pairings(axis)
    return lax.ppermute(block, axis, one), lax.ppermute(block, axis, two)


def sum_kernel(vectors, norm, rows, result):
    total = rows[0]
    for i in range(1, rows.shape[0]):
        total = total + rows[i]
    total = total * norm
    result[:, 0, :] = total[:, :vectors]
    result[:, 1, :] = total[:, vectors : 2 * vectors]


def per_device(start, probe, offsets, orbitals, index, kinds, hop_table, onsite_table):
    whole = start.shape[1]
    slots = offsets.shape[0]
    vectors = whole // PARTS
    width = 4
    groups = [(vectors, vectors * g) for g in range(PARTS)]
    cells = 2 * vectors * TILES
    edge_tiles = whole + (KINDS + 3) // 4
    tile = (ROWS, LANES)
    rows_shape = (STEPS, LANES)
    region = (cells, REGION, LANES)
    scratch = [region] * APPLY + [(2 * vectors, *tile)]
    parities = jnp.stack([lax.axis_index("gx") % 2, lax.axis_index("gy") % 2]).astype(jnp.int32)

    in_hbm = pl.BlockSpec(memory_space=pltpu.HBM)
    in_smem = pl.BlockSpec(memory_space=pltpu.SMEM)
    probe, block, pair_one, pair_two = pl.pallas_call(
        functools.partial(pack_kernel, whole, slots),
        out_shape=[
            jax.ShapeDtypeStruct(shape, jnp.float32)
            for shape in (probe.shape, (4 * whole + KINDS, *tile), (edge_tiles, *tile), (edge_tiles, *tile))
        ],
        in_specs=[in_hbm] * 6 + [in_smem] * 2,
        scratch_shapes=[
            pltpu.VMEM(start.shape, jnp.float32),
            pltpu.VMEM(offsets.shape, jnp.int32),
            pltpu.VMEM(index.shape, jnp.int32),
            pltpu.VMEM(kinds.shape, jnp.int32),
            pltpu.VMEM((1, hop_table.shape[0]), jnp.float32),
            pltpu.SemaphoreType.DMA((6,)),
        ],
        compiler_params=pltpu.CompilerParams(vmem_limit_bytes=VMEM_LIMIT),
    )(start, probe, offsets, index, kinds, hop_table[None], onsite_table, parities)
    one, two = pairings("gy")
    strips = jnp.concatenate([lax.ppermute(pair_one, "gy", one), lax.ppermute(pair_two, "gy", two)])
    block_one, block_two = swap(block, "gx")
    strips_one, strips_two = swap(strips, "gx")
    wide, coefs_own = call(
        functools.partial(own_kernel, whole),
        [(2 * whole * TILES, *tile), (COEF_ROWS * TILES, *tile)],
        scalars=2,
        operands=3,
    )(block, strips, parities)

    state_shape = (cells, *tile)
    others = [region] * (PARTS - 1)
    first, coefs, *others, rows = call(
        functools.partial(first_kernel, groups[0], whole, width),
        [state_shape, (COEF_ROWS * TILES, REGION, LANES), *others, rows_shape],
        scratch,
        scalars=7,
        operands=8,
    )(wide, coefs_own, block_one, block_two, strips_one, strips_two, probe, parities)
    states = [first]
    for g, other in enumerate(others, 1):
        state, rows = call(
            functools.partial(second_kernel, groups[g], whole, width), [state_shape, rows_shape], scratch[1:], operands=4
        )(other, coefs, probe, rows)
        states.append(state)
    for step in range(1, STEPS - 1):
        for g in range(PARTS):
            states[g], rows = call(
                functools.partial(middle_kernel, groups[g], whole, width, step),
                [state_shape, rows_shape],
                scratch,
                scalars=5,
                operands=7,
            )(states[g], *swap(states[g], "gx"), coefs, probe, parities, rows)
    done = []
    for g in range(PARTS - 1):
        state, rows = call(
            functools.partial(close_kernel, groups[g], whole, width),
            [(2, vectors, *start.shape[2:]), rows_shape],
            scratch,
            scalars=5,
            operands=7,
        )(states[g], *swap(states[g], "gx"), coefs, probe, parities, rows)
        done.append(state)
    final, copies = call(
        functools.partial(last_kernel, groups[-1], whole, width),
        [start.shape, (lax.axis_size("gx"), *rows_shape)],
        scratch,
        scalars=5,
        operands=7 + len(done),
    )(states[-1], *swap(states[-1], "gx"), coefs, probe, parities, rows, *done)
    part = jnp.sum(lax.all_to_all(copies, "gx", 0, 0), axis=0)
    count = lax.axis_size("gy")
    copies = jnp.broadcast_to(part[None], (count, *rows_shape))
    total_cells = start.shape[3] * start.shape[4] * lax.axis_size("gx") * count
    norm = 1.0 / math.sqrt(2.0 * 2 * total_cells)
    (intersections,) = call(functools.partial(sum_kernel, whole, norm), [(STEPS, 2, whole)], operands=1)(
        lax.all_to_all(copies, "gy", 0, 0)
    )
    return final, intersections


def solution(mesh):
    return jax.shard_map(
        per_device,
        mesh=mesh,
        in_specs=(
            P(None, None, None, "gx", "gy"),
            P(None, None, None, "gx", "gy"),
            P(None, None, "gx", "gy"),
            P(None, None, "gx", "gy"),
            P(None, None, "gx", "gy"),
            P(None, "gx", "gy"),
            P(),
            P(),
        ),
        out_specs=(P(None, None, None, "gx", "gy"), P()),
        check_vma=False,
    )
```

time: 112 us -> 96.5 us (0.86)
  waiting for transfers between devices: 19.8 us -> 4.7 us
  blocking collectives: 31.2 us -> 26.1 us
  starting transfers between devices: 25.1 us -> 28.9 us
  Pallas kernels: 28.8 us -> 30 us
    ppermute x10 -> x18, waiting for transfers between devices: 19.8 us -> 4.7 us  [the longest x1 2.36 us: per_device(): lax.ppermute(pair_two, 'gy', two)]
    all_to_all x2, blocking collectives: 31.2 us -> 26.1 us  [the longest x1 15.7 us: per_device(): lax.all_to_all(copies, 'gy', 0, 0)]
    ppermute x10 -> x18, starting transfers between devices: 25.1 us -> 28.9 us  [the longest x16 18.3 us: swap(): return (lax.ppermute(block, axis, one), lax.ppermute(block, axis, two))]
    unnamed x10 -> x15, local copies, waits for them, and re-layouts: 4.28 us -> 5.59 us
    pallas_call x6 -> x11, Pallas kernels: 28.8 us -> 30 us  [the longest x4 10.3 us: per_device(): call(functools.partial(middle_kernel, groups[g], whole, width, step), [st...]
  transfers between devices with their start and end apart: 10 -> 18, of which waited for: 8 -> 2; matrix products, arithmetic and copies ran while one was open for 0% -> 0% of each run, Pallas kernels for 0% -> 17%
where the time goes in v2:
time: 96.5 us; the launch traced here: 96.2 us
  Pallas kernels  30 us (31%)
  starting transfers between devices  28.9 us (30%)
  blocking collectives  26.1 us (27%)
  local copies, waits for them, and re-layouts  5.61 us (6%)
  waiting for transfers between devices  4.7 us (5%)
    ppermute x16, starting transfers between devices, swap(): return (lax.ppermute(block, axis, one), lax.ppermute(block, axis, two))  18.3 us
    all_to_all x1, blocking collectives, per_device(): lax.all_to_all(copies, 'gy', 0, 0)  15.7 us
    all_to_all x1, blocking collectives, per_device(): part = jnp.sum(lax.all_to_all(copies, 'gx', 0, 0), axis=0)  10.4 us
    pallas_call x4, Pallas kernels, per_device(): call(functools.partial(middle_kernel, groups[g], whole, width, step), [st...  10.3 us
    pallas_call x1, Pallas kernels, per_device(): call(functools.partial(first_kernel, groups[0], whole, width), [state_sha...  8.17 us
    ppermute x1, starting transfers between devices, per_device(): lax.ppermute(pair_two, 'gy', two)  7.02 us
    unnamed x15, local copies, waits for them, and re-layouts  5.59 us
    ppermute x1, starting transfers between devices, per_device(): lax.ppermute(pair_one, 'gy', one)  3.66 us
  transfers between devices with their start and end apart: 18, of which 2 were waited for; matrix products, arithmetic and copies ran while one was open for 0% of the time, Pallas kernels for 17%

profile of v2, /device:TPU:1, one launch (start us, length us, event | category | flops | bytes accessed | tf_op | source)
XLA Modules:
  0.0 96.2 jit_solution(14577303831400582389)
XLA Ops:
  6.3 1.6 %shard_map.86 = (f32[2,8,2,8,128]{4,3,2,1,0:T(8,128)S(1)}, f32[59,8,128]{2,1,0:T(8,128)S(1)}, f32[15,8,128]{2,1,0:T(8,128)S(1)}, f32[15,8,128]{2,1,0:T(8,128)S(1)}) custom-call(f32[2,8,2,8,128]{4,3,2,1,0:T(8,128)S(1)} %copy-done, f32[2,8,2,8,128]{4,3,2,1,0:T(8,128)S(1)} %copy-done.1, s32[10,2,8,128]{3,2,1,0:T(8,128)S(1)} %copy-done.2, ...), custom_call_target="tpu_custom_call" | custom-call | tf_op jit(solution)/shard_map/pallas_call | solution.py:444
  7.9 3.7 %collective-permute-start = (f32[15,8,128]{2,1,0:T(8,128)S(1)}, f32[15,8,128]{2,1,0:T(8,128)S(1)}, u32[]{:S(2)}, u32[]{:S(2)}) collective-permute-start(f32[15,8,128]{2,1,0:T(8,128)S(1)} %get-tuple-element.27), channel_id=1, source_target_pairs={{0,1},{1,0},{2,3},{3,2},{4,5},{5,4},{6,7},{7,6},{8,9},{9,8},{10,11... | collective-permute-start | bytes 184328 | tf_op jit(solution)/shard_map/ppermute | solution.py:462
  11.6 1.2 %collective-permute-start.3 = (f32[59,8,128]{2,1,0:T(8,128)S(1)}, f32[59,8,128]{2,1,0:T(8,128)S(1)}, u32[]{:S(2)}, u32[]{:S(2)}) collective-permute-start(f32[59,8,128]{2,1,0:T(8,128)S(1)} %get-tuple-element.26.block), channel_id=1, source_target_pairs={{0,240},{16,32},{32,16},{48,64},{64,48},{80,96},{96,80},{112,128},... | collective-permute-start | bytes 725000 | tf_op jit(solution)/shard_map/ppermute | solution.py:416
  12.7 2.0 %collective-permute-start.2 = (f32[59,8,128]{2,1,0:T(8,128)S(1)}, f32[59,8,128]{2,1,0:T(8,128)S(1)}, u32[]{:S(2)}, u32[]{:S(2)}) collective-permute-start(f32[59,8,128]{2,1,0:T(8,128)S(1)} %get-tuple-element.26.block), channel_id=1, source_target_pairs={{0,16},{16,0},{32,48},{48,32},{64,80},{80,64},{96,112},{112,96},{1... | collective-permute-start | bytes 725000 | tf_op jit(solution)/shard_map/ppermute | solution.py:416
  14.7 7.0 %collective-permute-start.1 = (f32[15,8,128]{2,1,0:T(8,128)S(1)}, f32[15,8,128]{2,1,0:T(8,128)S(1)}, u32[]{:S(2)}, u32[]{:S(2)}) collective-permute-start(f32[15,8,128]{2,1,0:T(8,128)S(1)} %get-tuple-element.28), channel_id=1, source_target_pairs={{0,15},{1,2},{2,1},{3,4},{4,3},{5,6},{6,5},{7,8},{8,7},{9,10},{10,... | collective-permute-start | bytes 184328 | tf_op jit(solution)/shard_map/ppermute | solution.py:462
  21.8 2.4 %collective-permute-done.1 = f32[15,8,128]{2,1,0:T(8,128)S(1)} collective-permute-done((f32[15,8,128]{2,1,0:T(8,128)S(1)}, f32[15,8,128]{2,1,0:T(8,128)S(1)}, u32[]{:S(2)}, u32[]{:S(2)}) %collective-permute-start.1) | collective-permute-done | bytes 61472 | tf_op jit(solution)/shard_map/ppermute | solution.py:462
  24.8 1.6 %shard_map.87 = (f32[48,8,128]{2,1,0:T(8,128)S(1)}, f32[141,8,128]{2,1,0:T(8,128)S(1)}) custom-call(f32[59,8,128]{2,1,0:T(8,128)S(1)} %get-tuple-element.26.block, f32[30,8,128]{2,1,0:T(8,128)S(1)} %constant_dynamic-update-slice_fusion.strips, s32[2]{0:T(128)S(1)} %pad_add_fusion.parities), custom_call_target="tpu_custom_call" | custom-call | tf_op jit(solution)/shard_map/pallas_call | solution.py:465
  26.4 2.3 %collective-permute-done.5.strips_two = f32[30,8,128]{2,1,0:T(8,128)S(1)} collective-permute-done((f32[30,8,128]{2,1,0:T(8,128)S(1)}, f32[30,8,128]{2,1,0:T(8,128)S(1)}, u32[]{:S(2)}, u32[]{:S(2)}) %collective-permute-start.5) | collective-permute-done | bytes 122912 | tf_op jit(solution)/shard_map/ppermute | solution.py:416
  28.7 8.2 %shard_map.88 = (f32[24,8,128]{2,1,0:T(8,128)S(1)}, f32[141,24,128]{2,1,0:T(8,128)S(1)}, f32[24,24,128]{2,1,0:T(8,128)S(1)}, f32[4,128]{1,0:T(4,128)S(1)}) custom-call(f32[48,8,128]{2,1,0:T(8,128)S(1)} %get-tuple-element.29.wide, f32[141,8,128]{2,1,0:T(8,128)S(1)} %get-tuple-element.30.coefs_own, f32[59,8,128]{2,1,0:T(8,128)S(1)} %collective-permute-done.2.block_one, ...), custom_call_target="tpu_custom_call" | custom-call | tf_op jit(solution)/shard_map/pallas_call | solution.py:474
  37.2 2.7 %collective-permute-start.8 = (f32[24,8,128]{2,1,0:T(8,128)S(1)}, f32[24,8,128]{2,1,0:T(8,128)S(1)}, u32[]{:S(2)}, u32[]{:S(2)}) collective-permute-start(f32[24,8,128]{2,1,0:T(8,128)S(1)} %get-tuple-element.36.own), channel_id=1, source_target_pairs={{0,16},{16,0},{32,48},{48,32},{64,80},{80,64},{96,112},{112,96},{1... | collective-permute-start | bytes 294920 | tf_op jit(solution)/shard_map/ppermute | solution.py:416
  39.9 2.0 %shard_map.89 = (f32[24,8,128]{2,1,0:T(8,128)S(1)}, f32[4,128]{1,0:T(4,128)S(1)}) custom-call(f32[24,24,128]{2,1,0:T(8,128)S(1)} %get-tuple-element.32.t0, f32[141,24,128]{2,1,0:T(8,128)S(1)} %get-tuple-element.33.coefs, f32[2,8,2,8,128]{4,3,2,1,0:T(8,128)S(1)} %get-tuple-element.31.probe, f32[4,128]{1,0:T(4,128)S(1)} %get-tuple-element.34.rows_in), custom_call_target="tpu_custom_call" | custom-call | tf_op jit(solution)/shard_map/pallas_call | solution.py:483
  41.9 3.3 %collective-permute-start.6 = (f32[24,8,128]{2,1,0:T(8,128)S(1)}, f32[24,8,128]{2,1,0:T(8,128)S(1)}, u32[]{:S(2)}, u32[]{:S(2)}) collective-permute-start(f32[24,8,128]{2,1,0:T(8,128)S(1)} %get-tuple-element.35.own), channel_id=1, source_target_pairs={{0,16},{16,0},{32,48},{48,32},{64,80},{80,64},{96,112},{112,96},{1... | collective-permute-start | bytes 294920 | tf_op jit(solution)/shard_map/ppermute | solution.py:416
  45.2 2.6 %shard_map.90 = (f32[24,8,128]{2,1,0:T(8,128)S(1)}, f32[4,128]{1,0:T(4,128)S(1)}) custom-call(f32[24,8,128]{2,1,0:T(8,128)S(1)} %get-tuple-element.36.own, f32[24,8,128]{2,1,0:T(8,128)S(1)} %collective-permute-done.8.one, f32[24,8,128]{2,1,0:T(8,128)S(1)} %collective-permute-done.9.two, f32[141,24,128]{2,1,0:T(8,128)S(1)} %get-tuple-element.33.coefs, ...), custom_call_target="tpu_custom_call" | custom-call | tf_op jit(solution)/shard_map/pallas_call | solution.py:489
  48.6 2.6 %shard_map.91 = (f32[24,8,128]{2,1,0:T(8,128)S(1)}, f32[4,128]{1,0:T(4,128)S(1)}) custom-call(f32[24,8,128]{2,1,0:T(8,128)S(1)} %get-tuple-element.35.own, f32[24,8,128]{2,1,0:T(8,128)S(1)} %collective-permute-done.6.one, f32[24,8,128]{2,1,0:T(8,128)S(1)} %collective-permute-done.7.two, f32[141,24,128]{2,1,0:T(8,128)S(1)} %get-tuple-element.33.coefs, ...), custom_call_target="tpu_custom_call" | custom-call | tf_op jit(solution)/shard_map/pallas_call | solution.py:489
  51.2 1.0 %collective-permute-start.11 = (f32[24,8,128]{2,1,0:T(8,128)S(1)}, f32[24,8,128]{2,1,0:T(8,128)S(1)}, u32[]{:S(2)}, u32[]{:S(2)}) collective-permute-start(f32[24,8,128]{2,1,0:T(8,128)S(1)} %get-tuple-element.39.own), channel_id=1, source_target_pairs={{0,240},{16,32},{32,16},{48,64},{64,48},{80,96},{96,80},{112,128},... | collective-permute-start | bytes 294920 | tf_op jit(solution)/shard_map/ppermute | solution.py:416
  52.2 2.4 %collective-permute-start.10 = (f32[24,8,128]{2,1,0:T(8,128)S(1)}, f32[24,8,128]{2,1,0:T(8,128)S(1)}, u32[]{:S(2)}, u32[]{:S(2)}) collective-permute-start(f32[24,8,128]{2,1,0:T(8,128)S(1)} %get-tuple-element.39.own), channel_id=1, source_target_pairs={{0,16},{16,0},{32,48},{48,32},{64,80},{80,64},{96,112},{112,96},{1... | collective-permute-start | bytes 294920 | tf_op jit(solution)/shard_map/ppermute | solution.py:416
  54.5 2.6 %shard_map.92 = (f32[24,8,128]{2,1,0:T(8,128)S(1)}, f32[4,128]{1,0:T(4,128)S(1)}) custom-call(f32[24,8,128]{2,1,0:T(8,128)S(1)} %get-tuple-element.40.own, f32[24,8,128]{2,1,0:T(8,128)S(1)} %collective-permute-done.12.one, f32[24,8,128]{2,1,0:T(8,128)S(1)} %collective-permute-done.13.two, f32[141,24,128]{2,1,0:T(8,128)S(1)} %get-tuple-element.33.coefs, ...), custom_call_target="tpu_custom_call" | custom-call | tf_op jit(solution)/shard_map/pallas_call | solution.py:489
  58.0 2.6 %shard_map.93 = (f32[24,8,128]{2,1,0:T(8,128)S(1)}, f32[4,128]{1,0:T(4,128)S(1)}) custom-call(f32[24,8,128]{2,1,0:T(8,128)S(1)} %get-tuple-element.39.own, f32[24,8,128]{2,1,0:T(8,128)S(1)} %collective-permute-done.10.one, f32[24,8,128]{2,1,0:T(8,128)S(1)} %collective-permute-done.11.two, f32[141,24,128]{2,1,0:T(8,128)S(1)} %get-tuple-element.33.coefs, ...), custom_call_target="tpu_custom_call" | custom-call | tf_op jit(solution)/shard_map/pallas_call | solution.py:489
  60.6 0.9 collective-permute-start.15
  61.5 2.1 %collective-permute-start.14 = (f32[24,8,128]{2,1,0:T(8,128)S(1)}, f32[24,8,128]{2,1,0:T(8,128)S(1)}, u32[]{:S(2)}, u32[]{:S(2)}) collective-permute-start(f32[24,8,128]{2,1,0:T(8,128)S(1)} %get-tuple-element.43.own), channel_id=1, source_target_pairs={{0,16},{16,0},{32,48},{48,32},{64,80},{80,64},{96,112},{112,96},{1... | collective-permute-start | bytes 294920 | tf_op jit(solution)/shard_map/ppermute | solution.py:416
  63.6 2.6 %shard_map.94 = (f32[2,4,2,8,128]{4,3,2,1,0:T(8,128)S(1)}, f32[4,128]{1,0:T(4,128)S(1)}) custom-call(f32[24,8,128]{2,1,0:T(8,128)S(1)} %get-tuple-element.44.own, f32[24,8,128]{2,1,0:T(8,128)S(1)} %collective-permute-done.16.one, f32[24,8,128]{2,1,0:T(8,128)S(1)} %collective-permute-done.17.two, f32[141,24,128]{2,1,0:T(8,128)S(1)} %get-tuple-element.33.coefs, ...), custom_call_target="tpu_custom_call" | custom-call | tf_op jit(solution)/shard_map/pallas_call | solution.py:498
  66.2 3.1 %shard_map.95 = (f32[2,8,2,8,128]{4,3,2,1,0:T(8,128)}, f32[16,4,128]{2,1,0:T(4,128)S(1)}) custom-call(f32[24,8,128]{2,1,0:T(8,128)S(1)} %get-tuple-element.43.own, f32[24,8,128]{2,1,0:T(8,128)S(1)} %collective-permute-done.14.one, f32[24,8,128]{2,1,0:T(8,128)S(1)} %collective-permute-done.15.two, f32[141,24,128]{2,1,0:T(8,128)S(1)} %get-tuple-element.33.coefs, ...), custom_call_target="tpu_custom_call" | custom-call | tf_op jit(solution)/shard_map/pallas_call | solution.py:506
  69.3 10.4 %all_to_all.10 = f32[16,4,128]{2,1,0:T(4,128)S(1)} all-to-all(f32[16,4,128]{2,1,0:T(4,128)S(1)} %get-tuple-element.49), channel_id=1, replica_groups=mesh['gx'=16,'gy'=16] {'gx'}, dimensions={0} | all-to-all | bytes 65536 | tf_op jit(solution)/shard_map/all_to_all | solution.py:513
  79.8 15.7 %all_to_all.11.rows = f32[16,4,128]{2,1,0:T(4,128)S(1)} all-to-all(f32[16,4,128]{2,1,0:T(4,128)S(1)} %broadcast_in_dim.10), channel_id=1, replica_groups=mesh['gx'=16,'gy'=16] {'gy'}, dimensions={0} | all-to-all | bytes 65536 | tf_op jit(solution)/shard_map/all_to_all | solution.py:519
  (44 shorter events, 9.2 us)
Async XLA Ops:
  0.7 0.9 copy-start
  1.6 0.9 copy-start.1
  2.5 0.9 copy-start.2
  3.4 0.9 copy-start.3
  4.3 0.7 copy-start.4
  5.0 0.7 copy-start.5
  7.9 13.8 %collective-permute-start = (f32[15,8,128]{2,1,0:T(8,128)S(1)}, f32[15,8,128]{2,1,0:T(8,128)S(1)}, u32[]{:S(2)}, u32[]{:S(2)}) collective-permute-start(f32[15,8,128]{2,1,0:T(8,128)S(1)} %get-tuple-element.27), channel_id=1, source_target_pairs={{0,1},{1,0},{2,3},{3,2},{4,5},{5,4},{6,7},{7,6},{8,9},{9,8},{10,11... | collective-permute-start | bytes 184328 | tf_op jit(solution)/shard_map/ppermute | solution.py:462
  11.6 17.1 %collective-permute-start.3 = (f32[59,8,128]{2,1,0:T(8,128)S(1)}, f32[59,8,128]{2,1,0:T(8,128)S(1)}, u32[]{:S(2)}, u32[]{:S(2)}) collective-permute-start(f32[59,8,128]{2,1,0:T(8,128)S(1)} %get-tuple-element.26.block), channel_id=1, source_target_pairs={{0,240},{16,32},{32,16},{48,64},{64,48},{80,96},{96,80},{112,128},... | collective-permute-start | bytes 725000 | tf_op jit(solution)/shard_map/ppermute | solution.py:416
  12.7 16.0 %collective-permute-start.2 = (f32[59,8,128]{2,1,0:T(8,128)S(1)}, f32[59,8,128]{2,1,0:T(8,128)S(1)}, u32[]{:S(2)}, u32[]{:S(2)}) collective-permute-start(f32[59,8,128]{2,1,0:T(8,128)S(1)} %get-tuple-element.26.block), channel_id=1, source_target_pairs={{0,16},{16,0},{32,48},{48,32},{64,80},{80,64},{96,112},{112,96},{1... | collective-permute-start | bytes 725000 | tf_op jit(solution)/shard_map/ppermute | solution.py:416
  14.7 9.4 %collective-permute-start.1 = (f32[15,8,128]{2,1,0:T(8,128)S(1)}, f32[15,8,128]{2,1,0:T(8,128)S(1)}, u32[]{:S(2)}, u32[]{:S(2)}) collective-permute-start(f32[15,8,128]{2,1,0:T(8,128)S(1)} %get-tuple-element.28), channel_id=1, source_target_pairs={{0,15},{1,2},{2,1},{3,4},{4,3},{5,6},{6,5},{7,8},{8,7},{9,10},{10,... | collective-permute-start | bytes 184328 | tf_op jit(solution)/shard_map/ppermute | solution.py:462
  24.1 4.6 %collective-permute-start.5 = (f32[30,8,128]{2,1,0:T(8,128)S(1)}, f32[30,8,128]{2,1,0:T(8,128)S(1)}, u32[]{:S(2)}, u32[]{:S(2)}) collective-permute-start(f32[30,8,128]{2,1,0:T(8,128)S(1)} %constant_dynamic-update-slice_fusion.strips), channel_id=1, source_target_pairs={{0,240},{16,32},{32,16},{48,64},{64,48},{80,96},{96,80},{112,128},... | collective-permute-start | bytes 368648 | tf_op jit(solution)/shard_map/ppermute | solution.py:416
  24.1 4.5 %collective-permute-start.4 = (f32[30,8,128]{2,1,0:T(8,128)S(1)}, f32[30,8,128]{2,1,0:T(8,128)S(1)}, u32[]{:S(2)}, u32[]{:S(2)}) collective-permute-start(f32[30,8,128]{2,1,0:T(8,128)S(1)} %constant_dynamic-update-slice_fusion.strips), channel_id=1, source_target_pairs={{0,16},{16,0},{32,48},{48,32},{64,80},{80,64},{96,112},{112,96},{1... | collective-permute-start | bytes 368648 | tf_op jit(solution)/shard_map/ppermute | solution.py:416
  36.9 8.4 %collective-permute-start.9 = (f32[24,8,128]{2,1,0:T(8,128)S(1)}, f32[24,8,128]{2,1,0:T(8,128)S(1)}, u32[]{:S(2)}, u32[]{:S(2)}) collective-permute-start(f32[24,8,128]{2,1,0:T(8,128)S(1)} %get-tuple-element.36.own), channel_id=1, source_target_pairs={{0,240},{16,32},{32,16},{48,64},{64,48},{80,96},{96,80},{112,128},... | collective-permute-start | bytes 294920 | tf_op jit(solution)/shard_map/ppermute | solution.py:416
  37.2 8.0 %collective-permute-start.8 = (f32[24,8,128]{2,1,0:T(8,128)S(1)}, f32[24,8,128]{2,1,0:T(8,128)S(1)}, u32[]{:S(2)}, u32[]{:S(2)}) collective-permute-start(f32[24,8,128]{2,1,0:T(8,128)S(1)} %get-tuple-element.36.own), channel_id=1, source_target_pairs={{0,16},{16,0},{32,48},{48,32},{64,80},{80,64},{96,112},{112,96},{1... | collective-permute-start | bytes 294920 | tf_op jit(solution)/shard_map/ppermute | solution.py:416
  41.9 6.7 %collective-permute-start.7 = (f32[24,8,128]{2,1,0:T(8,128)S(1)}, f32[24,8,128]{2,1,0:T(8,128)S(1)}, u32[]{:S(2)}, u32[]{:S(2)}) collective-permute-start(f32[24,8,128]{2,1,0:T(8,128)S(1)} %get-tuple-element.35.own), channel_id=1, source_target_pairs={{0,240},{16,32},{32,16},{48,64},{64,48},{80,96},{96,80},{112,128},... | collective-permute-start | bytes 294920 | tf_op jit(solution)/shard_map/ppermute | solution.py:416
  41.9 6.7 %collective-permute-start.6 = (f32[24,8,128]{2,1,0:T(8,128)S(1)}, f32[24,8,128]{2,1,0:T(8,128)S(1)}, u32[]{:S(2)}, u32[]{:S(2)}) collective-permute-start(f32[24,8,128]{2,1,0:T(8,128)S(1)} %get-tuple-element.35.own), channel_id=1, source_target_pairs={{0,16},{16,0},{32,48},{48,32},{64,80},{80,64},{96,112},{112,96},{1... | collective-permute-start | bytes 294920 | tf_op jit(solution)/shard_map/ppermute | solution.py:416
  47.8 6.7 %collective-permute-start.13 = (f32[24,8,128]{2,1,0:T(8,128)S(1)}, f32[24,8,128]{2,1,0:T(8,128)S(1)}, u32[]{:S(2)}, u32[]{:S(2)}) collective-permute-start(f32[24,8,128]{2,1,0:T(8,128)S(1)} %get-tuple-element.40.own), channel_id=1, source_target_pairs={{0,240},{16,32},{32,16},{48,64},{64,48},{80,96},{96,80},{112,128},... | collective-permute-start | bytes 294920 | tf_op jit(solution)/shard_map/ppermute | solution.py:416
  47.8 6.7 %collective-permute-start.12 = (f32[24,8,128]{2,1,0:T(8,128)S(1)}, f32[24,8,128]{2,1,0:T(8,128)S(1)}, u32[]{:S(2)}, u32[]{:S(2)}) collective-permute-start(f32[24,8,128]{2,1,0:T(8,128)S(1)} %get-tuple-element.40.own), channel_id=1, source_target_pairs={{0,16},{16,0},{32,48},{48,32},{64,80},{80,64},{96,112},{112,96},{1... | collective-permute-start | bytes 294920 | tf_op jit(solution)/shard_map/ppermute | solution.py:416
  51.2 6.8 %collective-permute-start.11 = (f32[24,8,128]{2,1,0:T(8,128)S(1)}, f32[24,8,128]{2,1,0:T(8,128)S(1)}, u32[]{:S(2)}, u32[]{:S(2)}) collective-permute-start(f32[24,8,128]{2,1,0:T(8,128)S(1)} %get-tuple-element.39.own), channel_id=1, source_target_pairs={{0,240},{16,32},{32,16},{48,64},{64,48},{80,96},{96,80},{112,128},... | collective-permute-start | bytes 294920 | tf_op jit(solution)/shard_map/ppermute | solution.py:416
  52.2 5.8 %collective-permute-start.10 = (f32[24,8,128]{2,1,0:T(8,128)S(1)}, f32[24,8,128]{2,1,0:T(8,128)S(1)}, u32[]{:S(2)}, u32[]{:S(2)}) collective-permute-start(f32[24,8,128]{2,1,0:T(8,128)S(1)} %get-tuple-element.39.own), channel_id=1, source_target_pairs={{0,16},{16,0},{32,48},{48,32},{64,80},{80,64},{96,112},{112,96},{1... | collective-permute-start | bytes 294920 | tf_op jit(solution)/shard_map/ppermute | solution.py:416
  57.1 6.5 %collective-permute-start.17 = (f32[24,8,128]{2,1,0:T(8,128)S(1)}, f32[24,8,128]{2,1,0:T(8,128)S(1)}, u32[]{:S(2)}, u32[]{:S(2)}) collective-permute-start(f32[24,8,128]{2,1,0:T(8,128)S(1)} %get-tuple-element.44.own), channel_id=1, source_target_pairs={{0,240},{16,32},{32,16},{48,64},{64,48},{80,96},{96,80},{112,128},... | collective-permute-start | bytes 294920 | tf_op jit(solution)/shard_map/ppermute | solution.py:416
  57.1 6.5 %collective-permute-start.16 = (f32[24,8,128]{2,1,0:T(8,128)S(1)}, f32[24,8,128]{2,1,0:T(8,128)S(1)}, u32[]{:S(2)}, u32[]{:S(2)}) collective-permute-start(f32[24,8,128]{2,1,0:T(8,128)S(1)} %get-tuple-element.44.own), channel_id=1, source_target_pairs={{0,16},{16,0},{32,48},{48,32},{64,80},{80,64},{96,112},{112,96},{1... | collective-permute-start | bytes 294920 | tf_op jit(solution)/shard_map/ppermute | solution.py:416
  60.6 5.6 %collective-permute-start.15 = (f32[24,8,128]{2,1,0:T(8,128)S(1)}, f32[24,8,128]{2,1,0:T(8,128)S(1)}, u32[]{:S(2)}, u32[]{:S(2)}) collective-permute-start(f32[24,8,128]{2,1,0:T(8,128)S(1)} %get-tuple-element.43.own), channel_id=1, source_target_pairs={{0,240},{16,32},{32,16},{48,64},{64,48},{80,96},{96,80},{112,128},... | collective-permute-start | bytes 294920 | tf_op jit(solution)/shard_map/ppermute | solution.py:416
  61.5 4.7 %collective-permute-start.14 = (f32[24,8,128]{2,1,0:T(8,128)S(1)}, f32[24,8,128]{2,1,0:T(8,128)S(1)}, u32[]{:S(2)}, u32[]{:S(2)}) collective-permute-start(f32[24,8,128]{2,1,0:T(8,128)S(1)} %get-tuple-element.43.own), channel_id=1, source_target_pairs={{0,16},{16,0},{32,48},{48,32},{64,80},{80,64},{96,112},{112,96},{1... | collective-permute-start | bytes 294920 | tf_op jit(solution)/shard_map/ppermute | solution.py:416
  (1 other events, 0.7 us)

commit v3 on v2

--- a/solution.py
+++ b/solution.py
@@ -60,6 +60,28 @@
     return even, odd, tail
 
 
+def in_batches(size, jobs):
+    jobs = list(jobs)
+    for start in range(0, len(jobs), size):
+        triples = [triple for job in jobs[start : start + size] for triple in job()]
+        for store, place, value in triples:
+            store(place, value)
+
+
+def into(ref, rows=None):
+    def store(place, value):
+        if rows is None:
+            ref[place] = value
+        else:
+            ref[place, pl.ds(rows, ROWS), :] = value
+
+    return store
+
+
+def copies(store, read, count, shift=0):
+    return [lambda at=at: [(store, at, read(at + shift))] for at in range(count)]
+
+
 def in_group(lanes, group):
     return (lanes >= EDGE * group) & (lanes < EDGE * (group + 1))
 
@@ -78,7 +100,7 @@
 
 def pack_kernel(
     vectors, slots, start, probe, offsets, index, kinds, hop_table, onsite_table, parities,
-    probe_copy, block, pair_one, pair_two, state, offsets_here, index_here, kinds_here, table_here, semaphores,
+    probe_copy, state, coef, pair_one, pair_two, offsets_here, index_here, kinds_here, table_here, semaphores,
 ):
     fetch(
         [
@@ -88,25 +110,27 @@
         semaphores,
     )
     lanes = lane_ids()
-    even = jnp.full((ROWS, LANES), parities[1], jnp.int32) == 0
-    coefs_at = 4 * vectors
+    even = is_even(parities[1])
 
     def send(at, to_right, to_left):
-        pair_one[at] = jnp.where(even, to_right, to_left)
-        pair_two[at] = jnp.where(even, to_left, to_right)
+        return [
+            (into(pair_one), at, jnp.where(even, to_right, to_left)),
+            (into(pair_two), at, jnp.where(even, to_left, to_right)),
+        ]
 
     low = lanes < 64
     first = in_group(lanes, 0) | in_group(lanes, 2)
-    for v in range(vectors):
+
+    def strip(v):
         strips = []
         for a in range(2):
-            block[4 * v + 2 * a] = state[0, v, a]
-            block[4 * v + 2 * a + 1] = state[1, v, a]
             real, imag = turned(state[0, v, a], state[1, v, a])
             strips.append(jnp.where(low, real, imag))
         to_right = jnp.where(first, strips[0], roll(strips[1], EDGE))
         to_left = jnp.where(first, roll(strips[1], -EDGE), strips[0])
-        send(v, to_right, to_left)
+        return send(v, to_right, to_left)
+
+    in_batches(vectors, [functools.partial(strip, v) for v in range(vectors)])
     entries = table_here[...]
     spare = LANES - entries.shape[1]
     table = jnp.broadcast_to(jnp.concatenate([entries, jnp.zeros((1, spare), jnp.float32)], axis=1), (ROWS, LANES))
@@ -126,23 +150,34 @@
         right = left = None
         for group in range(min(4, KINDS - start_at)):
             double = 2.0 * arrays[start_at + group]
-            block[coefs_at + start_at + group] = double
+            coef[start_at + group] = double
             base = roll(double, EDGE)
             from_tail = roll(base, EDGE * group)
             from_head = roll(base, EDGE * (group - 1))
             right = from_tail if right is None else jnp.where(in_group(lanes, group), from_tail, right)
             left = from_head if left is None else jnp.where(in_group(lanes, group), from_head, left)
-        send(vectors + start_at // 4, right, left)
-
-
-def sides(strips, parity):
+        for store, place, value in send(vectors + start_at // 4, right, left):
+            store(place, value)
+
+
+def is_even(parity):
+    return jnp.full((ROWS, LANES), parity, jnp.int32) == 0
+
+
+def ordered(one, two, even):
+    return (
+        lambda at: jnp.where(even, two[at], one[at]),
+        lambda at: jnp.where(even, one[at], two[at]),
+    )
+
+
+def halves(strips):
     edge = strips.shape[0] // 2
-    left_at = jnp.where(parity == 0, edge, 0)
-    return lambda at: strips[left_at + at], lambda at: strips[edge - left_at + at]
-
-
-def widen_state(block, left_of, right_of, v, a, lanes):
-    real, imag = turned(block[4 * v + 2 * a], block[4 * v + 2 * a + 1])
+    return strips.at[pl.ds(0, edge)], strips.at[pl.ds(edge, edge)]
+
+
+def widen_state(read, left_of, right_of, v, a, lanes):
+    real, imag = turned(read(4 * v + 2 * a), read(4 * v + 2 * a + 1))
     left = roll(left_of(v), -EDGE * a)
     right = roll(right_of(v), EDGE * a)
     first, third = in_group(lanes, 0), in_group(lanes, 2)
@@ -153,9 +188,9 @@
     )
 
 
-def widen_coef(vectors, block, left_of, right_of, j, lanes):
+def widen_coef(vectors, read, left_of, right_of, j, lanes):
     group = j % 4
-    body = roll(block[4 * vectors + j], EDGE)
+    body = roll(read(4 * vectors + j), EDGE)
     left = roll(left_of(vectors + j // 4), -EDGE * group)
     right = roll(right_of(vectors + j // 4), EDGE * (1 - group))
     first = in_group(lanes, 0)
@@ -164,38 +199,44 @@
     return even, roll(even, 64), jnp.where(lanes < 64, tail, roll(tail, 64))
 
 
-def spread(vectors, block, left_of, right_of, put):
+def spread(vectors, read, left_of, right_of, store):
     lanes = lane_ids()
-    for j in range(KINDS):
-        tiles = widen_coef(vectors, block, left_of, right_of, j, lanes)
-        for t in range(TILES):
-            put(TILES * j + t, tiles[t])
+
+    def job(j):
+        tiles = widen_coef(vectors, read, left_of, right_of, j, lanes)
+        result = [(store, TILES * j + t, tiles[t]) for t in range(TILES)]
         if j < CROSS and HALF[j // 2][1] != 0:
             moved = shift_tiles(tiles, HALF[j // 2][1], lanes)
             at = KINDS + SHIFT_SLOT[HALF[j // 2]] + j % 2
-            for t in range(TILES):
-                put(TILES * at + t, moved[t])
+            result += [(store, TILES * at + t, moved[t]) for t in range(TILES)]
+        return result
+
+    in_batches(4, [functools.partial(job, j) for j in range(KINDS)])
+
+
+def spread_state(vectors, read, left_of, right_of, store_of):
+    lanes = lane_ids()
+
+    def job(v, a):
+        store, place = store_of(v, a)
+        tiles = widen_state(read, left_of, right_of, v, a, lanes)
+        return [(store, place + t, tiles[t]) for t in range(TILES)]
+
+    in_batches(4, [functools.partial(job, v, a) for v in range(vectors) for a in range(2)])
+
+
+def block_kernel(vectors, state, coef, block):
+    in_batches(
+        16, [lambda v=v, a=a, c=c: [(into(block), 4 * v + 2 * a + c, state[c, v, a])] for v in range(vectors) for a in range(2) for c in range(2)]
+    )
+    in_batches(16, [lambda j=j: [(into(block), 4 * vectors + j, coef[j])] for j in range(KINDS)])
 
 
 def own_kernel(vectors, block, strips, parities, wide, coefs):
-    lanes = lane_ids()
-    left_of, right_of = sides(strips, parities[1])
-    for v in range(vectors):
-        for a in range(2):
-            tiles = widen_state(block, left_of, right_of, v, a, lanes)
-            for t in range(TILES):
-                wide[(2 * v + a) * TILES + t] = tiles[t]
-
-    def put(at, tile):
-        coefs[at] = tile
-
-    spread(vectors, block, left_of, right_of, put)
-
-
-def pair_tops(parities):
-    last = 2 * ROWS
-    top = pl.multiple_of(jnp.where(parities[0] == 0, last, 0), ROWS)
-    return top, pl.multiple_of(last - top, ROWS)
+    left_of, right_of = ordered(*halves(strips), is_even(parities[1]))
+    read = lambda at: block[at]
+    spread_state(vectors, read, left_of, right_of, lambda v, a: (into(wide), (2 * v + a) * TILES))
+    spread(vectors, read, left_of, right_of, into(coefs))
 
 
 def coefficient(coefs, dx, dy, a, t, top):
@@ -253,6 +294,7 @@
             def body(group, carry):
                 for top in tops:
                     images = apply_twice(terms[order - 1], coefs, a, group, width, top, lanes)
+                    stores = []
                     for w in range(width):
                         v = group * width + w
                         at = (2 * v + a) * TILES
@@ -262,8 +304,7 @@
                         else:
                             new = [images[w][t] - terms[order - 2][at + t, rows, :] for t in range(TILES)]
                         if order < APPLY:
-                            for t in range(TILES):
-                                terms[order][at + t, rows, :] = new[t]
+                            stores += [(into(terms[order], top), at + t, new[t]) for t in range(TILES)]
                             continue
                         even = []
                         odd = []
@@ -282,9 +323,10 @@
                         if a == 1:
                             same = same + products[v]
                             cross = cross + products[vectors + v]
-                        products[v] = same
-                        products[vectors + v] = cross
-                        finish(at, v, a, (real, imag, tail), (own_real, own_imag))
+                        stores += [(into(products), v, same), (into(products), vectors + v, cross)]
+                        stores += finish(at, v, a, (real, imag, tail), (own_real, own_imag))
+                    for store, place, value in stores:
+                        store(place, value)
                 return carry
 
             lax.fori_loop(0, vectors // width, body, 0)
@@ -306,48 +348,42 @@
 
 
 def put_state(state):
-    def finish(at, v, a, tiles, cells):
-        for t in range(TILES):
-            state[at + t] = tiles[t]
-
-    return finish
+    return lambda at, v, a, tiles, cells: [(into(state), at + t, tiles[t]) for t in range(TILES)]
 
 
 def put_cells(state, start):
-    def finish(at, v, a, tiles, cells):
-        state[0, start + v, a] = cells[0]
-        state[1, start + v, a] = cells[1]
-
-    return finish
+    return lambda at, v, a, tiles, cells: [(into(state), (c, start + v, a), cells[c]) for c in range(2)]
 
 
 def first_kernel(
     half, whole, width, wide, coefs_own, block_one, block_two, strips_one, strips_two, probe, parities, *refs
 ):
-    lanes = lane_ids()
     vectors, _ = half
     split = vectors < whole
     state, coefs = refs[:2]
     other, rows = refs[2:4] if split else (None, refs[2])
     t0, t1, t2, t3, products = refs[-5:]
-    for at in range(2 * whole * TILES):
-        into, place = (t0, at) if at < t0.shape[0] else (other, at - t0.shape[0])
-        into[place, pl.ds(ROWS, ROWS), :] = wide[at]
-    for at in range(COEF_ROWS * TILES):
-        coefs[at, pl.ds(ROWS, ROWS), :] = coefs_own[at]
-    for top, block, strips in zip(pair_tops(parities), (block_one, block_two), (strips_one, strips_two)):
-        left_of, right_of = sides(strips, parities[1])
-        for v in range(whole):
-            for a in range(2):
-                tiles = widen_state(block, left_of, right_of, v, a, lanes)
-                for t in range(TILES):
-                    into = t0 if v < vectors else other
-                    into[(2 * (v % vectors) + a) * TILES + t, pl.ds(top, ROWS), :] = tiles[t]
-
-        def put(at, tile, top=top):
-            coefs[at, pl.ds(top, ROWS), :] = tile
-
-        spread(whole, block, left_of, right_of, put)
+    cells = t0.shape[0]
+    in_batches(16, copies(into(t0, ROWS), lambda at: wide[at], cells))
+    if split:
+        in_batches(16, copies(into(other, ROWS), lambda at: wide[at], cells, cells))
+    in_batches(16, copies(into(coefs, ROWS), lambda at: coefs_own[at], COEF_ROWS * TILES))
+    even = is_even(parities[0])
+    blocks = ordered(block_one, block_two, even)
+    sides = [ordered(one, two, even) for one, two in zip(halves(strips_one), halves(strips_two))]
+    even = is_even(parities[1])
+    for part, top in ((0, 0), (1, 2 * ROWS)):
+        from_one, from_two = sides[0][part], sides[1][part]
+        left_of = lambda at: jnp.where(even, from_two(at), from_one(at))
+        right_of = lambda at: jnp.where(even, from_one(at), from_two(at))
+        spread_state(
+            whole,
+            blocks[part],
+            left_of,
+            right_of,
+            lambda v, a: (into(t0 if v < vectors else other, top), (2 * (v % vectors) + a) * TILES),
+        )
+        spread(whole, blocks[part], left_of, right_of, into(coefs, top))
     time_step(half, width, coefs, probe, (t0, t1, t2, t3), products, put_state(state))
     rows[...] = add_row(half, whole, 0, None, products)
 
@@ -358,10 +394,9 @@
 
 
 def gather_rows(first, own, one, two, parities):
-    top_one, top_two = pair_tops(parities)
-    for top, block in ((ROWS, own), (top_one, one), (top_two, two)):
-        for at in range(first.shape[0]):
-            first[at, pl.ds(top, ROWS), :] = block[at]
+    above, below = ordered(one, two, is_even(parities[0]))
+    for top, read in ((0, above), (ROWS, lambda at: own[at]), (2 * ROWS, below)):
+        in_batches(12, copies(into(first, top), read, first.shape[0]))
 
 
 def middle_kernel(
@@ -379,17 +414,15 @@
 
 
 def last_kernel(half, whole, width, own, one, two, coefs, probe, parities, rows_in, *refs):
-    state, copies, t0, t1, t2, t3, products = refs[-7:]
+    state, sent, t0, t1, t2, t3, products = refs[-7:]
     gather_rows(t0, own, one, two, parities)
     for done in refs[:-7]:
-        for part in range(2):
-            for v in range(done.shape[1]):
-                for a in range(2):
-                    state[part, v, a] = done[part, v, a]
+        places = [(c, v, a) for c in range(2) for v in range(done.shape[1]) for a in range(2)]
+        in_batches(16, [lambda at=at: [(into(state), at, done[at])] for at in places])
     time_step(half, width, coefs, probe, (t0, t1, t2, t3), products, put_cells(state, half[1]))
     rows = add_row(half, whole, STEPS - 1, rows_in, products)
-    for copy in range(copies.shape[0]):
-        copies[copy] = rows
+    for copy in range(sent.shape[0]):
+        sent[copy] = rows
 
 
 def call(kernel, out_shapes, scratch=(), scalars=None, operands=0):
@@ -441,15 +474,14 @@
 
     in_hbm = pl.BlockSpec(memory_space=pltpu.HBM)
     in_smem = pl.BlockSpec(memory_space=pltpu.SMEM)
-    probe, block, pair_one, pair_two = pl.pallas_call(
+    probe, state, coef, pair_one, pair_two = pl.pallas_call(
         functools.partial(pack_kernel, whole, slots),
         out_shape=[
             jax.ShapeDtypeStruct(shape, jnp.float32)
-            for shape in (probe.shape, (4 * whole + KINDS, *tile), (edge_tiles, *tile), (edge_tiles, *tile))
+            for shape in (probe.shape, start.shape, (KINDS, *tile), (edge_tiles, *tile), (edge_tiles, *tile))
         ],
         in_specs=[in_hbm] * 6 + [in_smem] * 2,
         scratch_shapes=[
-            pltpu.VMEM(start.shape, jnp.float32),
             pltpu.VMEM(offsets.shape, jnp.int32),
             pltpu.VMEM(index.shape, jnp.int32),
             pltpu.VMEM(kinds.shape, jnp.int32),
@@ -457,9 +489,17 @@
             pltpu.SemaphoreType.DMA((6,)),
         ],
         compiler_params=pltpu.CompilerParams(vmem_limit_bytes=VMEM_LIMIT),
-    )(start, probe, offsets, index, kinds, hop_table[None], onsite_table, parities)
+    )(
+        *(
+            pltpu.with_memory_space_constraint(array, pltpu.HBM)
+            for array in (start, probe, offsets, index, kinds, hop_table[None])
+        ),
+        onsite_table,
+        parities,
+    )
     one, two = pairings("gy")
     strips = jnp.concatenate([lax.ppermute(pair_one, "gy", one), lax.ppermute(pair_two, "gy", two)])
+    (block,) = call(functools.partial(block_kernel, whole), [(4 * whole + KINDS, *tile)], operands=2)(state, coef)
     block_one, block_two = swap(block, "gx")
     strips_one, strips_two = swap(strips, "gx")
     wide, coefs_own = call(

time: 96.5 us -> 92.1 us (0.954)
  local copies, waits for them, and re-layouts: 5.61 us -> 0.67 us
    unnamed x15 -> x3, local copies, waits for them, and re-layouts: 5.59 us -> 0.66 us
  transfers between devices with their start and end apart: 18 -> 18, of which waited for: 2 -> 2; matrix products, arithmetic and copies ran while one was open for 0% -> 0% of each run, Pallas kernels for 17% -> 18%
where the time goes in v3:
time: 92.1 us; the launch traced here: 91.9 us
  Pallas kernels  30.6 us (33%)
  starting transfers between devices  29 us (31%)
  blocking collectives  26.1 us (28%)
  waiting for transfers between devices  4.69 us (5%)
    ppermute x16, starting transfers between devices, swap(): return (lax.ppermute(block, axis, one), lax.ppermute(block, axis, two))  18.3 us
    all_to_all x1, blocking collectives, per_device(): lax.all_to_all(copies, 'gy', 0, 0)  15.7 us
    all_to_all x1, blocking collectives, per_device(): part = jnp.sum(lax.all_to_all(copies, 'gx', 0, 0), axis=0)  10.4 us
    pallas_call x4, Pallas kernels, per_device(): call(functools.partial(middle_kernel, groups[g], whole, width, step), [st...  10.3 us
    pallas_call x1, Pallas kernels, per_device(): call(functools.partial(first_kernel, groups[0], whole, width), [state_sha...  8.18 us
    ppermute x1, starting transfers between devices, per_device(): lax.ppermute(pair_two, 'gy', two)  7.02 us
    ppermute x1, starting transfers between devices, per_device(): lax.ppermute(pair_one, 'gy', one)  3.66 us
    pallas_call x1, Pallas kernels, per_device(): call(functools.partial(last_kernel, groups[-1], whole, width), [start.sha...  3.15 us
  transfers between devices with their start and end apart: 18, of which 2 were waited for; matrix products, arithmetic and copies ran while one was open for 0% of the time, Pallas kernels for 18%

profile of v3, /device:TPU:1, one launch (start us, length us, event | category | flops | bytes accessed | tf_op | source)
XLA Modules:
  0.0 91.9 jit_solution(16201592956990460090)
XLA Ops:
  1.4 2.1 %shard_map.86 = (f32[2,8,2,8,128]{4,3,2,1,0:T(8,128)S(1)}, f32[2,8,2,8,128]{4,3,2,1,0:T(8,128)S(1)}, f32[27,8,128]{2,1,0:T(8,128)S(1)}, f32[15,8,128]{2,1,0:T(8,128)S(1)}, f32[15,8,128]{2,1,0:T(8,128)S(1)}) custom-call(f32[2,8,2,8,128]{4,3,2,1,0:T(8,128)} %start.1, f32[2,8,2,8,128]{4,3,2,1,0:T(8,128)} %probe.1, s32[10,2,8,128]{3,2,1,0:T(8,128)} %offsets.1, ...), custom_call_target="tpu_custom_call" | custom-call | tf_op jit(solution)/shard_map/pallas_call | solution.py:477
  3.5 3.7 %collective-permute-start = (f32[15,8,128]{2,1,0:T(8,128)S(1)}, f32[15,8,128]{2,1,0:T(8,128)S(1)}, u32[]{:S(2)}, u32[]{:S(2)}) collective-permute-start(f32[15,8,128]{2,1,0:T(8,128)S(1)} %get-tuple-element.29), channel_id=1, source_target_pairs={{0,1},{1,0},{2,3},{3,2},{4,5},{5,4},{6,7},{7,6},{8,9},{9,8},{10,11... | collective-permute-start | bytes 184328 | tf_op jit(solution)/shard_map/ppermute | solution.py:501
  7.2 1.2 %collective-permute-start.3 = (f32[59,8,128]{2,1,0:T(8,128)S(1)}, f32[59,8,128]{2,1,0:T(8,128)S(1)}, u32[]{:S(2)}, u32[]{:S(2)}) collective-permute-start(f32[59,8,128]{2,1,0:T(8,128)S(1)} %shard_map.87.block), channel_id=1, source_target_pairs={{0,240},{16,32},{32,16},{48,64},{64,48},{80,96},{96,80},{112,128},... | collective-permute-start | bytes 725000 | tf_op jit(solution)/shard_map/ppermute | solution.py:449
  8.4 2.0 %collective-permute-start.2 = (f32[59,8,128]{2,1,0:T(8,128)S(1)}, f32[59,8,128]{2,1,0:T(8,128)S(1)}, u32[]{:S(2)}, u32[]{:S(2)}) collective-permute-start(f32[59,8,128]{2,1,0:T(8,128)S(1)} %shard_map.87.block), channel_id=1, source_target_pairs={{0,16},{16,0},{32,48},{48,32},{64,80},{80,64},{96,112},{112,96},{1... | collective-permute-start | bytes 725000 | tf_op jit(solution)/shard_map/ppermute | solution.py:449
  10.4 7.0 %collective-permute-start.1 = (f32[15,8,128]{2,1,0:T(8,128)S(1)}, f32[15,8,128]{2,1,0:T(8,128)S(1)}, u32[]{:S(2)}, u32[]{:S(2)}) collective-permute-start(f32[15,8,128]{2,1,0:T(8,128)S(1)} %get-tuple-element.30), channel_id=1, source_target_pairs={{0,15},{1,2},{2,1},{3,4},{4,3},{5,6},{6,5},{7,8},{8,7},{9,10},{10,... | collective-permute-start | bytes 184328 | tf_op jit(solution)/shard_map/ppermute | solution.py:501
  17.4 2.4 %collective-permute-done.1 = f32[15,8,128]{2,1,0:T(8,128)S(1)} collective-permute-done((f32[15,8,128]{2,1,0:T(8,128)S(1)}, f32[15,8,128]{2,1,0:T(8,128)S(1)}, u32[]{:S(2)}, u32[]{:S(2)}) %collective-permute-start.1) | collective-permute-done | bytes 61472 | tf_op jit(solution)/shard_map/ppermute | solution.py:501
  20.5 1.6 %shard_map.88 = (f32[48,8,128]{2,1,0:T(8,128)S(1)}, f32[141,8,128]{2,1,0:T(8,128)S(1)}) custom-call(f32[59,8,128]{2,1,0:T(8,128)S(1)} %shard_map.87.block, f32[30,8,128]{2,1,0:T(8,128)S(1)} %constant_dynamic-update-slice_fusion.strips, s32[2]{0:T(128)S(1)} %pad_add_fusion.parities), custom_call_target="tpu_custom_call" | custom-call | tf_op jit(solution)/shard_map/pallas_call | solution.py:505
  22.1 2.3 %collective-permute-done.5.strips_two = f32[30,8,128]{2,1,0:T(8,128)S(1)} collective-permute-done((f32[30,8,128]{2,1,0:T(8,128)S(1)}, f32[30,8,128]{2,1,0:T(8,128)S(1)}, u32[]{:S(2)}, u32[]{:S(2)}) %collective-permute-start.5) | collective-permute-done | bytes 122912 | tf_op jit(solution)/shard_map/ppermute | solution.py:449
  24.4 8.2 %shard_map.89 = (f32[24,8,128]{2,1,0:T(8,128)S(1)}, f32[141,24,128]{2,1,0:T(8,128)S(1)}, f32[24,24,128]{2,1,0:T(8,128)S(1)}, f32[4,128]{1,0:T(4,128)S(1)}) custom-call(f32[48,8,128]{2,1,0:T(8,128)S(1)} %get-tuple-element.31.wide, f32[141,8,128]{2,1,0:T(8,128)S(1)} %get-tuple-element.32.coefs_own, f32[59,8,128]{2,1,0:T(8,128)S(1)} %collective-permute-done.2.block_one, ...), custom_call_target="tpu_custom_call" | custom-call | tf_op jit(solution)/shard_map/pallas_call | solution.py:514
  32.9 2.7 %collective-permute-start.8 = (f32[24,8,128]{2,1,0:T(8,128)S(1)}, f32[24,8,128]{2,1,0:T(8,128)S(1)}, u32[]{:S(2)}, u32[]{:S(2)}) collective-permute-start(f32[24,8,128]{2,1,0:T(8,128)S(1)} %get-tuple-element.38.own), channel_id=1, source_target_pairs={{0,16},{16,0},{32,48},{48,32},{64,80},{80,64},{96,112},{112,96},{1... | collective-permute-start | bytes 294920 | tf_op jit(solution)/shard_map/ppermute | solution.py:449
  35.6 2.0 %shard_map.90 = (f32[24,8,128]{2,1,0:T(8,128)S(1)}, f32[4,128]{1,0:T(4,128)S(1)}) custom-call(f32[24,24,128]{2,1,0:T(8,128)S(1)} %get-tuple-element.34.t0, f32[141,24,128]{2,1,0:T(8,128)S(1)} %get-tuple-element.35.coefs, f32[2,8,2,8,128]{4,3,2,1,0:T(8,128)S(1)} %get-tuple-element.33.probe, f32[4,128]{1,0:T(4,128)S(1)} %get-tuple-element.36.rows_in), custom_call_target="tpu_custom_call" | custom-call | tf_op jit(solution)/shard_map/pallas_call | solution.py:523
  37.6 3.3 %collective-permute-start.6 = (f32[24,8,128]{2,1,0:T(8,128)S(1)}, f32[24,8,128]{2,1,0:T(8,128)S(1)}, u32[]{:S(2)}, u32[]{:S(2)}) collective-permute-start(f32[24,8,128]{2,1,0:T(8,128)S(1)} %get-tuple-element.37.own), channel_id=1, source_target_pairs={{0,16},{16,0},{32,48},{48,32},{64,80},{80,64},{96,112},{112,96},{1... | collective-permute-start | bytes 294920 | tf_op jit(solution)/shard_map/ppermute | solution.py:449
  40.9 2.6 %shard_map.91 = (f32[24,8,128]{2,1,0:T(8,128)S(1)}, f32[4,128]{1,0:T(4,128)S(1)}) custom-call(f32[24,8,128]{2,1,0:T(8,128)S(1)} %get-tuple-element.38.own, f32[24,8,128]{2,1,0:T(8,128)S(1)} %collective-permute-done.8.one, f32[24,8,128]{2,1,0:T(8,128)S(1)} %collective-permute-done.9.two, f32[141,24,128]{2,1,0:T(8,128)S(1)} %get-tuple-element.35.coefs, ...), custom_call_target="tpu_custom_call" | custom-call | tf_op jit(solution)/shard_map/pallas_call | solution.py:529
  44.3 2.6 %shard_map.92 = (f32[24,8,128]{2,1,0:T(8,128)S(1)}, f32[4,128]{1,0:T(4,128)S(1)}) custom-call(f32[24,8,128]{2,1,0:T(8,128)S(1)} %get-tuple-element.37.own, f32[24,8,128]{2,1,0:T(8,128)S(1)} %collective-permute-done.6.one, f32[24,8,128]{2,1,0:T(8,128)S(1)} %collective-permute-done.7.two, f32[141,24,128]{2,1,0:T(8,128)S(1)} %get-tuple-element.35.coefs, ...), custom_call_target="tpu_custom_call" | custom-call | tf_op jit(solution)/shard_map/pallas_call | solution.py:529
  46.9 1.0 %collective-permute-start.11 = (f32[24,8,128]{2,1,0:T(8,128)S(1)}, f32[24,8,128]{2,1,0:T(8,128)S(1)}, u32[]{:S(2)}, u32[]{:S(2)}) collective-permute-start(f32[24,8,128]{2,1,0:T(8,128)S(1)} %get-tuple-element.41.own), channel_id=1, source_target_pairs={{0,240},{16,32},{32,16},{48,64},{64,48},{80,96},{96,80},{112,128},... | collective-permute-start | bytes 294920 | tf_op jit(solution)/shard_map/ppermute | solution.py:449
  47.9 2.4 %collective-permute-start.10 = (f32[24,8,128]{2,1,0:T(8,128)S(1)}, f32[24,8,128]{2,1,0:T(8,128)S(1)}, u32[]{:S(2)}, u32[]{:S(2)}) collective-permute-start(f32[24,8,128]{2,1,0:T(8,128)S(1)} %get-tuple-element.41.own), channel_id=1, source_target_pairs={{0,16},{16,0},{32,48},{48,32},{64,80},{80,64},{96,112},{112,96},{1... | collective-permute-start | bytes 294920 | tf_op jit(solution)/shard_map/ppermute | solution.py:449
  50.3 2.6 %shard_map.93 = (f32[24,8,128]{2,1,0:T(8,128)S(1)}, f32[4,128]{1,0:T(4,128)S(1)}) custom-call(f32[24,8,128]{2,1,0:T(8,128)S(1)} %get-tuple-element.42.own, f32[24,8,128]{2,1,0:T(8,128)S(1)} %collective-permute-done.12.one, f32[24,8,128]{2,1,0:T(8,128)S(1)} %collective-permute-done.13.two, f32[141,24,128]{2,1,0:T(8,128)S(1)} %get-tuple-element.35.coefs, ...), custom_call_target="tpu_custom_call" | custom-call | tf_op jit(solution)/shard_map/pallas_call | solution.py:529
  53.7 2.6 %shard_map.94 = (f32[24,8,128]{2,1,0:T(8,128)S(1)}, f32[4,128]{1,0:T(4,128)S(1)}) custom-call(f32[24,8,128]{2,1,0:T(8,128)S(1)} %get-tuple-element.41.own, f32[24,8,128]{2,1,0:T(8,128)S(1)} %collective-permute-done.10.one, f32[24,8,128]{2,1,0:T(8,128)S(1)} %collective-permute-done.11.two, f32[141,24,128]{2,1,0:T(8,128)S(1)} %get-tuple-element.35.coefs, ...), custom_call_target="tpu_custom_call" | custom-call | tf_op jit(solution)/shard_map/pallas_call | solution.py:529
  56.3 0.9 %collective-permute-start.15 = (f32[24,8,128]{2,1,0:T(8,128)S(1)}, f32[24,8,128]{2,1,0:T(8,128)S(1)}, u32[]{:S(2)}, u32[]{:S(2)}) collective-permute-start(f32[24,8,128]{2,1,0:T(8,128)S(1)} %get-tuple-element.45.own), channel_id=1, source_target_pairs={{0,240},{16,32},{32,16},{48,64},{64,48},{80,96},{96,80},{112,128},... | collective-permute-start | bytes 294920 | tf_op jit(solution)/shard_map/ppermute | solution.py:449
  57.2 2.1 %collective-permute-start.14 = (f32[24,8,128]{2,1,0:T(8,128)S(1)}, f32[24,8,128]{2,1,0:T(8,128)S(1)}, u32[]{:S(2)}, u32[]{:S(2)}) collective-permute-start(f32[24,8,128]{2,1,0:T(8,128)S(1)} %get-tuple-element.45.own), channel_id=1, source_target_pairs={{0,16},{16,0},{32,48},{48,32},{64,80},{80,64},{96,112},{112,96},{1... | collective-permute-start | bytes 294920 | tf_op jit(solution)/shard_map/ppermute | solution.py:449
  59.3 2.6 %shard_map.95 = (f32[2,4,2,8,128]{4,3,2,1,0:T(8,128)S(1)}, f32[4,128]{1,0:T(4,128)S(1)}) custom-call(f32[24,8,128]{2,1,0:T(8,128)S(1)} %get-tuple-element.46.own, f32[24,8,128]{2,1,0:T(8,128)S(1)} %collective-permute-done.16.one, f32[24,8,128]{2,1,0:T(8,128)S(1)} %collective-permute-done.17.two, f32[141,24,128]{2,1,0:T(8,128)S(1)} %get-tuple-element.35.coefs, ...), custom_call_target="tpu_custom_call" | custom-call | tf_op jit(solution)/shard_map/pallas_call | solution.py:538
  61.9 3.1 %shard_map.96 = (f32[2,8,2,8,128]{4,3,2,1,0:T(8,128)}, f32[16,4,128]{2,1,0:T(4,128)S(1)}) custom-call(f32[24,8,128]{2,1,0:T(8,128)S(1)} %get-tuple-element.45.own, f32[24,8,128]{2,1,0:T(8,128)S(1)} %collective-permute-done.14.one, f32[24,8,128]{2,1,0:T(8,128)S(1)} %collective-permute-done.15.two, f32[141,24,128]{2,1,0:T(8,128)S(1)} %get-tuple-element.35.coefs, ...), custom_call_target="tpu_custom_call" | custom-call | tf_op jit(solution)/shard_map/pallas_call | solution.py:546
  65.1 10.4 %all_to_all.10 = f32[16,4,128]{2,1,0:T(4,128)S(1)} all-to-all(f32[16,4,128]{2,1,0:T(4,128)S(1)} %get-tuple-element.51), channel_id=1, replica_groups=mesh['gx'=16,'gy'=16] {'gx'}, dimensions={0} | all-to-all | bytes 65536 | tf_op jit(solution)/shard_map/all_to_all | solution.py:553
  75.6 15.7 %all_to_all.11.rows = f32[16,4,128]{2,1,0:T(4,128)S(1)} all-to-all(f32[16,4,128]{2,1,0:T(4,128)S(1)} %broadcast_in_dim.10), channel_id=1, replica_groups=mesh['gx'=16,'gy'=16] {'gy'}, dimensions={0} | all-to-all | bytes 65536 | tf_op jit(solution)/shard_map/all_to_all | solution.py:559
  (33 shorter events, 4.2 us)
Async XLA Ops:
  0.7 0.7 copy-start
  3.5 14.0 %collective-permute-start = (f32[15,8,128]{2,1,0:T(8,128)S(1)}, f32[15,8,128]{2,1,0:T(8,128)S(1)}, u32[]{:S(2)}, u32[]{:S(2)}) collective-permute-start(f32[15,8,128]{2,1,0:T(8,128)S(1)} %get-tuple-element.29), channel_id=1, source_target_pairs={{0,1},{1,0},{2,3},{3,2},{4,5},{5,4},{6,7},{7,6},{8,9},{9,8},{10,11... | collective-permute-start | bytes 184328 | tf_op jit(solution)/shard_map/ppermute | solution.py:501
  7.2 17.2 %collective-permute-start.3 = (f32[59,8,128]{2,1,0:T(8,128)S(1)}, f32[59,8,128]{2,1,0:T(8,128)S(1)}, u32[]{:S(2)}, u32[]{:S(2)}) collective-permute-start(f32[59,8,128]{2,1,0:T(8,128)S(1)} %shard_map.87.block), channel_id=1, source_target_pairs={{0,240},{16,32},{32,16},{48,64},{64,48},{80,96},{96,80},{112,128},... | collective-permute-start | bytes 725000 | tf_op jit(solution)/shard_map/ppermute | solution.py:449
  8.4 16.0 %collective-permute-start.2 = (f32[59,8,128]{2,1,0:T(8,128)S(1)}, f32[59,8,128]{2,1,0:T(8,128)S(1)}, u32[]{:S(2)}, u32[]{:S(2)}) collective-permute-start(f32[59,8,128]{2,1,0:T(8,128)S(1)} %shard_map.87.block), channel_id=1, source_target_pairs={{0,16},{16,0},{32,48},{48,32},{64,80},{80,64},{96,112},{112,96},{1... | collective-permute-start | bytes 725000 | tf_op jit(solution)/shard_map/ppermute | solution.py:449
  10.4 9.4 %collective-permute-start.1 = (f32[15,8,128]{2,1,0:T(8,128)S(1)}, f32[15,8,128]{2,1,0:T(8,128)S(1)}, u32[]{:S(2)}, u32[]{:S(2)}) collective-permute-start(f32[15,8,128]{2,1,0:T(8,128)S(1)} %get-tuple-element.30), channel_id=1, source_target_pairs={{0,15},{1,2},{2,1},{3,4},{4,3},{5,6},{6,5},{7,8},{8,7},{9,10},{10,... | collective-permute-start | bytes 184328 | tf_op jit(solution)/shard_map/ppermute | solution.py:501
  19.8 4.6 %collective-permute-start.5 = (f32[30,8,128]{2,1,0:T(8,128)S(1)}, f32[30,8,128]{2,1,0:T(8,128)S(1)}, u32[]{:S(2)}, u32[]{:S(2)}) collective-permute-start(f32[30,8,128]{2,1,0:T(8,128)S(1)} %constant_dynamic-update-slice_fusion.strips), channel_id=1, source_target_pairs={{0,240},{16,32},{32,16},{48,64},{64,48},{80,96},{96,80},{112,128},... | collective-permute-start | bytes 368648 | tf_op jit(solution)/shard_map/ppermute | solution.py:449
  19.8 4.5 %collective-permute-start.4 = (f32[30,8,128]{2,1,0:T(8,128)S(1)}, f32[30,8,128]{2,1,0:T(8,128)S(1)}, u32[]{:S(2)}, u32[]{:S(2)}) collective-permute-start(f32[30,8,128]{2,1,0:T(8,128)S(1)} %constant_dynamic-update-slice_fusion.strips), channel_id=1, source_target_pairs={{0,16},{16,0},{32,48},{48,32},{64,80},{80,64},{96,112},{112,96},{1... | collective-permute-start | bytes 368648 | tf_op jit(solution)/shard_map/ppermute | solution.py:449
  32.6 8.4 %collective-permute-start.9 = (f32[24,8,128]{2,1,0:T(8,128)S(1)}, f32[24,8,128]{2,1,0:T(8,128)S(1)}, u32[]{:S(2)}, u32[]{:S(2)}) collective-permute-start(f32[24,8,128]{2,1,0:T(8,128)S(1)} %get-tuple-element.38.own), channel_id=1, source_target_pairs={{0,240},{16,32},{32,16},{48,64},{64,48},{80,96},{96,80},{112,128},... | collective-permute-start | bytes 294920 | tf_op jit(solution)/shard_map/ppermute | solution.py:449
  32.9 8.0 %collective-permute-start.8 = (f32[24,8,128]{2,1,0:T(8,128)S(1)}, f32[24,8,128]{2,1,0:T(8,128)S(1)}, u32[]{:S(2)}, u32[]{:S(2)}) collective-permute-start(f32[24,8,128]{2,1,0:T(8,128)S(1)} %get-tuple-element.38.own), channel_id=1, source_target_pairs={{0,16},{16,0},{32,48},{48,32},{64,80},{80,64},{96,112},{112,96},{1... | collective-permute-start | bytes 294920 | tf_op jit(solution)/shard_map/ppermute | solution.py:449
  37.6 6.7 %collective-permute-start.7 = (f32[24,8,128]{2,1,0:T(8,128)S(1)}, f32[24,8,128]{2,1,0:T(8,128)S(1)}, u32[]{:S(2)}, u32[]{:S(2)}) collective-permute-start(f32[24,8,128]{2,1,0:T(8,128)S(1)} %get-tuple-element.37.own), channel_id=1, source_target_pairs={{0,240},{16,32},{32,16},{48,64},{64,48},{80,96},{96,80},{112,128},... | collective-permute-start | bytes 294920 | tf_op jit(solution)/shard_map/ppermute | solution.py:449
  37.6 6.7 %collective-permute-start.6 = (f32[24,8,128]{2,1,0:T(8,128)S(1)}, f32[24,8,128]{2,1,0:T(8,128)S(1)}, u32[]{:S(2)}, u32[]{:S(2)}) collective-permute-start(f32[24,8,128]{2,1,0:T(8,128)S(1)} %get-tuple-element.37.own), channel_id=1, source_target_pairs={{0,16},{16,0},{32,48},{48,32},{64,80},{80,64},{96,112},{112,96},{1... | collective-permute-start | bytes 294920 | tf_op jit(solution)/shard_map/ppermute | solution.py:449
  43.5 6.7 %collective-permute-start.13 = (f32[24,8,128]{2,1,0:T(8,128)S(1)}, f32[24,8,128]{2,1,0:T(8,128)S(1)}, u32[]{:S(2)}, u32[]{:S(2)}) collective-permute-start(f32[24,8,128]{2,1,0:T(8,128)S(1)} %get-tuple-element.42.own), channel_id=1, source_target_pairs={{0,240},{16,32},{32,16},{48,64},{64,48},{80,96},{96,80},{112,128},... | collective-permute-start | bytes 294920 | tf_op jit(solution)/shard_map/ppermute | solution.py:449
  43.5 6.7 %collective-permute-start.12 = (f32[24,8,128]{2,1,0:T(8,128)S(1)}, f32[24,8,128]{2,1,0:T(8,128)S(1)}, u32[]{:S(2)}, u32[]{:S(2)}) collective-permute-start(f32[24,8,128]{2,1,0:T(8,128)S(1)} %get-tuple-element.42.own), channel_id=1, source_target_pairs={{0,16},{16,0},{32,48},{48,32},{64,80},{80,64},{96,112},{112,96},{1... | collective-permute-start | bytes 294920 | tf_op jit(solution)/shard_map/ppermute | solution.py:449
  46.9 6.8 %collective-permute-start.11 = (f32[24,8,128]{2,1,0:T(8,128)S(1)}, f32[24,8,128]{2,1,0:T(8,128)S(1)}, u32[]{:S(2)}, u32[]{:S(2)}) collective-permute-start(f32[24,8,128]{2,1,0:T(8,128)S(1)} %get-tuple-element.41.own), channel_id=1, source_target_pairs={{0,240},{16,32},{32,16},{48,64},{64,48},{80,96},{96,80},{112,128},... | collective-permute-start | bytes 294920 | tf_op jit(solution)/shard_map/ppermute | solution.py:449
  47.9 5.8 %collective-permute-start.10 = (f32[24,8,128]{2,1,0:T(8,128)S(1)}, f32[24,8,128]{2,1,0:T(8,128)S(1)}, u32[]{:S(2)}, u32[]{:S(2)}) collective-permute-start(f32[24,8,128]{2,1,0:T(8,128)S(1)} %get-tuple-element.41.own), channel_id=1, source_target_pairs={{0,16},{16,0},{32,48},{48,32},{64,80},{80,64},{96,112},{112,96},{1... | collective-permute-start | bytes 294920 | tf_op jit(solution)/shard_map/ppermute | solution.py:449
  52.8 6.5 %collective-permute-start.17 = (f32[24,8,128]{2,1,0:T(8,128)S(1)}, f32[24,8,128]{2,1,0:T(8,128)S(1)}, u32[]{:S(2)}, u32[]{:S(2)}) collective-permute-start(f32[24,8,128]{2,1,0:T(8,128)S(1)} %get-tuple-element.46.own), channel_id=1, source_target_pairs={{0,240},{16,32},{32,16},{48,64},{64,48},{80,96},{96,80},{112,128},... | collective-permute-start | bytes 294920 | tf_op jit(solution)/shard_map/ppermute | solution.py:449
  52.9 6.5 %collective-permute-start.16 = (f32[24,8,128]{2,1,0:T(8,128)S(1)}, f32[24,8,128]{2,1,0:T(8,128)S(1)}, u32[]{:S(2)}, u32[]{:S(2)}) collective-permute-start(f32[24,8,128]{2,1,0:T(8,128)S(1)} %get-tuple-element.46.own), channel_id=1, source_target_pairs={{0,16},{16,0},{32,48},{48,32},{64,80},{80,64},{96,112},{112,96},{1... | collective-permute-start | bytes 294920 | tf_op jit(solution)/shard_map/ppermute | solution.py:449
  56.3 5.6 %collective-permute-start.15 = (f32[24,8,128]{2,1,0:T(8,128)S(1)}, f32[24,8,128]{2,1,0:T(8,128)S(1)}, u32[]{:S(2)}, u32[]{:S(2)}) collective-permute-start(f32[24,8,128]{2,1,0:T(8,128)S(1)} %get-tuple-element.45.own), channel_id=1, source_target_pairs={{0,240},{16,32},{32,16},{48,64},{64,48},{80,96},{96,80},{112,128},... | collective-permute-start | bytes 294920 | tf_op jit(solution)/shard_map/ppermute | solution.py:449
  57.2 4.7 %collective-permute-start.14 = (f32[24,8,128]{2,1,0:T(8,128)S(1)}, f32[24,8,128]{2,1,0:T(8,128)S(1)}, u32[]{:S(2)}, u32[]{:S(2)}) collective-permute-start(f32[24,8,128]{2,1,0:T(8,128)S(1)} %get-tuple-element.45.own), channel_id=1, source_target_pairs={{0,16},{16,0},{32,48},{48,32},{64,80},{80,64},{96,112},{112,96},{1... | collective-permute-start | bytes 294920 | tf_op jit(solution)/shard_map/ppermute | solution.py:449

commit v4 on v3

--- a/solution.py
+++ b/solution.py
@@ -98,14 +98,19 @@
         copy.wait()
 
 
+def wide_table(entries):
+    spare = jnp.zeros((1, LANES - entries.shape[1]), jnp.float32)
+    return jnp.broadcast_to(jnp.concatenate([entries, spare], axis=1), (ROWS, LANES))
+
+
 def pack_kernel(
     vectors, slots, start, probe, offsets, index, kinds, hop_table, onsite_table, parities,
-    probe_copy, state, coef, pair_one, pair_two, offsets_here, index_here, kinds_here, table_here, semaphores,
+    probe_copy, state, coef, pair_one, pair_two, offsets_here, index_here, kinds_here, table_here, levels_here, semaphores,
 ):
     fetch(
         [
             (start, state), (offsets, offsets_here), (index, index_here), (kinds, kinds_here),
-            (hop_table, table_here), (probe, probe_copy),
+            (hop_table, table_here), (onsite_table, levels_here), (probe, probe_copy),
         ],
         semaphores,
     )
@@ -131,9 +136,8 @@
         return send(v, to_right, to_left)
 
     in_batches(vectors, [functools.partial(strip, v) for v in range(vectors)])
-    entries = table_here[...]
-    spare = LANES - entries.shape[1]
-    table = jnp.broadcast_to(jnp.concatenate([entries, jnp.zeros((1, spare), jnp.float32)], axis=1), (ROWS, LANES))
+    table = wide_table(table_here[...])
+    levels = wide_table(levels_here[...])
     arrays = [jnp.zeros((ROWS, LANES), jnp.float32) for _ in range(KINDS)]
     for a in range(2):
         for slot in range(slots):
@@ -144,8 +148,7 @@
                 arrays[at] = arrays[at] + jnp.where(code == 5 * (p + 2) + q + 2, amount, 0.0)
             if a == 0:
                 arrays[CROSS] = arrays[CROSS] + jnp.where(code == 12, amount, 0.0)
-        for entry in range(onsite_table.shape[0]):
-            arrays[ONSITE + a] = jnp.where(kinds_here[a] == entry, onsite_table[entry], arrays[ONSITE + a])
+        arrays[ONSITE + a] = jnp.take_along_axis(levels, kinds_here[a], axis=1)
     for start_at in range(0, KINDS, 4):
         right = left = None
         for group in range(min(4, KINDS - start_at)):
@@ -171,11 +174,6 @@
     )
 
 
-def halves(strips):
-    edge = strips.shape[0] // 2
-    return strips.at[pl.ds(0, edge)], strips.at[pl.ds(edge, edge)]
-
-
 def widen_state(read, left_of, right_of, v, a, lanes):
     real, imag = turned(read(4 * v + 2 * a), read(4 * v + 2 * a + 1))
     left = roll(left_of(v), -EDGE * a)
@@ -232,8 +230,9 @@
     in_batches(16, [lambda j=j: [(into(block), 4 * vectors + j, coef[j])] for j in range(KINDS)])
 
 
-def own_kernel(vectors, block, strips, parities, wide, coefs):
-    left_of, right_of = ordered(*halves(strips), is_even(parities[1]))
+def own_kernel(vectors, block, strips, wide, coefs):
+    edge = strips.shape[0] // 2
+    left_of, right_of = lambda at: strips[at], lambda at: strips[edge + at]
     read = lambda at: block[at]
     spread_state(vectors, read, left_of, right_of, lambda v, a: (into(wide), (2 * v + a) * TILES))
     spread(vectors, read, left_of, right_of, into(coefs))
@@ -370,12 +369,11 @@
     in_batches(16, copies(into(coefs, ROWS), lambda at: coefs_own[at], COEF_ROWS * TILES))
     even = is_even(parities[0])
     blocks = ordered(block_one, block_two, even)
-    sides = [ordered(one, two, even) for one, two in zip(halves(strips_one), halves(strips_two))]
-    even = is_even(parities[1])
+    strips = ordered(strips_one, strips_two, even)
+    edge = strips_one.shape[0] // 2
     for part, top in ((0, 0), (1, 2 * ROWS)):
-        from_one, from_two = sides[0][part], sides[1][part]
-        left_of = lambda at: jnp.where(even, from_two(at), from_one(at))
-        right_of = lambda at: jnp.where(even, from_one(at), from_two(at))
+        left_of = strips[part]
+        right_of = lambda at, part=part: strips[part](edge + at)
         spread_state(
             whole,
             blocks[part],
@@ -480,34 +478,35 @@
             jax.ShapeDtypeStruct(shape, jnp.float32)
             for shape in (probe.shape, start.shape, (KINDS, *tile), (edge_tiles, *tile), (edge_tiles, *tile))
         ],
-        in_specs=[in_hbm] * 6 + [in_smem] * 2,
+        in_specs=[in_hbm] * 7 + [in_smem],
         scratch_shapes=[
             pltpu.VMEM(offsets.shape, jnp.int32),
             pltpu.VMEM(index.shape, jnp.int32),
             pltpu.VMEM(kinds.shape, jnp.int32),
             pltpu.VMEM((1, hop_table.shape[0]), jnp.float32),
-            pltpu.SemaphoreType.DMA((6,)),
+            pltpu.VMEM((1, onsite_table.shape[0]), jnp.float32),
+            pltpu.SemaphoreType.DMA((7,)),
         ],
         compiler_params=pltpu.CompilerParams(vmem_limit_bytes=VMEM_LIMIT),
     )(
         *(
             pltpu.with_memory_space_constraint(array, pltpu.HBM)
-            for array in (start, probe, offsets, index, kinds, hop_table[None])
+            for array in (start, probe, offsets, index, kinds, hop_table[None], onsite_table[None])
         ),
-        onsite_table,
         parities,
     )
     one, two = pairings("gy")
-    strips = jnp.concatenate([lax.ppermute(pair_one, "gy", one), lax.ppermute(pair_two, "gy", two)])
+    side_one, side_two = lax.ppermute(pair_one, "gy", one), lax.ppermute(pair_two, "gy", two)
+    even = parities[1] == 0
+    strips = jnp.concatenate([jnp.where(even, side_two, side_one), jnp.where(even, side_one, side_two)])
     (block,) = call(functools.partial(block_kernel, whole), [(4 * whole + KINDS, *tile)], operands=2)(state, coef)
     block_one, block_two = swap(block, "gx")
     strips_one, strips_two = swap(strips, "gx")
     wide, coefs_own = call(
         functools.partial(own_kernel, whole),
         [(2 * whole * TILES, *tile), (COEF_ROWS * TILES, *tile)],
-        scalars=2,
-        operands=3,
-    )(block, strips, parities)
+        operands=2,
+    )(block, strips)
 
     state_shape = (cells, *tile)
     others = [region] * (PARTS - 1)

time: 92.1 us -> 90.5 us (0.983)
  starting transfers between devices: 29 us -> 31.7 us
  waiting for transfers between devices: 4.69 us -> 2.29 us
    ppermute x16, starting transfers between devices: 18.3 us -> 22.7 us  [swap(): return (lax.ppermute(block, axis, one), lax.ppermute(block, axis, two))]
    ppermute x1, starting transfers between devices: 3.66 us -> 0.01 us  [per_device(): lax.ppermute(pair_one, 'gy', one)]
    ppermute x1, waiting for transfers between devices: 2.36 us -> 0.01 us  [per_device(): lax.ppermute(pair_two, 'gy', two)]
    ppermute x1, starting transfers between devices: 7.02 us -> 8.95 us  [per_device(): lax.ppermute(pair_two, 'gy', two)]
    ppermute x16, waiting for transfers between devices: 2.32 us -> 0.98 us  [swap(): return (lax.ppermute(block, axis, one), lax.ppermute(block, axis, two))]
    ppermute x1, waiting for transfers between devices: 0.01 us -> 1.3 us  [per_device(): lax.ppermute(pair_one, 'gy', one)]
    all_to_all x1, blocking collectives: 15.7 us -> 14.8 us  [per_device(): lax.all_to_all(copies, 'gy', 0, 0)]
where the time goes in v4:
time: 90.5 us; the launch traced here: 90.3 us
  starting transfers between devices  31.7 us (35%)
  Pallas kernels  30.3 us (33%)
  blocking collectives  25.2 us (28%)
  waiting for transfers between devices  2.29 us (3%)
    ppermute x16, starting transfers between devices, swap(): return (lax.ppermute(block, axis, one), lax.ppermute(block, axis, two))  22.7 us
    all_to_all x1, blocking collectives, per_device(): lax.all_to_all(copies, 'gy', 0, 0)  14.8 us
    all_to_all x1, blocking collectives, per_device(): part = jnp.sum(lax.all_to_all(copies, 'gx', 0, 0), axis=0)  10.4 us
    pallas_call x4, Pallas kernels, per_device(): call(functools.partial(middle_kernel, groups[g], whole, width, step), [st...  10.3 us
    ppermute x1, starting transfers between devices, per_device(): lax.ppermute(pair_two, 'gy', two)  8.95 us
    pallas_call x1, Pallas kernels, per_device(): call(functools.partial(first_kernel, groups[0], whole, width), [state_sha...  8.18 us
    pallas_call x1, Pallas kernels, per_device(): call(functools.partial(last_kernel, groups[-1], whole, width), [start.sha...  3.15 us
    pallas_call x1, Pallas kernels, per_device(): call(functools.partial(close_kernel, groups[g], whole, width), [(2, vecto...  2.58 us
  transfers between devices with their start and end apart: 18, of which 2 were waited for; matrix products, arithmetic and copies ran while one was open for 0% of the time, Pallas kernels for 18%

profile of v4, /device:TPU:1, one launch (start us, length us, event | category | flops | bytes accessed | tf_op | source)
XLA Modules:
  0.0 90.3 jit_solution(14547219142111832928)
XLA Ops:
  0.7 2.1 %shard_map.86 = (f32[2,8,2,8,128]{4,3,2,1,0:T(8,128)S(1)}, f32[2,8,2,8,128]{4,3,2,1,0:T(8,128)S(1)}, f32[27,8,128]{2,1,0:T(8,128)S(1)}, f32[15,8,128]{2,1,0:T(8,128)S(1)}, f32[15,8,128]{2,1,0:T(8,128)S(1)}) custom-call(f32[2,8,2,8,128]{4,3,2,1,0:T(8,128)} %start.1, f32[2,8,2,8,128]{4,3,2,1,0:T(8,128)} %probe.1, s32[10,2,8,128]{3,2,1,0:T(8,128)} %offsets.1, ...), custom_call_target="tpu_custom_call" | custom-call | tf_op jit(solution)/shard_map/pallas_call | solution.py:475
  2.8 9.0 %collective-permute-start = (f32[15,8,128]{2,1,0:T(8,128)S(1)}, f32[15,8,128]{2,1,0:T(8,128)S(1)}, u32[]{:S(2)}, u32[]{:S(2)}) collective-permute-start(f32[15,8,128]{2,1,0:T(8,128)S(1)} %get-tuple-element.29), channel_id=1, source_target_pairs={{0,15},{1,2},{2,1},{3,4},{4,3},{5,6},{6,5},{7,8},{8,7},{9,10},{10,... | collective-permute-start | bytes 184328 | tf_op jit(solution)/shard_map/ppermute | solution.py:499
  11.8 1.2 %collective-permute-start.3 = (f32[59,8,128]{2,1,0:T(8,128)S(1)}, f32[59,8,128]{2,1,0:T(8,128)S(1)}, u32[]{:S(2)}, u32[]{:S(2)}) collective-permute-start(f32[59,8,128]{2,1,0:T(8,128)S(1)} %shard_map.87.block), channel_id=1, source_target_pairs={{0,240},{16,32},{32,16},{48,64},{64,48},{80,96},{96,80},{112,128},... | collective-permute-start | bytes 725000 | tf_op jit(solution)/shard_map/ppermute | solution.py:447
  13.0 2.0 %collective-permute-start.2 = (f32[59,8,128]{2,1,0:T(8,128)S(1)}, f32[59,8,128]{2,1,0:T(8,128)S(1)}, u32[]{:S(2)}, u32[]{:S(2)}) collective-permute-start(f32[59,8,128]{2,1,0:T(8,128)S(1)} %shard_map.87.block), channel_id=1, source_target_pairs={{0,16},{16,0},{32,48},{48,32},{64,80},{80,64},{96,112},{112,96},{1... | collective-permute-start | bytes 725000 | tf_op jit(solution)/shard_map/ppermute | solution.py:447
  15.1 1.3 %collective-permute-done.1 = f32[15,8,128]{2,1,0:T(8,128)S(1)} collective-permute-done((f32[15,8,128]{2,1,0:T(8,128)S(1)}, f32[15,8,128]{2,1,0:T(8,128)S(1)}, u32[]{:S(2)}, u32[]{:S(2)}) %collective-permute-start.1) | collective-permute-done | bytes 61472 | tf_op jit(solution)/shard_map/ppermute | solution.py:499
  16.4 2.4 %collective-permute-start.5 = (f32[30,8,128]{2,1,0:T(8,128)S(1)}, f32[30,8,128]{2,1,0:T(8,128)S(1)}, u32[]{:S(2)}, u32[]{:S(2)}) collective-permute-start(f32[30,8,128]{2,1,0:T(8,128)S(1)} %pad_maximum_fusion.strips), channel_id=1, source_target_pairs={{0,240},{16,32},{32,16},{48,64},{64,48},{80,96},{96,80},{112,128},... | collective-permute-start | bytes 368648 | tf_op jit(solution)/shard_map/ppermute | solution.py:447
  19.6 1.1 %shard_map.88 = (f32[48,8,128]{2,1,0:T(8,128)S(1)}, f32[141,8,128]{2,1,0:T(8,128)S(1)}) custom-call(f32[59,8,128]{2,1,0:T(8,128)S(1)} %shard_map.87.block, f32[30,8,128]{2,1,0:T(8,128)S(1)} %pad_maximum_fusion.strips), custom_call_target="tpu_custom_call" | custom-call | tf_op jit(solution)/shard_map/pallas_call | solution.py:505
  21.7 8.2 %shard_map.89 = (f32[24,8,128]{2,1,0:T(8,128)S(1)}, f32[141,24,128]{2,1,0:T(8,128)S(1)}, f32[24,24,128]{2,1,0:T(8,128)S(1)}, f32[4,128]{1,0:T(4,128)S(1)}) custom-call(f32[48,8,128]{2,1,0:T(8,128)S(1)} %get-tuple-element.31.wide, f32[141,8,128]{2,1,0:T(8,128)S(1)} %get-tuple-element.32.coefs_own, f32[59,8,128]{2,1,0:T(8,128)S(1)} %collective-permute-done.2.block_one, ...), custom_call_target="tpu_custom_call" | custom-call | tf_op jit(solution)/shard_map/pallas_call | solution.py:513
  29.9 1.7 %collective-permute-start.9 = (f32[24,8,128]{2,1,0:T(8,128)S(1)}, f32[24,8,128]{2,1,0:T(8,128)S(1)}, u32[]{:S(2)}, u32[]{:S(2)}) collective-permute-start(f32[24,8,128]{2,1,0:T(8,128)S(1)} %get-tuple-element.38.own), channel_id=1, source_target_pairs={{0,240},{16,32},{32,16},{48,64},{64,48},{80,96},{96,80},{112,128},... | collective-permute-start | bytes 294920 | tf_op jit(solution)/shard_map/ppermute | solution.py:447
  31.6 3.0 %collective-permute-start.8 = (f32[24,8,128]{2,1,0:T(8,128)S(1)}, f32[24,8,128]{2,1,0:T(8,128)S(1)}, u32[]{:S(2)}, u32[]{:S(2)}) collective-permute-start(f32[24,8,128]{2,1,0:T(8,128)S(1)} %get-tuple-element.38.own), channel_id=1, source_target_pairs={{0,16},{16,0},{32,48},{48,32},{64,80},{80,64},{96,112},{112,96},{1... | collective-permute-start | bytes 294920 | tf_op jit(solution)/shard_map/ppermute | solution.py:447
  34.5 2.2 %shard_map.90 = (f32[24,8,128]{2,1,0:T(8,128)S(1)}, f32[4,128]{1,0:T(4,128)S(1)}) custom-call(f32[24,24,128]{2,1,0:T(8,128)S(1)} %get-tuple-element.34.t0, f32[141,24,128]{2,1,0:T(8,128)S(1)} %get-tuple-element.35.coefs, f32[2,8,2,8,128]{4,3,2,1,0:T(8,128)S(1)} %get-tuple-element.33.probe, f32[4,128]{1,0:T(4,128)S(1)} %get-tuple-element.36.rows_in), custom_call_target="tpu_custom_call" | custom-call | tf_op jit(solution)/shard_map/pallas_call | solution.py:522
  37.0 3.5 %collective-permute-start.6 = (f32[24,8,128]{2,1,0:T(8,128)S(1)}, f32[24,8,128]{2,1,0:T(8,128)S(1)}, u32[]{:S(2)}, u32[]{:S(2)}) collective-permute-start(f32[24,8,128]{2,1,0:T(8,128)S(1)} %get-tuple-element.37.own), channel_id=1, source_target_pairs={{0,16},{16,0},{32,48},{48,32},{64,80},{80,64},{96,112},{112,96},{1... | collective-permute-start | bytes 294920 | tf_op jit(solution)/shard_map/ppermute | solution.py:447
  40.5 2.6 %shard_map.91 = (f32[24,8,128]{2,1,0:T(8,128)S(1)}, f32[4,128]{1,0:T(4,128)S(1)}) custom-call(f32[24,8,128]{2,1,0:T(8,128)S(1)} %get-tuple-element.38.own, f32[24,8,128]{2,1,0:T(8,128)S(1)} %collective-permute-done.8.one, f32[24,8,128]{2,1,0:T(8,128)S(1)} %collective-permute-done.9.two, f32[141,24,128]{2,1,0:T(8,128)S(1)} %get-tuple-element.35.coefs, ...), custom_call_target="tpu_custom_call" | custom-call | tf_op jit(solution)/shard_map/pallas_call | solution.py:528
  43.9 2.6 %shard_map.92 = (f32[24,8,128]{2,1,0:T(8,128)S(1)}, f32[4,128]{1,0:T(4,128)S(1)}) custom-call(f32[24,8,128]{2,1,0:T(8,128)S(1)} %get-tuple-element.37.own, f32[24,8,128]{2,1,0:T(8,128)S(1)} %collective-permute-done.6.one, f32[24,8,128]{2,1,0:T(8,128)S(1)} %collective-permute-done.7.two, f32[141,24,128]{2,1,0:T(8,128)S(1)} %get-tuple-element.35.coefs, ...), custom_call_target="tpu_custom_call" | custom-call | tf_op jit(solution)/shard_map/pallas_call | solution.py:528
  46.5 1.0 %collective-permute-start.11 = (f32[24,8,128]{2,1,0:T(8,128)S(1)}, f32[24,8,128]{2,1,0:T(8,128)S(1)}, u32[]{:S(2)}, u32[]{:S(2)}) collective-permute-start(f32[24,8,128]{2,1,0:T(8,128)S(1)} %get-tuple-element.41.own), channel_id=1, source_target_pairs={{0,240},{16,32},{32,16},{48,64},{64,48},{80,96},{96,80},{112,128},... | collective-permute-start | bytes 294920 | tf_op jit(solution)/shard_map/ppermute | solution.py:447
  47.5 2.1 %collective-permute-start.10 = (f32[24,8,128]{2,1,0:T(8,128)S(1)}, f32[24,8,128]{2,1,0:T(8,128)S(1)}, u32[]{:S(2)}, u32[]{:S(2)}) collective-permute-start(f32[24,8,128]{2,1,0:T(8,128)S(1)} %get-tuple-element.41.own), channel_id=1, source_target_pairs={{0,16},{16,0},{32,48},{48,32},{64,80},{80,64},{96,112},{112,96},{1... | collective-permute-start | bytes 294920 | tf_op jit(solution)/shard_map/ppermute | solution.py:447
  49.6 2.6 %shard_map.93 = (f32[24,8,128]{2,1,0:T(8,128)S(1)}, f32[4,128]{1,0:T(4,128)S(1)}) custom-call(f32[24,8,128]{2,1,0:T(8,128)S(1)} %get-tuple-element.42.own, f32[24,8,128]{2,1,0:T(8,128)S(1)} %collective-permute-done.12.one, f32[24,8,128]{2,1,0:T(8,128)S(1)} %collective-permute-done.13.two, f32[141,24,128]{2,1,0:T(8,128)S(1)} %get-tuple-element.35.coefs, ...), custom_call_target="tpu_custom_call" | custom-call | tf_op jit(solution)/shard_map/pallas_call | solution.py:528
  53.0 2.6 %shard_map.94 = (f32[24,8,128]{2,1,0:T(8,128)S(1)}, f32[4,128]{1,0:T(4,128)S(1)}) custom-call(f32[24,8,128]{2,1,0:T(8,128)S(1)} %get-tuple-element.41.own, f32[24,8,128]{2,1,0:T(8,128)S(1)} %collective-permute-done.10.one, f32[24,8,128]{2,1,0:T(8,128)S(1)} %collective-permute-done.11.two, f32[141,24,128]{2,1,0:T(8,128)S(1)} %get-tuple-element.35.coefs, ...), custom_call_target="tpu_custom_call" | custom-call | tf_op jit(solution)/shard_map/pallas_call | solution.py:528
  55.6 1.0 %collective-permute-start.15 = (f32[24,8,128]{2,1,0:T(8,128)S(1)}, f32[24,8,128]{2,1,0:T(8,128)S(1)}, u32[]{:S(2)}, u32[]{:S(2)}) collective-permute-start(f32[24,8,128]{2,1,0:T(8,128)S(1)} %get-tuple-element.45.own), channel_id=1, source_target_pairs={{0,240},{16,32},{32,16},{48,64},{64,48},{80,96},{96,80},{112,128},... | collective-permute-start | bytes 294920 | tf_op jit(solution)/shard_map/ppermute | solution.py:447
  56.6 2.1 %collective-permute-start.14 = (f32[24,8,128]{2,1,0:T(8,128)S(1)}, f32[24,8,128]{2,1,0:T(8,128)S(1)}, u32[]{:S(2)}, u32[]{:S(2)}) collective-permute-start(f32[24,8,128]{2,1,0:T(8,128)S(1)} %get-tuple-element.45.own), channel_id=1, source_target_pairs={{0,16},{16,0},{32,48},{48,32},{64,80},{80,64},{96,112},{112,96},{1... | collective-permute-start | bytes 294920 | tf_op jit(solution)/shard_map/ppermute | solution.py:447
  58.7 2.6 %shard_map.95 = (f32[2,4,2,8,128]{4,3,2,1,0:T(8,128)S(1)}, f32[4,128]{1,0:T(4,128)S(1)}) custom-call(f32[24,8,128]{2,1,0:T(8,128)S(1)} %get-tuple-element.46.own, f32[24,8,128]{2,1,0:T(8,128)S(1)} %collective-permute-done.16.one, f32[24,8,128]{2,1,0:T(8,128)S(1)} %collective-permute-done.17.two, f32[141,24,128]{2,1,0:T(8,128)S(1)} %get-tuple-element.35.coefs, ...), custom_call_target="tpu_custom_call" | custom-call | tf_op jit(solution)/shard_map/pallas_call | solution.py:537
  61.3 3.1 %shard_map.96 = (f32[2,8,2,8,128]{4,3,2,1,0:T(8,128)}, f32[16,4,128]{2,1,0:T(4,128)S(1)}) custom-call(f32[24,8,128]{2,1,0:T(8,128)S(1)} %get-tuple-element.45.own, f32[24,8,128]{2,1,0:T(8,128)S(1)} %collective-permute-done.14.one, f32[24,8,128]{2,1,0:T(8,128)S(1)} %collective-permute-done.15.two, f32[141,24,128]{2,1,0:T(8,128)S(1)} %get-tuple-element.35.coefs, ...), custom_call_target="tpu_custom_call" | custom-call | tf_op jit(solution)/shard_map/pallas_call | solution.py:545
  64.4 10.4 %all_to_all.10 = f32[16,4,128]{2,1,0:T(4,128)S(1)} all-to-all(f32[16,4,128]{2,1,0:T(4,128)S(1)} %get-tuple-element.51), channel_id=1, replica_groups=mesh['gx'=16,'gy'=16] {'gx'}, dimensions={0} | all-to-all | bytes 65536 | tf_op jit(solution)/shard_map/all_to_all | solution.py:552
  74.9 14.8 %all_to_all.11.rows = f32[16,4,128]{2,1,0:T(4,128)S(1)} all-to-all(f32[16,4,128]{2,1,0:T(4,128)S(1)} %broadcast_in_dim.14), channel_id=1, replica_groups=mesh['gx'=16,'gy'=16] {'gy'}, dimensions={0} | all-to-all | bytes 65536 | tf_op jit(solution)/shard_map/all_to_all | solution.py:558
  (31 shorter events, 4.5 us)
Async XLA Ops:
  2.8 12.2 %collective-permute-start = (f32[15,8,128]{2,1,0:T(8,128)S(1)}, f32[15,8,128]{2,1,0:T(8,128)S(1)}, u32[]{:S(2)}, u32[]{:S(2)}) collective-permute-start(f32[15,8,128]{2,1,0:T(8,128)S(1)} %get-tuple-element.29), channel_id=1, source_target_pairs={{0,15},{1,2},{2,1},{3,4},{4,3},{5,6},{6,5},{7,8},{8,7},{9,10},{10,... | collective-permute-start | bytes 184328 | tf_op jit(solution)/shard_map/ppermute | solution.py:499
  11.8 4.6 %collective-permute-start.1 = (f32[15,8,128]{2,1,0:T(8,128)S(1)}, f32[15,8,128]{2,1,0:T(8,128)S(1)}, u32[]{:S(2)}, u32[]{:S(2)}) collective-permute-start(f32[15,8,128]{2,1,0:T(8,128)S(1)} %get-tuple-element.30), channel_id=1, source_target_pairs={{0,1},{1,0},{2,3},{3,2},{4,5},{5,4},{6,7},{7,6},{8,9},{9,8},{10,11... | collective-permute-start | bytes 184328 | tf_op jit(solution)/shard_map/ppermute | solution.py:499
  11.8 9.9 %collective-permute-start.3 = (f32[59,8,128]{2,1,0:T(8,128)S(1)}, f32[59,8,128]{2,1,0:T(8,128)S(1)}, u32[]{:S(2)}, u32[]{:S(2)}) collective-permute-start(f32[59,8,128]{2,1,0:T(8,128)S(1)} %shard_map.87.block), channel_id=1, source_target_pairs={{0,240},{16,32},{32,16},{48,64},{64,48},{80,96},{96,80},{112,128},... | collective-permute-start | bytes 725000 | tf_op jit(solution)/shard_map/ppermute | solution.py:447
  13.0 8.6 %collective-permute-start.2 = (f32[59,8,128]{2,1,0:T(8,128)S(1)}, f32[59,8,128]{2,1,0:T(8,128)S(1)}, u32[]{:S(2)}, u32[]{:S(2)}) collective-permute-start(f32[59,8,128]{2,1,0:T(8,128)S(1)} %shard_map.87.block), channel_id=1, source_target_pairs={{0,16},{16,0},{32,48},{48,32},{64,80},{80,64},{96,112},{112,96},{1... | collective-permute-start | bytes 725000 | tf_op jit(solution)/shard_map/ppermute | solution.py:447
  16.4 5.3 %collective-permute-start.5 = (f32[30,8,128]{2,1,0:T(8,128)S(1)}, f32[30,8,128]{2,1,0:T(8,128)S(1)}, u32[]{:S(2)}, u32[]{:S(2)}) collective-permute-start(f32[30,8,128]{2,1,0:T(8,128)S(1)} %pad_maximum_fusion.strips), channel_id=1, source_target_pairs={{0,240},{16,32},{32,16},{48,64},{64,48},{80,96},{96,80},{112,128},... | collective-permute-start | bytes 368648 | tf_op jit(solution)/shard_map/ppermute | solution.py:447
  18.8 2.9 %collective-permute-start.4 = (f32[30,8,128]{2,1,0:T(8,128)S(1)}, f32[30,8,128]{2,1,0:T(8,128)S(1)}, u32[]{:S(2)}, u32[]{:S(2)}) collective-permute-start(f32[30,8,128]{2,1,0:T(8,128)S(1)} %pad_maximum_fusion.strips), channel_id=1, source_target_pairs={{0,16},{16,0},{32,48},{48,32},{64,80},{80,64},{96,112},{112,96},{1... | collective-permute-start | bytes 368648 | tf_op jit(solution)/shard_map/ppermute | solution.py:447
  29.9 10.7 %collective-permute-start.9 = (f32[24,8,128]{2,1,0:T(8,128)S(1)}, f32[24,8,128]{2,1,0:T(8,128)S(1)}, u32[]{:S(2)}, u32[]{:S(2)}) collective-permute-start(f32[24,8,128]{2,1,0:T(8,128)S(1)} %get-tuple-element.38.own), channel_id=1, source_target_pairs={{0,240},{16,32},{32,16},{48,64},{64,48},{80,96},{96,80},{112,128},... | collective-permute-start | bytes 294920 | tf_op jit(solution)/shard_map/ppermute | solution.py:447
  31.6 8.9 %collective-permute-start.8 = (f32[24,8,128]{2,1,0:T(8,128)S(1)}, f32[24,8,128]{2,1,0:T(8,128)S(1)}, u32[]{:S(2)}, u32[]{:S(2)}) collective-permute-start(f32[24,8,128]{2,1,0:T(8,128)S(1)} %get-tuple-element.38.own), channel_id=1, source_target_pairs={{0,16},{16,0},{32,48},{48,32},{64,80},{80,64},{96,112},{112,96},{1... | collective-permute-start | bytes 294920 | tf_op jit(solution)/shard_map/ppermute | solution.py:447
  36.8 7.1 %collective-permute-start.7 = (f32[24,8,128]{2,1,0:T(8,128)S(1)}, f32[24,8,128]{2,1,0:T(8,128)S(1)}, u32[]{:S(2)}, u32[]{:S(2)}) collective-permute-start(f32[24,8,128]{2,1,0:T(8,128)S(1)} %get-tuple-element.37.own), channel_id=1, source_target_pairs={{0,240},{16,32},{32,16},{48,64},{64,48},{80,96},{96,80},{112,128},... | collective-permute-start | bytes 294920 | tf_op jit(solution)/shard_map/ppermute | solution.py:447
  37.0 6.9 %collective-permute-start.6 = (f32[24,8,128]{2,1,0:T(8,128)S(1)}, f32[24,8,128]{2,1,0:T(8,128)S(1)}, u32[]{:S(2)}, u32[]{:S(2)}) collective-permute-start(f32[24,8,128]{2,1,0:T(8,128)S(1)} %get-tuple-element.37.own), channel_id=1, source_target_pairs={{0,16},{16,0},{32,48},{48,32},{64,80},{80,64},{96,112},{112,96},{1... | collective-permute-start | bytes 294920 | tf_op jit(solution)/shard_map/ppermute | solution.py:447
  43.1 6.5 %collective-permute-start.13 = (f32[24,8,128]{2,1,0:T(8,128)S(1)}, f32[24,8,128]{2,1,0:T(8,128)S(1)}, u32[]{:S(2)}, u32[]{:S(2)}) collective-permute-start(f32[24,8,128]{2,1,0:T(8,128)S(1)} %get-tuple-element.42.own), channel_id=1, source_target_pairs={{0,240},{16,32},{32,16},{48,64},{64,48},{80,96},{96,80},{112,128},... | collective-permute-start | bytes 294920 | tf_op jit(solution)/shard_map/ppermute | solution.py:447
  43.1 6.5 %collective-permute-start.12 = (f32[24,8,128]{2,1,0:T(8,128)S(1)}, f32[24,8,128]{2,1,0:T(8,128)S(1)}, u32[]{:S(2)}, u32[]{:S(2)}) collective-permute-start(f32[24,8,128]{2,1,0:T(8,128)S(1)} %get-tuple-element.42.own), channel_id=1, source_target_pairs={{0,16},{16,0},{32,48},{48,32},{64,80},{80,64},{96,112},{112,96},{1... | collective-permute-start | bytes 294920 | tf_op jit(solution)/shard_map/ppermute | solution.py:447
  46.5 6.5 %collective-permute-start.11 = (f32[24,8,128]{2,1,0:T(8,128)S(1)}, f32[24,8,128]{2,1,0:T(8,128)S(1)}, u32[]{:S(2)}, u32[]{:S(2)}) collective-permute-start(f32[24,8,128]{2,1,0:T(8,128)S(1)} %get-tuple-element.41.own), channel_id=1, source_target_pairs={{0,240},{16,32},{32,16},{48,64},{64,48},{80,96},{96,80},{112,128},... | collective-permute-start | bytes 294920 | tf_op jit(solution)/shard_map/ppermute | solution.py:447
  47.5 5.5 %collective-permute-start.10 = (f32[24,8,128]{2,1,0:T(8,128)S(1)}, f32[24,8,128]{2,1,0:T(8,128)S(1)}, u32[]{:S(2)}, u32[]{:S(2)}) collective-permute-start(f32[24,8,128]{2,1,0:T(8,128)S(1)} %get-tuple-element.41.own), channel_id=1, source_target_pairs={{0,16},{16,0},{32,48},{48,32},{64,80},{80,64},{96,112},{112,96},{1... | collective-permute-start | bytes 294920 | tf_op jit(solution)/shard_map/ppermute | solution.py:447
  52.2 6.5 %collective-permute-start.17 = (f32[24,8,128]{2,1,0:T(8,128)S(1)}, f32[24,8,128]{2,1,0:T(8,128)S(1)}, u32[]{:S(2)}, u32[]{:S(2)}) collective-permute-start(f32[24,8,128]{2,1,0:T(8,128)S(1)} %get-tuple-element.46.own), channel_id=1, source_target_pairs={{0,240},{16,32},{32,16},{48,64},{64,48},{80,96},{96,80},{112,128},... | collective-permute-start | bytes 294920 | tf_op jit(solution)/shard_map/ppermute | solution.py:447
  52.2 6.5 %collective-permute-start.16 = (f32[24,8,128]{2,1,0:T(8,128)S(1)}, f32[24,8,128]{2,1,0:T(8,128)S(1)}, u32[]{:S(2)}, u32[]{:S(2)}) collective-permute-start(f32[24,8,128]{2,1,0:T(8,128)S(1)} %get-tuple-element.46.own), channel_id=1, source_target_pairs={{0,16},{16,0},{32,48},{48,32},{64,80},{80,64},{96,112},{112,96},{1... | collective-permute-start | bytes 294920 | tf_op jit(solution)/shard_map/ppermute | solution.py:447
  55.6 5.7 %collective-permute-start.15 = (f32[24,8,128]{2,1,0:T(8,128)S(1)}, f32[24,8,128]{2,1,0:T(8,128)S(1)}, u32[]{:S(2)}, u32[]{:S(2)}) collective-permute-start(f32[24,8,128]{2,1,0:T(8,128)S(1)} %get-tuple-element.45.own), channel_id=1, source_target_pairs={{0,240},{16,32},{32,16},{48,64},{64,48},{80,96},{96,80},{112,128},... | collective-permute-start | bytes 294920 | tf_op jit(solution)/shard_map/ppermute | solution.py:447
  56.6 4.7 %collective-permute-start.14 = (f32[24,8,128]{2,1,0:T(8,128)S(1)}, f32[24,8,128]{2,1,0:T(8,128)S(1)}, u32[]{:S(2)}, u32[]{:S(2)}) collective-permute-start(f32[24,8,128]{2,1,0:T(8,128)S(1)} %get-tuple-element.45.own), channel_id=1, source_target_pairs={{0,16},{16,0},{32,48},{48,32},{64,80},{80,64},{96,112},{112,96},{1... | collective-permute-start | bytes 294920 | tf_op jit(solution)/shard_map/ppermute | solution.py:447
